TPU v7x, 128 devices: a whole 4x4x4 slice. The times are simulated.
128 devices in a mesh: dp: 4 (over y_hi, core), frames: 32 (over z, y_lo, x).
Axes of the slice: x: 4, y: 4 (y_hi: 2, y_lo: 2; y = y_hi * 2 + y_lo), z: 4, core: 2. Of those that a mesh axis runs over, the one named last changes fastest.
Arguments:
- clean_input: bfloat16 [4, 4096, 1024], P('dp', 'frames'), may hold values from -6 to 6
- corrupt_input: bfloat16 [4, 4096, 1024], P('dp', 'frames'), may hold values from -6 to 6
- patch_mask: int32 [4, 4096], P('dp', 'frames'), may hold values 0 or 1
- lengths: int32 [4], P('dp'), may hold values from 2049 to 4096, as said below
- site_ids: int32 [8], replicated, may hold values from 0 to 3
- w_query: bfloat16 [1024, 512], replicated
- w_key: bfloat16 [1024, 512], replicated
- w_value: bfloat16 [1024, 512], replicated, may hold values from -0.1875 to 0.1875
- w_attn_out: bfloat16 [512, 1024], replicated, may hold values from -0.25 to 0.25
- w_pointwise_in: bfloat16 [1024, 2048], replicated, may hold values from -0.1875 to 0.1875
- depth_kernel: bfloat16 [31, 1024], replicated, may hold values from -1 to 1
- w_pointwise_out: bfloat16 [1024, 1024], replicated, may hold values from -0.1875 to 0.1875
- cotangent: bfloat16 [4, 4096, 1024], P('dp', 'frames'), may hold values from -0.25 to 0.25
Outputs:
- attribution: float32 [4, 8, 4096], P('dp', None, 'frames')
- grad_pointwise_in: float32 [1024, 2048], P(('dp', 'frames'))
- grad_pointwise_out: float32 [1024, 1024], P(('dp', 'frames'))
Inputs may be any that keep to these rules, and one draw needn't show every extreme that they name: `lengths`: in every draw one recording has 4096 frames.
All inputs are finite; a program needn't handle non-finite values. No bound on the sum of `patch_mask` on one device may be relied on, other than what follows from the above.
Results may differ from a plain program's by a relative error of at most 0.025.
Values may be sent and summed in bfloat16 or wider, within the bound.
No kernel may reach another device: no remote copies, remote signals or barrier semaphores. Data moves between devices by JAX's collectives and lax.ppermute only.
A program may use at most 128 MiB of HBM per device.

v0:
```python
import jax
import jax.numpy as jnp
from jax import lax
from jax.sharding import PartitionSpec as P

HEADS = 8
DH = 64
KERNEL = 31


EPSILON = 1e-05
FLOOR = -1e30


def with_halo(block, sides, width):
    for axis, dim in sides:
        count = lax.axis_size(axis)
        forward = [(i, i + 1) for i in range(count - 1)]
        backward = [(target, source) for source, target in forward]
        low = lax.ppermute(
            lax.slice_in_dim(block, block.shape[dim] - width, None, axis=dim), axis, forward
        )
        high = lax.ppermute(lax.slice_in_dim(block, 0, width, axis=dim), axis, backward)
        block = jnp.concatenate([low, block, high], axis=dim)
    return block


def normalize(values):
    mean = jnp.mean(values, axis=-1, keepdims=True)
    centred = values - mean
    variance = jnp.mean(centred * centred, axis=-1, keepdims=True)
    inverse = lax.rsqrt(variance + EPSILON)
    return (centred * inverse, inverse)


def norm_back(grad, normed, inverse):
    return (
        grad
        - jnp.mean(grad, axis=-1, keepdims=True)
        - normed * jnp.mean(grad * normed, axis=-1, keepdims=True)
    ) * inverse


def depthwise(padded, kernel, count):
    result = jnp.zeros((count, padded.shape[1]), jnp.float32)
    for tap_index in range(kernel.shape[0]):
        result = result + kernel[tap_index].astype(jnp.float32) * padded[
            tap_index : tap_index + count
        ].astype(jnp.float32)
    return result


def attend_init(count):
    return (
        jnp.full((HEADS, count), FLOOR, jnp.float32),
        jnp.zeros((HEADS, count), jnp.float32),
        jnp.zeros((count, HEADS, DH), jnp.float32),
    )


def attend_step(state, query, keys, values, length):
    best, total, accum = state
    count = keys.shape[0]
    query_heads = query.reshape(query.shape[0], HEADS, DH)
    key_heads = keys.reshape(count, HEADS, DH)
    value_heads = values.reshape(count, HEADS, DH)
    scores = jnp.einsum(
        "qhd,khd->hqk", query_heads, key_heads, preferred_element_type=jnp.float32
    ) * DH ** (-0.5)
    live = jnp.arange(count) < length
    scores = jnp.where(live[None, None, :], scores, FLOOR)
    newbest = jnp.maximum(best, jnp.max(scores, axis=-1))
    weights = jnp.exp(scores - newbest[:, :, None]) * live[None, None, :].astype(jnp.float32)
    total = jnp.sum(weights, axis=-1)
    addend = jnp.einsum(
        "hqk,khd->qhd",
        weights.astype(jnp.bfloat16),
        value_heads,
        preferred_element_type=jnp.float32,
    )
    accum = addend
    return (newbest, total, accum)


def attend_finish(state):
    best, total, accum = state
    return (
        (accum / jnp.transpose(total)[:, :, None])
        .reshape(accum.shape[0], HEADS * DH)
        .astype(jnp.bfloat16)
    )


def contract_rows(left, right):
    return lax.dot_general(
        left, right, (((0,), (0,)), ((), ())), preferred_element_type=jnp.float32
    )


def per_device(
    clean_input,
    corrupt_input,
    patch_mask,
    lengths,
    site_ids,
    w_query,
    w_key,
    w_value,
    w_attn_out,
    w_pointwise_in,
    depth_kernel,
    w_pointwise_out,
    cotangent,
):
    frame_rows = clean_input.shape[1]
    width = clean_input.shape[2]
    half = KERNEL // 2
    first_frame = lax.axis_index("frames") * frame_rows
    length = lengths[0]
    valid = (first_frame + jnp.arange(frame_rows) < length).astype(jnp.float32)[:, None]
    clean = clean_input[0]
    patched = jnp.where(patch_mask[0][:, None] == 1, corrupt_input[0], clean)

    def project(source):
        normed, inverse = normalize(source.astype(jnp.float32))
        hidden = normed.astype(jnp.bfloat16)
        query = jnp.dot(hidden, w_query, preferred_element_type=jnp.float32).astype(jnp.bfloat16)
        keys = jnp.dot(hidden, w_key, preferred_element_type=jnp.float32).astype(jnp.bfloat16)
        values = jnp.dot(hidden, w_value, preferred_element_type=jnp.float32).astype(jnp.bfloat16)
        return (query, keys, values)

    clean_query, clean_keys, clean_values = project(clean)
    patch_query, patch_keys, patch_values = project(patched)
    pieces = (
        lax.all_gather(clean_keys, "frames", axis=0, tiled=True),
        lax.all_gather(clean_values, "frames", axis=0, tiled=True),
    )
    clean_state = attend_step(attend_init(frame_rows), clean_query, pieces[0], pieces[1], length)
    pieces = (
        lax.all_gather(patch_keys, "frames", axis=0, tiled=True),
        lax.all_gather(patch_values, "frames", axis=0, tiled=True),
    )
    patch_state = attend_step(attend_init(frame_rows), patch_query, pieces[0], pieces[1], length)

    def rim(gated):
        return with_halo(gated, (("frames", 0),), half)

    def forward(source, context):
        joined = source.astype(jnp.float32) + jnp.dot(
            context, w_attn_out, preferred_element_type=jnp.float32
        )
        resid = joined.astype(jnp.bfloat16)
        resid_normed, resid_inverse = normalize(resid.astype(jnp.float32))
        lowered = resid_normed.astype(jnp.bfloat16)
        mixed = jnp.dot(lowered, w_pointwise_in, preferred_element_type=jnp.float32)
        sigmoid_gate = jax.nn.sigmoid(mixed[:, width:])
        gated = (mixed[:, :width] * sigmoid_gate * valid).astype(jnp.bfloat16)
        spread = depthwise(rim(gated), depth_kernel, frame_rows)
        zed, zed_inverse = normalize(spread)
        swished = (zed * jax.nn.sigmoid(zed)).astype(jnp.bfloat16)
        output = (
            resid.astype(jnp.float32)
            + jnp.dot(swished, w_pointwise_out, preferred_element_type=jnp.float32)
        ).astype(jnp.bfloat16)
        return (
            resid,
            resid_normed,
            resid_inverse,
            lowered,
            mixed,
            sigmoid_gate,
            gated,
            zed,
            zed_inverse,
            swished,
            output,
        )

    (
        resid,
        resid_normed,
        resid_inverse,
        lowered,
        mixed,
        sigmoid_gate,
        gated,
        zed,
        zed_inverse,
        swished,
        output,
    ) = forward(clean, attend_finish(clean_state))
    patch_run = forward(patched, attend_finish(patch_state))
    grad_output = (cotangent[0].astype(jnp.float32) * valid).astype(jnp.bfloat16)
    grad_swished = lax.dot_general(
        grad_output, w_pointwise_out, (((1,), (1,)), ((), ())), preferred_element_type=jnp.float32
    )
    zed_sigmoid = jax.nn.sigmoid(zed)
    grad_zed = grad_swished * (zed_sigmoid * (1.0 + zed * (1.0 - zed_sigmoid)))
    grad_spread = norm_back(grad_zed, zed, zed_inverse)
    padded_grad = with_halo(grad_spread.astype(jnp.bfloat16), (("frames", 0),), half).astype(
        grad_spread.dtype
    )
    grad_gated = depthwise(padded_grad, depth_kernel[::-1], frame_rows) * valid
    grad_mixed = jnp.concatenate(
        (
            grad_gated * sigmoid_gate,
            grad_gated * mixed[:, :width] * sigmoid_gate * (1.0 - sigmoid_gate),
        ),
        axis=1,
    ).astype(jnp.bfloat16)
    grad_lowered = lax.dot_general(
        grad_mixed, w_pointwise_in, (((1,), (1,)), ((), ())), preferred_element_type=jnp.float32
    )
    grad_resid = grad_output.astype(jnp.float32) + norm_back(
        grad_lowered, resid_normed, resid_inverse
    )

    def score(patch_value, clean_value, grad):
        return jnp.sum(
            (patch_value.astype(jnp.float32) - clean_value.astype(jnp.float32)) * grad, axis=1
        )

    table = jnp.stack(
        (
            score(patch_run[0], resid, grad_resid),
            score(patch_run[6], gated, grad_gated),
            score(patch_run[9], swished, grad_swished),
            score(patch_run[10], output, grad_output.astype(jnp.float32)),
        ),
        axis=0,
    )
    chosen = (site_ids[:, None] == jnp.arange(4)[None, :]).astype(jnp.float32)
    attribution = jnp.sum(chosen[:, :, None] * table[None, :, :], axis=1)[None]
    summed = lax.psum_scatter(
        jnp.concatenate(
            (contract_rows(lowered, grad_mixed), contract_rows(swished, grad_output)), axis=1
        ),
        ("dp", "frames"),
        scatter_dimension=0,
        tiled=True,
    )
    return (attribution, summed[:, : 2 * width], summed[:, 2 * width :])


def solution(mesh):
    placed = (
        P("dp", "frames", None),
        P("dp", "frames", None),
        P("dp", "frames"),
        P("dp"),
        P(),
        P(),
        P(),
        P(),
        P(),
        P(),
        P(),
        P(),
        P("dp", "frames", None),
    )
    return jax.shard_map(
        per_device,
        mesh=mesh,
        in_specs=placed,
        out_specs=(P("dp", None, "frames"), P(("dp", "frames"), None), P(("dp", "frames"), None)),
        check_vma=False,
    )
```

profile of v0, /device:TPU:10, one launch (start us, length us, event | category | flops | bytes accessed | tf_op | source)
XLA Modules:
  0.0 1367.6 jit_solution(15165224280234410323)
XLA Ops:
  7.2 0.8 compare_bitcast_fusion
  8.0 1.3 convert_reduce_fusion.1
  9.3 1.2 fusion.45
  10.5 2.3 convolution_convert_fusion
  13.1 2.2 convolution_convert_fusion.3
  15.4 2.3 convolution_convert_fusion.2
  17.8 2.2 convolution_convert_fusion.5
  20.1 1.7 convolution_convert_fusion.1
  21.8 1.6 convolution_convert_fusion.4
  24.3 1.0 slice_convert_fusion.28
  25.4 1.2 slice_convert_fusion.29
  26.6 139.5 %all-gather.11.cloned.1.call-done = bf16[4096,512]{1,0:T(8,128)(2,1)} async-done(((bf16[128,512]{1,0:T(8,128)(2,1)}), bf16[4096,512]{1,0:T(8,128)(2,1)}) %all-gather.11.cloned.1.call-update) | async-done | bytes 4194320 | tf_op jit(solution)/shard_map/all_gather | solution.py:135
  166.1 6.4 copy.35
  172.5 152.2 %all-gather.7.cloned.1.call-done = bf16[4096,512]{1,0:T(8,128)(2,1)} async-done(((bf16[128,512]{1,0:T(8,128)(2,1)}), bf16[4096,512]{1,0:T(8,128)(2,1)}) %all-gather.7.cloned.1.call-update) | async-done | bytes 4194320 | tf_op jit(solution)/shard_map/all_gather | solution.py:140
  324.7 6.4 copy.32
  331.1 152.2 %all-gather.9.cloned.1.call-done = bf16[4096,512]{1,0:T(8,128)(2,1)} async-done(((bf16[128,512]{1,0:T(8,128)(2,1)}), bf16[4096,512]{1,0:T(8,128)(2,1)}) %all-gather.9.cloned.1.call-update) | async-done | bytes 4194320 | tf_op jit(solution)/shard_map/all_gather | solution.py:136
  483.4 6.4 copy.33
  489.8 10.4 fusion.220
  500.2 11.1 fusion
  511.4 14.2 %fusion.2 = (f32[8,128]{1,0:T(8,128)S(1)}, f32[8,128]{1,0:T(8,128)S(1)}) fusion(f32[8,128,4096]{2,1,0:T(8,128)} %get-tuple-element.63, f32[4096]{0:T(1024)S(1)} %fusion.188, f32[8,128]{1,0:T(8,128)S(1)} %broadcast_maximum_fusion.1, pred[4096]{0:T(1024)(128)(4,1)S(1)} %iota_compare_fusion, f32[8,128]{1,0:T(8,128)S(1)} %broadcast_maximum_fusion, ...), kind=kLoop, calls=%fused_computation.7 | loop fusion | flops 41940992 | bytes 33591296 | tf_op jit(solution)/shard_map/reduce_sum | solution.py:74
  525.6 8.2 fusion.32
  534.5 107.8 %all-gather.5.cloned.1.call-done = bf16[4096,512]{1,0:T(8,128)(2,1)} async-done(((bf16[128,512]{1,0:T(8,128)(2,1)}), bf16[4096,512]{1,0:T(8,128)(2,1)}) %all-gather.5.cloned.1.call-update) | async-done | bytes 4194320 | tf_op jit(solution)/shard_map/all_gather | solution.py:141
  642.4 6.4 copy.30
  648.8 11.5 fusion.38
  661.0 0.8 fusion.197
  661.7 0.8 fusion.129
  662.8 2.7 collective-permute-start.4
  665.6 3.1 collective-permute-start.5
  668.7 2.7 collective-permute-start
  671.5 4.6 collective-permute-start.1
  676.1 2.7 fusion.211
  679.0 2.7 fusion.213
  681.9 1.6 multiply_reduce_fusion.4
  683.8 2.3 collective-permute-start.2
  686.1 5.7 collective-permute-start.3
  691.8 0.9 fusion.199
  692.7 2.3 collective-permute-done.3
  695.0 2.4 multiply_convert_fusion.4
  697.8 0.7 copy-done.9
  698.5 1.4 fusion.127
  699.9 4.9 pad_maximum_fusion
  704.8 0.6 copy-done.13
  706.0 1.9 fusion.22
  708.0 3.9 fusion.209
  712.3 0.7 multiply_reduce_fusion.7
  713.0 645.2 %reduce-scatter.2.cloned.1.call-done = f32[8,3072]{1,0:T(8,128)} async-done(((f32[1024,3072]{1,0:T(8,128)}), f32[8,3072]{1,0:T(8,128)}) %reduce-scatter.2.cloned.1.call-update) | async-done | bytes 98320 | tf_op jit(solution)/shard_map/reduce_scatter | solution.py:234
  1358.2 1.5 slice.843
  1359.7 1.4 slice.844
  (91 shorter events, 4.5 us)
Async XLA Ops:
  7.2 674.7 %copy-start = (bf16[1024,1024]{1,0:T(8,128)(2,1)S(1)}, bf16[1024,1024]{1,0:T(8,128)(2,1)}, u32[]{:S(2)}) copy-start(bf16[1024,1024]{1,0:T(8,128)(2,1)} %param.24) | copy-start | bytes 6291460
  7.2 158.9 %all-gather.11.cloned.1.call-start = ((), (), s32[]{:S(2)}) async-start(), calls=%async_computation.4 | async-start | bytes 4325376 | tf_op jit(solution)/shard_map/all_gather | solution.py:135
  12.8 311.9 %all-gather.7.cloned.1.call-start = ((), (), s32[]{:S(2)}) async-start(), calls=%async_computation.2 | async-start | bytes 4325376 | tf_op jit(solution)/shard_map/all_gather | solution.py:140
  15.3 468.0 %all-gather.9.cloned.1.call-start = ((), (), s32[]{:S(2)}) async-start(), calls=%async_computation.3 | async-start | bytes 4325376 | tf_op jit(solution)/shard_map/all_gather | solution.py:136
  17.7 624.6 %all-gather.5.cloned.1.call-start = ((), (), s32[]{:S(2)}) async-start(), calls=%async_computation.1 | async-start | bytes 4325376 | tf_op jit(solution)/shard_map/all_gather | solution.py:141
  20.0 1338.1 %reduce-scatter.2.cloned.1.call-start = ((), (), s32[]{:S(2)}) async-start(), calls=%async_computation.5 | async-start | bytes 12681216 | tf_op jit(solution)/shard_map/reduce_scatter | solution.py:234
  489.8 10.4 copy-start.2
  511.4 14.2 %copy-start.6 = (bf16[4096,512]{0,1:T(8,128)(2,1)S(1)}, bf16[4096,512]{0,1:T(8,128)(2,1)}, u32[]{:S(2)}) copy-start(bf16[4096,512]{0,1:T(8,128)(2,1)} %copy.33) | copy-start | bytes 12582916
  525.6 8.3 copy-start.3
  525.6 8.2 copy-start.7
  648.8 11.6 copy-start.8
  648.8 12.2 copy-start.1
  660.3 21.6 %copy-start.11 = (bf16[1,128,1024]{2,1,0:T(8,128)(2,1)S(1)}, bf16[1,128,1024]{2,1,0:T(8,128)(2,1)}, u32[]{:S(2)}) copy-start(bf16[1,128,1024]{2,1,0:T(8,128)(2,1)} %param.25) | copy-start | bytes 786436
  660.7 22.8 %copy-start.4 = (f32[128,1024]{1,0:T(8,128)}, f32[128,1024]{1,0:T(8,128)S(1)}, u32[]{:S(2)}) copy-start(f32[128,1024]{1,0:T(8,128)S(1)} %get-tuple-element.65) | copy-start | bytes 1572868
  662.8 13.2 collective-permute-start.4
  665.6 10.5 collective-permute-start.5
  668.7 10.3 collective-permute-start
  671.5 7.6 collective-permute-start.1
  678.7 16.2 %copy-start.10 = (f32[128,1024]{1,0:T(8,128)}, f32[128,1024]{1,0:T(8,128)S(1)}, u32[]{:S(2)}) copy-start(f32[128,1024]{1,0:T(8,128)S(1)} %get-tuple-element.16) | copy-start | bytes 1572868
  678.8 16.2 %copy-start.15 = (f32[128]{0:T(128)}, f32[128]{0:T(128)S(1)}, u32[]{:S(2)}) copy-start(f32[128]{0:T(128)S(1)} %broadcast_multiply_fusion) | copy-start | bytes 1540
  679.0 16.0 %copy-start.17 = (f32[128]{0:T(128)}, f32[128]{0:T(128)S(1)}, u32[]{:S(2)}) copy-start(f32[128]{0:T(128)S(1)} %add_rsqrt_fusion) | copy-start | bytes 1540
  683.8 8.8 collective-permute-start.2
  686.1 8.8 collective-permute-start.3
  697.8 0.7 copy-start.9
  704.8 0.7 copy-start.13
  704.8 1.2 copy-start.16
  704.8 1.2 copy-start.18
  704.8 7.5 copy-start.14
  705.4 6.4 copy-start.5
  705.4 6.5 copy-start.12
Sparse Core Ops, SparseCore 0:
  12.9 153.1 all-gather.10
  167.8 156.9 all-gather.6
  326.4 156.9 all-gather.8
  484.9 157.4 all-gather.4
  704.9 653.2 reduce-scatter.1
where the time goes:
time: 1380 us; the launch traced here: 1370 us
  waiting for transfers between devices  1200 us (87%)
  matrix products  66.2 us (5%)
  other arithmetic  35.5 us (3%)
  local copies, waits for them, and re-layouts  30.1 us (2%)
  starting transfers between devices  21.3 us (2%)
  between operations  15 us (1%)
    reduce_scatter x1, waiting for transfers between devices, per_device(): lax.psum_scatter(jnp.concatenate((contract_rows(lowered, grad_mixed), con...  645 us
    all_gather x1, waiting for transfers between devices, per_device(): lax.all_gather(clean_values, 'frames', axis=0, tiled=True)  152 us
    all_gather x1, waiting for transfers between devices, per_device(): lax.all_gather(patch_keys, 'frames', axis=0, tiled=True)  152 us
    all_gather x1, waiting for transfers between devices, per_device(): lax.all_gather(clean_keys, 'frames', axis=0, tiled=True)  140 us
    all_gather x1, waiting for transfers between devices, per_device(): lax.all_gather(patch_values, 'frames', axis=0, tiled=True)  108 us
  transfers between devices with their start and end apart: 11, of which 6 were waited for; matrix products, arithmetic and copies ran while one was open for 6% of the time, Pallas kernels for 0%

commit v1 on v0

v1 whole, which is shorter than its diff:
```python
import jax
import jax.numpy as jnp
from jax import lax
from jax.experimental import pallas as pl
from jax.experimental.pallas import tpu as pltpu
from jax.sharding import PartitionSpec as P

HEADS = 8
DH = 64
KERNEL = 31
RIM = 32
EPSILON = 1e-05
FLOOR = -1e30
LOG2E = 1.4426950408889634
F32 = jnp.float32
BF16 = jnp.bfloat16
ROWS = 128
WIDTH = 1024
CLEAN = ROWS + 2 * RIM
PATCH = ROWS + RIM
BOTH = CLEAN + PATCH
INNER = ROWS + RIM


def lane_of(rows):
    return lax.broadcasted_iota(jnp.int32, (rows, 128), 1)


def swap(tile):
    return pltpu.roll(tile, 64, 1)


def moments(values):
    mean = jnp.mean(values, axis=-1, keepdims=True)
    centred = values - mean
    variance = jnp.mean(centred * centred, axis=-1, keepdims=True)
    return centred, lax.rsqrt(variance + EPSILON)


def dot(left, right):
    return jnp.dot(left, right, preferred_element_type=F32)


def dot_nt(left, right):
    return lax.dot_general(left, right, (((1,), (1,)), ((), ())), preferred_element_type=F32)


def dot_tn(left, right):
    return lax.dot_general(left, right, (((0,), (0,)), ((), ())), preferred_element_type=F32)


def sigmoid(values):
    return 1.0 / (1.0 + jnp.exp(-values))


def lane_sum(values):
    total = values[:, :128]
    for start in range(128, values.shape[1], 128):
        total = total + values[:, start : start + 128]
    return total


def project_kernel(
    clean_ref, corrupt_ref, cot_ref, mask_ref, wq_ref, wk_ref, wv_ref,
    msg_ref, patched_ref, up_ref, down_ref, hidden_ref, mask_col,
):
    spread_mask = jnp.broadcast_to(mask_ref[...].astype(F32), (ROWS, ROWS))
    mask_col[...] = spread_mask.T

    def rows(i, carry):
        at = pl.ds(pl.multiple_of(i * 16, 16), 16)
        below = pl.ds(pl.multiple_of(ROWS + i * 16, 16), 16)
        clean = clean_ref[at, :].astype(F32)
        corrupt = corrupt_ref[at, :].astype(F32)
        patched = jnp.where(mask_col[at, 0:1] == 1.0, corrupt, clean)
        patched_ref[at, :] = patched.astype(BF16)
        for dest, source in ((at, clean), (below, patched)):
            centred, inverse = moments(source)
            hidden_ref[dest, :] = (centred * inverse).astype(BF16)
        return carry

    lax.fori_loop(0, ROWS // 16, rows, 0)
    half = RIM // 2
    up_ref[0:RIM, :] = clean_ref[ROWS - RIM : ROWS, :]
    up_ref[RIM : RIM + half, :] = patched_ref[ROWS - half : ROWS, :]
    up_ref[RIM + half :, :] = cot_ref[ROWS - half : ROWS, :]
    down_ref[0:RIM, :] = clean_ref[0:RIM, :]
    down_ref[RIM : RIM + half, :] = patched_ref[0:half, :]
    down_ref[RIM + half :, :] = cot_ref[0:half, :]

    low = lane_of(ROWS) < 64
    low_q = lane_of(32) < 64
    for pair in range(2):
        cols = slice(pair * 256, pair * 256 + 256)
        hidden = hidden_ref[...]
        query = dot(hidden, wq_ref[:, cols])
        keys = dot(hidden, wk_ref[:, cols])
        values = dot(hidden, wv_ref[:, cols])
        for sub in range(2):
            tile = slice(sub * 128, sub * 128 + 128)
            for run in range(2):
                part = slice(run * ROWS, run * ROWS + ROWS)
                k, v, q = keys[part, tile], values[part, tile], query[part, tile]
                base = run * 16 + (pair * 2 + sub) * 4
                even = jnp.where(low, k, swap(v)).astype(BF16)
                odd = jnp.where(low, swap(k), v).astype(BF16)
                for side in range(2):
                    msg_ref[base + side, 0:ROWS, :] = even
                    msg_ref[base + 2 + side, 0:ROWS, :] = odd
                    qa = q[side * 64 : side * 64 + 32]
                    qb = q[side * 64 + 32 : side * 64 + 64]
                    msg_ref[base + side, ROWS : ROWS + 32, :] = jnp.where(
                        low_q, qa, swap(qb)
                    ).astype(BF16)
                    msg_ref[base + 2 + side, ROWS : ROWS + 32, :] = jnp.where(
                        low_q, swap(qa), qb
                    ).astype(BF16)


def attend_kernel(scal_ref, recv_ref, out_ref, kt_ref, v_ref, s0_ref, s1_ref, m0_ref, m1_ref, c_ref):
    length = scal_ref[1]
    side = scal_ref[3]
    sources = recv_ref.shape[0]
    count = sources * ROWS
    lane = lane_of(ROWS)

    def load(s, carry):
        kv = recv_ref[s, 0:ROWS, :].astype(F32)
        frame = s * ROWS + lax.broadcasted_iota(jnp.int32, (ROWS, 128), 0)
        bias = jnp.where(frame < length, 0.0, FLOOR)
        keyed = jnp.where(lane < 64, kv, jnp.where(lane == 64, bias, 0.0))
        at = pl.ds(pl.multiple_of(s * ROWS, ROWS), ROWS)
        kt_ref[:, at] = keyed.T.astype(BF16)
        v_ref[at, :] = jnp.where(lane < 64, 1.0, kv).astype(BF16)
        return carry

    lax.fori_loop(0, sources, load, 0)

    chunk = 512
    pieces = count // chunk
    blocks = sources // 4
    scale = DH ** (-0.5) * LOG2E

    def queries(b):
        raw = recv_ref[pl.ds(b * 4, 4), ROWS : ROWS + 32, :].astype(F32).reshape(128, 128)
        fill = jnp.where(lane == 64, 1.0, 0.0)
        return jnp.concatenate(
            [jnp.where(lane < 64, raw, fill), jnp.where(lane < 64, swap(raw), fill)], axis=0
        ).astype(BF16)

    def score_piece(query, s_ref, k, top):
        scores = dot(query, kt_ref[:, k * chunk : (k + 1) * chunk])
        s_ref[:, k * chunk : (k + 1) * chunk] = scores
        for j in range(chunk // 128):
            tile = scores[:, j * 128 : (j + 1) * 128]
            top = tile if top is None else jnp.maximum(top, tile)
        return top

    def finish_top(m_ref, top):
        m_ref[...] = jnp.broadcast_to(jnp.max(top, axis=1, keepdims=True), (256, 128))

    def weigh_piece(s_ref, top, k, accum):
        scores = s_ref[:, k * chunk : (k + 1) * chunk]
        weights = jnp.exp2((scores - top) * scale).astype(BF16)
        addend = dot(weights, v_ref[k * chunk : (k + 1) * chunk, :])
        return addend if accum is None else accum + addend

    def store(b, accum):
        first, second = accum[:128], accum[128:]
        result = jnp.where(lane < 64, swap(first) / first, second / swap(second))
        c_ref[pl.ds(b * 128, 128), :] = result

    def step(b, s_ref, m_ref, next_b, next_s, next_m):
        query = None if next_s is None else queries(next_b)
        top, accum = None, None
        best = jnp.tile(m_ref[...], (1, chunk // 128))
        for k in range(pieces):
            if query is not None:
                top = score_piece(query, next_s, k, top)
            accum = weigh_piece(s_ref, best, k, accum)
        if query is not None:
            finish_top(next_m, top)
        store(b, accum)

    query, top = queries(0), None
    for k in range(pieces):
        top = score_piece(query, s0_ref, k, top)
    finish_top(m0_ref, top)

    def pair(i, carry):
        step(2 * i, s0_ref, m0_ref, 2 * i + 1, s1_ref, m1_ref)
        step(2 * i + 1, s1_ref, m1_ref, 2 * i + 2, s0_ref, m0_ref)
        return carry

    lax.fori_loop(0, blocks // 2 - 1, pair, 0)
    step(blocks - 2, s0_ref, m0_ref, blocks - 1, s1_ref, m1_ref)
    step(blocks - 1, s1_ref, m1_ref, None, None, None)

    low = lane_of(16) < 64

    def pack(d, carry):
        own = c_ref[pl.ds(pl.multiple_of(d * 32, 32), 32), :]
        after = lax.rem(d + 1, sources)
        before = lax.rem(d + sources - 1, sources)
        other = jnp.where(side == 0, after, before)
        rim = c_ref[pl.ds(pl.multiple_of(other * 32, 32), 32), :]
        first, second = rim[:16], rim[16:]
        rim_a = jnp.where(low, first, swap(second))
        rim_b = jnp.where(low, swap(first), second)
        out_ref[d, 0:32, :] = own.astype(BF16)
        out_ref[d, 32:48, :] = jnp.where(side == 0, rim_a, rim_b).astype(BF16)
        return carry

    lax.fori_loop(0, sources, pack, 0)


def depthwise(source, source_row, taps_ref, order, target, count):
    def rows(i, carry):
        first = source_row + i * 8
        taps = [taps_ref[t * 8 : t * 8 + 8, :] for t in order]
        sums = [None] * 8
        for s in range(KERNEL + 7):
            piece = source[pl.ds(pl.multiple_of((first + s) * 8, 8), 8), :]
            for o in range(8):
                if 0 <= s - o < KERNEL:
                    term = taps[s - o] * piece
                    sums[o] = term if sums[o] is None else sums[o] + term
        for o in range(8):
            target[pl.ds(pl.multiple_of((i * 8 + o) * 8, 8), 8), :] = sums[o]
        return carry

    lax.fori_loop(0, count // 8, rows, 0)


def put_rows(ref, row, tile, values):
    for r in range(0, values.shape[0], 8):
        ref[pl.ds((row + r) * 8 + tile, 8, stride=8), :] = values[r : r + 8]


def get_rows(ref, row, count):
    groups = []
    for r in range(0, count, 8):
        tiles = [ref[pl.ds((row + r) * 8 + t, 8, stride=8), :] for t in range(8)]
        groups.append(jnp.concatenate(tiles, axis=1))
    return jnp.concatenate(groups, axis=0) if len(groups) > 1 else groups[0]


def block_kernel(
    scal_ref, site_ref, ctx_in, clean_ref, patched_ref, cot_ref, up_ref, down_ref,
    wao_ref, win_ref, depth_ref, wout_ref,
    attr_ref, own_ref, send_ref, gm_ref, go_ref,
    ctx_ref, x_ref, resid_ref, low_ref, mv_ref, sg_ref, g2_ref, s2_ref, zed_ref, zinv_ref,
    sw_ref, gox_ref, gs_ref, gsp2_ref, gg2_ref, gl_ref, t0_ref, t1_ref, t2_ref, taps_ref,
):
    first_frame, length, core = scal_ref[0], scal_ref[1], scal_ref[2]
    half = RIM // 2

    for run in range(2):
        for t in range(HEADS // 2):
            at = slice(t * 128, t * 128 + 128)
            base = run * 16 + t * 4
            halves = {}
            for side in range(2):
                even = ctx_in[base + side].astype(F32)
                odd = ctx_in[base + 2 + side].astype(F32)
                low = lane_of(48) < 64
                halves[side] = (
                    jnp.where(low, even, swap(odd)).astype(BF16),
                    jnp.where(low, swap(even), odd).astype(BF16),
                )
            (lo0, hi0), (lo1, hi1) = halves[0], halves[1]
            parts = [lo1[32:48], hi1[32:48], lo0[:32], hi0[:32], lo1[:32], hi1[:32], lo0[32:48], hi0[32:48]]
            row = 0
            if run == 1:
                parts = parts[1:-1]
                row = CLEAN
            for part in parts:
                ctx_ref[row : row + part.shape[0], at] = part
                row += part.shape[0]

    x_ref[0:RIM, :] = up_ref[0:RIM, :]
    x_ref[RIM : RIM + ROWS, :] = clean_ref[...]
    x_ref[RIM + ROWS : CLEAN, :] = down_ref[0:RIM, :]
    x_ref[CLEAN : CLEAN + half, :] = up_ref[RIM : RIM + half, :]
    x_ref[CLEAN + half : CLEAN + half + ROWS, :] = patched_ref[...]
    x_ref[CLEAN + half + ROWS : BOTH, :] = down_ref[RIM : RIM + half, :]

    for r in range(0, KERNEL + 1, 8):
        got = min(8, KERNEL - r)
        block = depth_ref[r : r + got, :].astype(F32)
        if got < 8:
            block = jnp.concatenate([block, jnp.zeros((8 - got, WIDTH), F32)], axis=0)
        for t in range(8):
            put_rows(taps_ref, r, t, block[:, t * 128 : t * 128 + 128])

    frame0 = first_frame - half
    for piece, row, offset in (
        (up_ref[RIM + half :, :], 0, -half),
        (cot_ref[...], half, 0),
        (down_ref[RIM + half :, :], half + ROWS, ROWS),
    ):
        n = piece.shape[0]
        frame = first_frame + offset + lax.broadcasted_iota(jnp.int32, (n, 1), 0)
        keep = jnp.where(frame < length, 1.0, 0.0)
        gox_ref[row : row + n, :] = (piece.astype(F32) * keep).astype(BF16)
    go_ref[...] = gox_ref[half : half + ROWS, :]

    for j in range(4):
        at = slice(j * 256, j * 256 + 256)
        joined = x_ref[:, at].astype(F32) + dot(ctx_ref[...], wao_ref[:, at])
        resid_ref[:, at] = joined.astype(BF16)

    def lower(i, carry):
        at = pl.ds(pl.multiple_of(i * 16, 16), 16)
        centred, inverse = moments(resid_ref[at, :].astype(F32))
        low_ref[at, :] = (centred * inverse).astype(BF16)
        return carry

    lax.fori_loop(0, BOTH // 16, lower, 0)

    row = lax.broadcasted_iota(jnp.int32, (BOTH, 1), 0)
    frame = first_frame + jnp.where(row < CLEAN, row - RIM, row - CLEAN - half)
    live = jnp.where((frame >= 0) & (frame < length), 1.0, 0.0)
    for j in range(4):
        at = slice(j * 256, j * 256 + 256)
        gate_at = slice(WIDTH + j * 256, WIDTH + j * 256 + 256)
        value = dot(low_ref[...], win_ref[:, at])
        gate = sigmoid(dot(low_ref[...], win_ref[:, gate_at]))
        mv_ref[:, at] = value[RIM : RIM + ROWS]
        sg_ref[:, at] = gate[RIM : RIM + ROWS]
        gated = (value * gate * live).astype(BF16).astype(F32)
        for t in range(2):
            put_rows(g2_ref, 0, j * 2 + t, gated[:, t * 128 : t * 128 + 128])

    forward = list(range(KERNEL))
    edge = half - KERNEL // 2
    depthwise(g2_ref, edge, taps_ref, forward, s2_ref, INNER)

    def clean_rows(i, carry):
        r = pl.multiple_of(i * 16, 16)
        centred, inverse = moments(get_rows(s2_ref, r, 16))
        zed = centred * inverse
        zed_ref[pl.ds(r, 16), :] = zed
        zinv_ref[pl.ds(r, 16), :] = jnp.broadcast_to(inverse, (16, 128))
        sw_ref[pl.ds(r, 16), :] = (zed * sigmoid(zed)).astype(BF16)
        return carry

    lax.fori_loop(0, INNER // 16, clean_rows, 0)
    depthwise(g2_ref, CLEAN + edge, taps_ref, forward, s2_ref, ROWS)

    def patch_rows(i, carry):
        r = pl.multiple_of(i * 16, 16)
        centred, inverse = moments(get_rows(s2_ref, r, 16))
        zed = centred * inverse
        sw_ref[pl.ds(pl.multiple_of(INNER + r, 16), 16), :] = (zed * sigmoid(zed)).astype(BF16)
        return carry

    lax.fori_loop(0, ROWS // 16, patch_rows, 0)

    t3 = jnp.zeros((ROWS, 128), F32)
    for j in range(4):
        at = slice(j * 256, j * 256 + 256)
        out = dot(sw_ref[half : INNER + ROWS, :], wout_ref[:, at])
        out_clean = resid_ref[RIM : RIM + ROWS, at].astype(F32) + out[:ROWS]
        out_patch = resid_ref[CLEAN + half : CLEAN + half + ROWS, at].astype(F32) + out[ROWS + half :]
        gap = out_patch.astype(BF16).astype(F32) - out_clean.astype(BF16).astype(F32)
        t3 = t3 + lane_sum(gap * go_ref[:, at].astype(F32))

    for j in range(4):
        at = slice(j * 256, j * 256 + 256)
        gs_ref[:, at] = dot_nt(gox_ref[...], wout_ref[at, :])

    def back_rows(i, carry):
        r = pl.multiple_of(i * 16, 16)
        zed = zed_ref[pl.ds(r, 16), :]
        grad = gs_ref[pl.ds(r, 16), :]
        gate = sigmoid(zed)
        grad_zed = grad * (gate * (1.0 + zed * (1.0 - gate)))
        mean = jnp.mean(grad_zed, axis=-1, keepdims=True)
        along = jnp.mean(grad_zed * zed, axis=-1, keepdims=True)
        result = (grad_zed - mean - zed * along) * zinv_ref[pl.ds(r, 16), 0:1]
        for g in range(0, 16, 8):
            for t in range(8):
                gsp2_ref[pl.ds((r + g) * 8 + t, 8, stride=8), :] = result[
                    g : g + 8, t * 128 : t * 128 + 128
                ]
        return carry

    lax.fori_loop(0, INNER // 16, back_rows, 0)

    def swished_rows(i, carry):
        r = pl.multiple_of(i * 16, 16)
        inner = pl.ds(pl.multiple_of(half + r, 16), 16)
        other = pl.ds(pl.multiple_of(INNER + r, 16), 16)
        gap = sw_ref[other, :].astype(F32) - sw_ref[inner, :].astype(F32)
        t2_ref[pl.ds(r, 16), :] = lane_sum(gap * gs_ref[inner, :])
        return carry

    lax.fori_loop(0, ROWS // 16, swished_rows, 0)
    depthwise(gsp2_ref, edge, taps_ref, forward[::-1], gg2_ref, ROWS)

    def mixed_rows(i, carry):
        r = pl.multiple_of(i * 16, 16)
        at = pl.ds(r, 16)
        frame = first_frame + r + lax.broadcasted_iota(jnp.int32, (16, 1), 0)
        grad = get_rows(gg2_ref, r, 16) * jnp.where(frame < length, 1.0, 0.0)
        gap = get_rows(g2_ref, CLEAN + half + r, 16) - get_rows(g2_ref, RIM + r, 16)
        t1_ref[at, :] = lane_sum(gap * grad)
        gate = sg_ref[at, :]
        gm_ref[at, 0:WIDTH] = (grad * gate).astype(BF16)
        gm_ref[at, WIDTH:] = (grad * mv_ref[at, :] * gate * (1.0 - gate)).astype(BF16)
        return carry

    lax.fori_loop(0, ROWS // 16, mixed_rows, 0)
    for j in range(4):
        at = slice(j * 256, j * 256 + 256)
        gl_ref[:, at] = dot_nt(gm_ref[...], win_ref[at, :])

    def resid_rows(i, carry):
        r = pl.multiple_of(i * 16, 16)
        at = pl.ds(r, 16)
        clean = resid_ref[pl.ds(pl.multiple_of(RIM + r, 16), 16), :].astype(F32)
        patch = resid_ref[pl.ds(pl.multiple_of(CLEAN + half + r, 16), 16), :].astype(F32)
        centred, inverse = moments(clean)
        normed = centred * inverse
        grad = gl_ref[at, :]
        mean = jnp.mean(grad, axis=-1, keepdims=True)
        along = jnp.mean(grad * normed, axis=-1, keepdims=True)
        grad_resid = go_ref[at, :].astype(F32) + (grad - mean - normed * along) * inverse
        t0_ref[at, :] = lane_sum((patch - clean) * grad_resid)
        return carry

    lax.fori_loop(0, ROWS // 16, resid_rows, 0)

    columns = [
        jnp.sum(part, axis=1, keepdims=True) for part in (t0_ref[...], t1_ref[...], t2_ref[...], t3)
    ]
    lane = lane_of(ROWS)
    chosen = jnp.zeros((ROWS, 128), F32)
    for i in range(attr_ref.shape[0]):
        site = site_ref[i]
        column = columns[0]
        for k in range(1, 4):
            column = jnp.where(site == k, columns[k], column)
        chosen = jnp.where(lane == i, column, chosen)
    attr_ref[...] = chosen.T[: attr_ref.shape[0]]

    for part in range(4):
        lo = (part // 2) * 512
        dest = part * 256
        source = low_ref if part < 2 else sw_ref
        row = RIM if part < 2 else half
        lo = (part % 2) * 512
        first = source[row : row + ROWS, lo : lo + 256].astype(F32)
        second = source[row : row + ROWS, lo + 256 : lo + 512].astype(F32)
        own_ref[:, dest : dest + 256] = jnp.where(core == 0, first, second).astype(BF16)
        send_ref[:, dest : dest + 256] = jnp.where(core == 0, second, first).astype(BF16)


def weight_kernel(own_ref, other_ref, gm_ref, gm_other, go_ref, go_other, out_ref):
    low = jnp.concatenate([own_ref[:, 0:512], other_ref[:, 0:512]], axis=0)
    swished = jnp.concatenate([own_ref[:, 512:1024], other_ref[:, 512:1024]], axis=0)
    for j in range(0, 2 * WIDTH, 256):
        grads = jnp.concatenate([gm_ref[:, j : j + 256], gm_other[:, j : j + 256]], axis=0)
        out_ref[:, j : j + 256] = dot_tn(low, grads).astype(BF16)
    for j in range(0, WIDTH, 256):
        grads = jnp.concatenate([go_ref[:, j : j + 256], go_other[:, j : j + 256]], axis=0)
        out_ref[:, 2 * WIDTH + j : 2 * WIDTH + j + 256] = dot_tn(swished, grads).astype(BF16)


VMEM = pl.BlockSpec(memory_space=pltpu.VMEM)
SMEM = pl.BlockSpec(memory_space=pltpu.SMEM)


def kernel_call(body, out_shape, in_specs, scratch, limit, flops, moved):
    return pl.pallas_call(
        body,
        out_shape=out_shape,
        in_specs=in_specs,
        out_specs=[VMEM] * len(out_shape),
        scratch_shapes=scratch,
        compiler_params=pltpu.CompilerParams(vmem_limit_bytes=limit << 20),
        cost_estimate=pl.CostEstimate(flops=flops, bytes_accessed=moved, transcendentals=0),
    )


def shape(dims, dtype):
    return jax.ShapeDtypeStruct(dims, dtype)


def per_device(
    clean_input, corrupt_input, patch_mask, lengths, site_ids, w_query, w_key, w_value,
    w_attn_out, w_pointwise_in, depth_kernel, w_pointwise_out, cotangent,
):
    frames = lax.axis_size("frames")
    position = lax.axis_index("frames")
    core = lax.rem(lax.axis_index("dp"), 2)
    scalars = jnp.stack(
        [position * ROWS, lengths[0], core, lax.rem(position, 2)]
    ).astype(jnp.int32)
    clean, corrupt, cot = clean_input[0], corrupt_input[0], cotangent[0]

    msg, patched, up, down = kernel_call(
        project_kernel,
        [shape((frames, ROWS + 32, 128), BF16), shape((ROWS, WIDTH), BF16),
         shape((2 * RIM, WIDTH), BF16), shape((2 * RIM, WIDTH), BF16)],
        [VMEM] * 7,
        [pltpu.VMEM((2 * ROWS, WIDTH), BF16), pltpu.VMEM((ROWS, ROWS), F32)],
        24, 8 * 10**8, 6 * 10**6,
    )(clean, corrupt, cot, patch_mask, w_query, w_key, w_value)
    forward = [(i, i + 1) for i in range(frames - 1)]
    backward = [(i + 1, i) for i in range(frames - 1)]
    from_left = lax.ppermute(up, "frames", forward)
    from_right = lax.ppermute(down, "frames", backward)
    recv = lax.all_to_all(msg, "frames", 0, 0, tiled=True)
    count = frames * ROWS
    (context,) = kernel_call(
        attend_kernel,
        [shape((frames, 48, 128), BF16)],
        [SMEM, VMEM],
        [pltpu.VMEM((128, count), BF16), pltpu.VMEM((count, 128), BF16),
         pltpu.VMEM((256, count), F32), pltpu.VMEM((256, count), F32),
         pltpu.VMEM((256, 128), F32), pltpu.VMEM((256, 128), F32),
         pltpu.VMEM((frames * 32, 128), F32)],
        40, 8 * 10**9, 10**6,
    )(scalars, recv)
    contexts = lax.all_to_all(context, "frames", 0, 0, tiled=True)
    attribution, own, send, grad_mixed, grad_output = kernel_call(
        block_kernel,
        [shape((site_ids.shape[0], ROWS), F32), shape((ROWS, 1024), BF16), shape((ROWS, 1024), BF16),
         shape((ROWS, 2 * WIDTH), BF16), shape((ROWS, WIDTH), BF16)],
        [SMEM, SMEM] + [VMEM] * 10,
        [pltpu.VMEM((BOTH, 512), BF16), pltpu.VMEM((BOTH, WIDTH), BF16),
         pltpu.VMEM((BOTH, WIDTH), BF16), pltpu.VMEM((BOTH, WIDTH), BF16),
         pltpu.VMEM((ROWS, WIDTH), F32), pltpu.VMEM((ROWS, WIDTH), F32),
         pltpu.VMEM((BOTH * 8, 128), F32), pltpu.VMEM((INNER * 8, 128), F32),
         pltpu.VMEM((INNER, WIDTH), F32), pltpu.VMEM((INNER, 128), F32),
         pltpu.VMEM((INNER + ROWS, WIDTH), BF16), pltpu.VMEM((INNER, WIDTH), BF16),
         pltpu.VMEM((INNER, WIDTH), F32), pltpu.VMEM((INNER * 8, 128), F32),
         pltpu.VMEM((ROWS * 8, 128), F32), pltpu.VMEM((ROWS, WIDTH), F32),
         pltpu.VMEM((ROWS, 128), F32), pltpu.VMEM((ROWS, 128), F32), pltpu.VMEM((ROWS, 128), F32),
         pltpu.VMEM((32 * 8, 128), F32)],
        48, 4 * 10**9, 10**7,
    )(scalars, site_ids, contexts, clean, patched, cot, from_left, from_right,
      w_attn_out, w_pointwise_in, depth_kernel, w_pointwise_out)

    cores = [(i, i ^ 1) for i in range(lax.axis_size("dp"))]
    other, gm_other, go_other = (
        lax.ppermute(part, "dp", cores) for part in (send, grad_mixed, grad_output)
    )
    (partial,) = kernel_call(
        weight_kernel,
        [shape((512, 3 * WIDTH), BF16)],
        [VMEM] * 6,
        [],
        32, 8 * 10**8, 10**7,
    )(own, other, grad_mixed, gm_other, grad_output, go_other)
    groups = [
        [(2 * y + c) * frames + f for y in range(2) for f in range(frames)] for c in range(2)
    ]
    pieces = lax.all_to_all(
        partial.reshape(2 * frames, 8, 3 * WIDTH), ("dp", "frames"), 0, 0,
        axis_index_groups=groups, tiled=True,
    )
    summed = jnp.sum(pieces.astype(F32), axis=0)
    return attribution[None], summed[:, : 2 * WIDTH], summed[:, 2 * WIDTH :]


def solution(mesh):
    placed = (
        P("dp", "frames", None), P("dp", "frames", None), P("dp", "frames"), P("dp"), P(), P(), P(),
        P(), P(), P(), P(), P(), P("dp", "frames", None),
    )
    return jax.shard_map(
        per_device,
        mesh=mesh,
        in_specs=placed,
        out_specs=(P("dp", None, "frames"), P(("dp", "frames"), None), P(("dp", "frames"), None)),
        check_vma=False,
    )
```

time: 1380 us -> 161 us (0.12)
  waiting for transfers between devices: 1200 us -> 23.8 us
  matrix products: 66.2 us -> 0 us
  blocking collectives: 0 us -> 52.2 us
  Pallas kernels: 0 us -> 47.7 us
  other arithmetic: 35.5 us -> 0.53 us
  local copies, waits for them, and re-layouts: 30.1 us -> 10 us
    reduce_scatter x1 -> x0, waiting for transfers between devices: 645 us -> none  [per_device(): lax.psum_scatter(jnp.concatenate((contract_rows(lowered, grad_mixed), con...]
    all_gather x4 -> x0, waiting for transfers between devices: 552 us -> none  [the longest x1 152 us: per_device(): lax.all_gather(clean_values, 'frames', axis=0, tiled=True)]
    dot_general x20 -> x0, matrix products: 66.2 us -> none  [the longest x2 21.6 us: attend_step(): jnp.einsum('qhd,khd->hqk', query_heads, key_heads, preferred_element_type...]
    all_to_all x0 -> x1, blocking collectives: none -> 52.2 us  [per_device(): lax.all_to_all(partial.reshape(2 * frames, 8, 3 * WIDTH), ('dp', 'frames'...]
    pallas_call x0 -> x4, Pallas kernels: none -> 47.7 us  [the longest x1 24.8 us: per_device(): kernel_call(block_kernel, [shape((site_ids.shape[0], ROWS), F32), shape((...]
    all_gather x4 -> x0, local copies, waits for them, and re-layouts: 25.6 us -> none  [the longest x1 6.41 us: per_device(): lax.all_gather(clean_keys, 'frames', axis=0, tiled=True)]
    reduce_sum x12 -> x1, other arithmetic: 24.1 us -> 0.46 us  [per_device(): summed = jnp.sum(pieces.astype(F32), axis=0)]
    all_to_all x0 -> x2, waiting for transfers between devices: none -> 17.4 us  [the longest x1 17.4 us: per_device(): recv = lax.all_to_all(msg, 'frames', 0, 0, tiled=True)]
  transfers between devices with their start and end apart: 11 -> 7, of which waited for: 6 -> 5; matrix products, arithmetic and copies ran while one was open for 6% -> 0% of each run, Pallas kernels for 0% -> 0%
where the time goes in v1:
time: 161 us; the launch traced here: 158 us
  blocking collectives  52.2 us (32%)
  Pallas kernels  47.7 us (30%)
  waiting for transfers between devices  23.8 us (15%)
  starting transfers between devices  22.3 us (14%)
  local copies, waits for them, and re-layouts  10 us (6%)
    all_to_all x1, blocking collectives, per_device(): lax.all_to_all(partial.reshape(2 * frames, 8, 3 * WIDTH), ('dp', 'frames'...  52.2 us
    pallas_call x1, Pallas kernels, per_device(): kernel_call(block_kernel, [shape((site_ids.shape[0], ROWS), F32), shape((...  24.8 us
    pallas_call x1, Pallas kernels, per_device(): kernel_call(attend_kernel, [shape((frames, 48, 128), BF16)], [SMEM, VMEM]...  17.5 us
    all_to_all x1, waiting for transfers between devices, per_device(): recv = lax.all_to_all(msg, 'frames', 0, 0, tiled=True)  17.4 us
    all_to_all x1, starting transfers between devices, per_device(): recv = lax.all_to_all(msg, 'frames', 0, 0, tiled=True)  9.36 us
    unnamed x26, local copies, waits for them, and re-layouts  8.78 us
    all_to_all x1, starting transfers between devices, per_device(): contexts = lax.all_to_all(context, 'frames', 0, 0, tiled=True)  6.43 us
    pallas_call x1, Pallas kernels, per_device(): kernel_call(project_kernel, [shape((frames, ROWS + 32, 128), BF16), shape...  4.33 us
  transfers between devices with their start and end apart: 7, of which 5 were waited for; matrix products, arithmetic and copies ran while one was open for 0% of the time, Pallas kernels for 0%

profile of v1, /device:TPU:10, one launch (start us, length us, event | category | flops | bytes accessed | tf_op | source)
XLA Modules:
  0.0 157.9 jit_solution(17185841529857943195)
XLA Ops:
  0.6 0.0 copy-start
  0.6 1.2 copy-done
  1.9 0.0 copy-start.1
  1.9 1.2 copy-done.1
  3.1 0.0 copy-start.2
  3.1 1.2 copy-done.2
  4.3 0.9 copy-done.3
  5.3 0.0 copy-start.4
  5.3 0.9 copy-done.4
  6.2 0.0 copy-start.6
  6.2 0.9 copy-done.6
  7.2 0.0 copy-start.8
  7.2 0.7 copy-done.8
  7.8 4.3 %shard_map.148 = (bf16[32,160,128]{2,1,0:T(8,128)(2,1)}, bf16[128,1024]{1,0:T(8,128)(2,1)S(1)}, bf16[64,1024]{1,0:T(8,128)(2,1)S(1)}, bf16[64,1024]{1,0:T(8,128)(2,1)S(1)}) custom-call(bf16[128,1024]{1,0:T(8,128)(2,1)S(1)} %bitcast.10, bf16[128,1024]{1,0:T(8,128)(2,1)S(1)} %bitcast.9, bf16[128,1024]{1,0:T(8,128)(2,1)S(1)} %bitcast.12, ...), custom_call_target="tpu_custom_call" | custom-call | flops 800000000 | bytes 6000000 | tf_op jit(solution)/shard_map/pallas_call | solution.py:503
  12.1 9.4 %all-to-all-start = ((bf16[32,160,128]{2,1,0:T(8,128)(2,1)}), bf16[32,160,128]{2,1,0:T(8,128)(2,1)S(1)}, u32[]{:S(2)}, u32[]{:S(2)}) async-start(bf16[32,160,128]{2,1,0:T(8,128)(2,1)} %get-tuple-element.12), calls=%async_computation | async-start | bytes 2621440 | tf_op jit(solution)/shard_map/all_to_all | solution.py:515
  22.2 0.1 pad_add_fusion.scal_ref
  22.2 0.0 copy-start.5
  22.2 0.0 copy-start.7
  22.2 0.0 copy-start.10
  22.3 0.0 copy-start.11
  22.3 0.0 copy-start.12
  22.3 17.4 %all-to-all-done.recv_ref = bf16[32,160,128]{2,1,0:T(8,128)(2,1)S(1)} async-done(((bf16[32,160,128]{2,1,0:T(8,128)(2,1)}), bf16[32,160,128]{2,1,0:T(8,128)(2,1)S(1)}, u32[]{:S(2)}, u32[]{:S(2)}) %all-to-all-start) | async-done | bytes 1310752 | tf_op jit(solution)/shard_map/all_to_all | solution.py:515
  39.7 17.5 %shard_map.149 = bf16[32,48,128]{2,1,0:T(8,128)(2,1)} custom-call(s32[4]{0:T(128)S(1)} %pad_add_fusion.scal_ref, bf16[32,160,128]{2,1,0:T(8,128)(2,1)S(1)} %all-to-all-done.recv_ref), custom_call_target="tpu_custom_call" | custom-call | flops 8000000000 | bytes 1000000 | tf_op jit(solution)/shard_map/pallas_call | solution.py:517
  57.2 6.4 %all-to-all-start.1 = ((bf16[32,48,128]{2,1,0:T(8,128)(2,1)}), bf16[32,48,128]{2,1,0:T(8,128)(2,1)S(1)}, u32[]{:S(2)}, u32[]{:S(2)}) async-start(bf16[32,48,128]{2,1,0:T(8,128)(2,1)} %shard_map.149), calls=%async_computation.1 | async-start | bytes 786432 | tf_op jit(solution)/shard_map/all_to_all | solution.py:527
  63.6 3.4 %collective-permute-start = (bf16[64,1024]{1,0:T(8,128)(2,1)S(1)}, bf16[64,1024]{1,0:T(8,128)(2,1)S(1)}, u32[]{:S(2)}, u32[]{:S(2)}) collective-permute-start(bf16[64,1024]{1,0:T(8,128)(2,1)S(1)} %get-tuple-element.14), channel_id=1, source_target_pairs={{0,1},{1,2},{2,3},{3,4},{4,5},{5,6},{6,7},{7,8},{8,9},{9,10},{10,1... | collective-permute-start | bytes 393224 | tf_op jit(solution)/shard_map/ppermute | solution.py:513
  67.0 2.7 %collective-permute-start.1 = (bf16[64,1024]{1,0:T(8,128)(2,1)S(1)}, bf16[64,1024]{1,0:T(8,128)(2,1)S(1)}, u32[]{:S(2)}, u32[]{:S(2)}) collective-permute-start(bf16[64,1024]{1,0:T(8,128)(2,1)S(1)} %get-tuple-element.15), channel_id=1, source_target_pairs={{1,0},{2,1},{3,2},{4,3},{5,4},{6,5},{7,6},{8,7},{9,8},{10,9},{11,1... | collective-permute-start | bytes 393224 | tf_op jit(solution)/shard_map/ppermute | solution.py:514
  69.7 1.9 %collective-permute-done.up_ref = bf16[64,1024]{1,0:T(8,128)(2,1)S(1)} collective-permute-done((bf16[64,1024]{1,0:T(8,128)(2,1)S(1)}, bf16[64,1024]{1,0:T(8,128)(2,1)S(1)}, u32[]{:S(2)}, u32[]{:S(2)}) %collective-permute-start) | collective-permute-done | bytes 131104 | tf_op jit(solution)/shard_map/ppermute | solution.py:513
  71.5 2.4 %collective-permute-done.1.down_ref = bf16[64,1024]{1,0:T(8,128)(2,1)S(1)} collective-permute-done((bf16[64,1024]{1,0:T(8,128)(2,1)S(1)}, bf16[64,1024]{1,0:T(8,128)(2,1)S(1)}, u32[]{:S(2)}, u32[]{:S(2)}) %collective-permute-start.1) | collective-permute-done | bytes 131104 | tf_op jit(solution)/shard_map/ppermute | solution.py:514
  73.9 0.0 all-to-all-done.1.ctx_in
  73.9 0.0 copy-done.5
  73.9 0.0 copy-done.7
  73.9 0.0 copy-done.10
  73.9 0.0 copy-done.11
  73.9 0.0 copy-done.12
  73.9 0.0 copy-start.9
  73.9 1.6 %copy-done.9 = bf16[1024,1024]{1,0:T(8,128)(2,1)S(1)} copy-done((bf16[1024,1024]{1,0:T(8,128)(2,1)S(1)}, bf16[1024,1024]{1,0:T(8,128)(2,1)}, u32[]{:S(2)}) %copy-start.9) | copy-done | bytes 2097176
  75.5 24.8 %shard_map.150 = (f32[8,128]{1,0:T(8,128)}, bf16[128,1024]{1,0:T(8,128)(2,1)S(1)}, bf16[128,1024]{1,0:T(8,128)(2,1)S(1)}, bf16[128,2048]{1,0:T(8,128)(2,1)S(1)}, bf16[128,1024]{1,0:T(8,128)(2,1)S(1)}) custom-call(s32[4]{0:T(128)S(1)} %pad_add_fusion.scal_ref, s32[8]{0:T(128)S(1)} %copy-done.12, bf16[32,48,128]{2,1,0:T(8,128)(2,1)S(1)} %all-to-all-done.1.ctx_in, ...), custom_call_target="tpu_custom_call" | custom-call | flops 4000000000 | bytes 10000000 | tf_op jit(solution)/shard_map/pallas_call | solution.py:528
  100.3 0.0 collective-permute-start.3
  100.3 0.5 collective-permute-start.2
  100.8 0.0 collective-permute-start.4
  100.8 1.8 %collective-permute-done.2.other_ref = bf16[128,1024]{1,0:T(8,128)(2,1)S(1)} collective-permute-done((bf16[128,1024]{1,0:T(8,128)(2,1)S(1)}, bf16[128,1024]{1,0:T(8,128)(2,1)S(1)}, u32[]{:S(2)}, u32[]{:S(2)}) %collective-permute-start.2) | collective-permute-done | bytes 262176 | tf_op jit(solution)/shard_map/ppermute | solution.py:549
  102.6 0.4 collective-permute-done.4.go_other
  103.0 0.0 collective-permute-done.3.gm_other
  103.0 1.0 shard_map.151
  104.0 52.2 %all_to_all.15 = bf16[64,8,3072]{2,1,0:T(8,128)(2,1)S(1)} all-to-all(bf16[64,8,3072]{2,1,0:T(8,128)(2,1)S(1)} %bitcast.8), channel_id=1, replica_groups={{0,1,2,3,4,5,6,7,8,9,10,11,12,13,14,15,16,17,18,19,20,21,22,23,24,25,26..., dimensions={0} | all-to-all | bytes 6291456 | tf_op jit(solution)/shard_map/all_to_all | solution.py:561
  156.2 0.5 convert_reduce_fusion
  156.6 0.6 slice.9
  157.3 0.6 slice.8
  (1 shorter events, 0.0 us)
Async XLA Ops:
  0.6 1.2 copy-start
  1.9 1.2 copy-start.1
  3.1 1.2 copy-start.2
  4.3 0.9 copy-start.3
  5.3 0.9 copy-start.4
  6.2 0.9 copy-start.6
  7.2 0.7 copy-start.8
  12.1 27.5 %all-to-all-start = ((bf16[32,160,128]{2,1,0:T(8,128)(2,1)}), bf16[32,160,128]{2,1,0:T(8,128)(2,1)S(1)}, u32[]{:S(2)}, u32[]{:S(2)}) async-start(bf16[32,160,128]{2,1,0:T(8,128)(2,1)} %get-tuple-element.12), calls=%async_computation | async-start | bytes 2621440 | tf_op jit(solution)/shard_map/all_to_all | solution.py:515
  22.2 51.6 %copy-start.5 = (bf16[1,128,1024]{2,1,0:T(8,128)(2,1)S(1)}, bf16[1,128,1024]{2,1,0:T(8,128)(2,1)}, u32[]{:S(2)}) copy-start(bf16[1,128,1024]{2,1,0:T(8,128)(2,1)} %param.13) | copy-start | bytes 786436
  22.2 51.6 %copy-start.7 = (bf16[1,128,1024]{2,1,0:T(8,128)(2,1)S(1)}, bf16[1,128,1024]{2,1,0:T(8,128)(2,1)}, u32[]{:S(2)}) copy-start(bf16[1,128,1024]{2,1,0:T(8,128)(2,1)} %param.25) | copy-start | bytes 786436
  22.2 51.6 %copy-start.10 = (bf16[512,1024]{1,0:T(8,128)(2,1)S(1)}, bf16[512,1024]{1,0:T(8,128)(2,1)}, u32[]{:S(2)}) copy-start(bf16[512,1024]{1,0:T(8,128)(2,1)} %wao_ref.1) | copy-start | bytes 3145732
  22.3 51.6 %copy-start.11 = (bf16[31,1024]{1,0:T(8,128)(2,1)S(1)}, bf16[31,1024]{1,0:T(8,128)(2,1)}, u32[]{:S(2)}) copy-start(bf16[31,1024]{1,0:T(8,128)(2,1)} %depth_ref.1) | copy-start | bytes 190468
  22.3 51.6 %copy-start.12 = (s32[8]{0:T(128)S(1)}, s32[8]{0:T(128)}, u32[]{:S(2)}) copy-start(s32[8]{0:T(128)} %site_ref.1) | copy-start | bytes 100
  57.2 16.7 %all-to-all-start.1 = ((bf16[32,48,128]{2,1,0:T(8,128)(2,1)}), bf16[32,48,128]{2,1,0:T(8,128)(2,1)S(1)}, u32[]{:S(2)}, u32[]{:S(2)}) async-start(bf16[32,48,128]{2,1,0:T(8,128)(2,1)} %shard_map.149), calls=%async_computation.1 | async-start | bytes 786432 | tf_op jit(solution)/shard_map/all_to_all | solution.py:527
  63.6 7.9 %collective-permute-start = (bf16[64,1024]{1,0:T(8,128)(2,1)S(1)}, bf16[64,1024]{1,0:T(8,128)(2,1)S(1)}, u32[]{:S(2)}, u32[]{:S(2)}) collective-permute-start(bf16[64,1024]{1,0:T(8,128)(2,1)S(1)} %get-tuple-element.14), channel_id=1, source_target_pairs={{0,1},{1,2},{2,3},{3,4},{4,5},{5,6},{6,7},{7,8},{8,9},{9,10},{10,1... | collective-permute-start | bytes 393224 | tf_op jit(solution)/shard_map/ppermute | solution.py:513
  67.0 6.9 %collective-permute-start.1 = (bf16[64,1024]{1,0:T(8,128)(2,1)S(1)}, bf16[64,1024]{1,0:T(8,128)(2,1)S(1)}, u32[]{:S(2)}, u32[]{:S(2)}) collective-permute-start(bf16[64,1024]{1,0:T(8,128)(2,1)S(1)} %get-tuple-element.15), channel_id=1, source_target_pairs={{1,0},{2,1},{3,2},{4,3},{5,4},{6,5},{7,6},{8,7},{9,8},{10,9},{11,1... | collective-permute-start | bytes 393224 | tf_op jit(solution)/shard_map/ppermute | solution.py:514
  73.9 1.6 %copy-start.9 = (bf16[1024,1024]{1,0:T(8,128)(2,1)S(1)}, bf16[1024,1024]{1,0:T(8,128)(2,1)}, u32[]{:S(2)}) copy-start(bf16[1024,1024]{1,0:T(8,128)(2,1)} %wout_ref.1) | copy-start | bytes 6291460
  100.3 2.7 %collective-permute-start.3 = (bf16[128,2048]{1,0:T(8,128)(2,1)S(1)}, bf16[128,2048]{1,0:T(8,128)(2,1)S(1)}, u32[]{:S(2)}, u32[]{:S(2)}) collective-permute-start(bf16[128,2048]{1,0:T(8,128)(2,1)S(1)} %get-tuple-element.19.gm_ref), channel_id=1, source_target_pairs={{0,32},{32,0},{64,96},{96,64},{1,33},{33,1},{65,97},{97,65},{2,34}... | collective-permute-start | bytes 1572872 | tf_op jit(solution)/shard_map/ppermute | solution.py:549
  100.3 2.3 %collective-permute-start.2 = (bf16[128,1024]{1,0:T(8,128)(2,1)S(1)}, bf16[128,1024]{1,0:T(8,128)(2,1)S(1)}, u32[]{:S(2)}, u32[]{:S(2)}) collective-permute-start(bf16[128,1024]{1,0:T(8,128)(2,1)S(1)} %get-tuple-element.18), channel_id=1, source_target_pairs={{0,32},{32,0},{64,96},{96,64},{1,33},{33,1},{65,97},{97,65},{2,34}... | collective-permute-start | bytes 786440 | tf_op jit(solution)/shard_map/ppermute | solution.py:549
  100.8 2.1 %collective-permute-start.4 = (bf16[128,1024]{1,0:T(8,128)(2,1)S(1)}, bf16[128,1024]{1,0:T(8,128)(2,1)S(1)}, u32[]{:S(2)}, u32[]{:S(2)}) collective-permute-start(bf16[128,1024]{1,0:T(8,128)(2,1)S(1)} %get-tuple-element.20.go_ref), channel_id=1, source_target_pairs={{0,32},{32,0},{64,96},{96,64},{1,33},{33,1},{65,97},{97,65},{2,34}... | collective-permute-start | bytes 786440 | tf_op jit(solution)/shard_map/ppermute | solution.py:549

commit v2 on v1

--- a/solution.py
+++ b/solution.py
@@ -61,11 +61,29 @@
 
 
 def project_kernel(
-    clean_ref, corrupt_ref, cot_ref, mask_ref, wq_ref, wk_ref, wv_ref,
-    msg_ref, patched_ref, up_ref, down_ref, hidden_ref, mask_col,
+    clean_hbm, corrupt_hbm, cot_hbm, mask_ref, wq_hbm, wk_hbm, wv_hbm,
+    msg_ref, patched_ref, up_ref, down_ref,
+    hidden_ref, mask_col, clean_ref, corrupt_ref, wq_ref, wk_ref, wv_ref, sems,
 ):
+    half = RIM // 2
+    copies = [
+        pltpu.make_async_copy(source, target, sems.at[i])
+        for i, (source, target) in enumerate((
+            (clean_hbm, clean_ref),
+            (corrupt_hbm, corrupt_ref),
+            (wk_hbm, wk_ref),
+            (wv_hbm, wv_ref),
+            (wq_hbm, wq_ref),
+            (cot_hbm.at[pl.ds(ROWS - half, half)], up_ref.at[pl.ds(RIM + half, half)]),
+            (cot_hbm.at[pl.ds(0, half)], down_ref.at[pl.ds(RIM + half, half)]),
+        ))
+    ]
+    for copy in copies:
+        copy.start()
     spread_mask = jnp.broadcast_to(mask_ref[...].astype(F32), (ROWS, ROWS))
     mask_col[...] = spread_mask.T
+    copies[0].wait()
+    copies[1].wait()
 
     def rows(i, carry):
         at = pl.ds(pl.multiple_of(i * 16, 16), 16)
@@ -80,13 +98,12 @@
         return carry
 
     lax.fori_loop(0, ROWS // 16, rows, 0)
-    half = RIM // 2
     up_ref[0:RIM, :] = clean_ref[ROWS - RIM : ROWS, :]
     up_ref[RIM : RIM + half, :] = patched_ref[ROWS - half : ROWS, :]
-    up_ref[RIM + half :, :] = cot_ref[ROWS - half : ROWS, :]
     down_ref[0:RIM, :] = clean_ref[0:RIM, :]
     down_ref[RIM : RIM + half, :] = patched_ref[0:half, :]
-    down_ref[RIM + half :, :] = cot_ref[0:half, :]
+    for copy in copies[2:]:
+        copy.wait()
 
     low = lane_of(ROWS) < 64
     low_q = lane_of(32) < 64
@@ -245,46 +262,28 @@
     return jnp.concatenate(groups, axis=0) if len(groups) > 1 else groups[0]
 
 
-def block_kernel(
-    scal_ref, site_ref, ctx_in, clean_ref, patched_ref, cot_ref, up_ref, down_ref,
-    wao_ref, win_ref, depth_ref, wout_ref,
-    attr_ref, own_ref, send_ref, gm_ref, go_ref,
-    ctx_ref, x_ref, resid_ref, low_ref, mv_ref, sg_ref, g2_ref, s2_ref, zed_ref, zinv_ref,
-    sw_ref, gox_ref, gs_ref, gsp2_ref, gg2_ref, gl_ref, t0_ref, t1_ref, t2_ref, taps_ref,
-):
-    first_frame, length, core = scal_ref[0], scal_ref[1], scal_ref[2]
-    half = RIM // 2
-
-    for run in range(2):
-        for t in range(HEADS // 2):
-            at = slice(t * 128, t * 128 + 128)
-            base = run * 16 + t * 4
-            halves = {}
-            for side in range(2):
-                even = ctx_in[base + side].astype(F32)
-                odd = ctx_in[base + 2 + side].astype(F32)
-                low = lane_of(48) < 64
-                halves[side] = (
-                    jnp.where(low, even, swap(odd)).astype(BF16),
-                    jnp.where(low, swap(even), odd).astype(BF16),
-                )
-            (lo0, hi0), (lo1, hi1) = halves[0], halves[1]
-            parts = [lo1[32:48], hi1[32:48], lo0[:32], hi0[:32], lo1[:32], hi1[:32], lo0[32:48], hi0[32:48]]
-            row = 0
-            if run == 1:
-                parts = parts[1:-1]
-                row = CLEAN
-            for part in parts:
-                ctx_ref[row : row + part.shape[0], at] = part
-                row += part.shape[0]
-
-    x_ref[0:RIM, :] = up_ref[0:RIM, :]
-    x_ref[RIM : RIM + ROWS, :] = clean_ref[...]
-    x_ref[RIM + ROWS : CLEAN, :] = down_ref[0:RIM, :]
-    x_ref[CLEAN : CLEAN + half, :] = up_ref[RIM : RIM + half, :]
-    x_ref[CLEAN + half : CLEAN + half + ROWS, :] = patched_ref[...]
-    x_ref[CLEAN + half + ROWS : BOTH, :] = down_ref[RIM : RIM + half, :]
-
+def place_context(ctx_in, ctx_ref, run, trimmed):
+    low = lane_of(48) < 64
+    for t in range(HEADS // 2):
+        at = slice(t * 128, t * 128 + 128)
+        base = run * 16 + t * 4
+        halves = []
+        for side in range(2):
+            even = ctx_in[base + side].astype(F32)
+            odd = ctx_in[base + 2 + side].astype(F32)
+            halves.append((
+                jnp.where(low, even, swap(odd)).astype(BF16),
+                jnp.where(low, swap(even), odd).astype(BF16),
+            ))
+        (lo0, hi0), (lo1, hi1) = halves
+        parts = [lo1[32:48], hi1[32:48], lo0[:32], hi0[:32], lo1[:32], hi1[:32], lo0[32:48], hi0[32:48]]
+        row = 0
+        for part in parts[1:-1] if trimmed else parts:
+            ctx_ref[row : row + part.shape[0], at] = part
+            row += part.shape[0]
+
+
+def place_taps(depth_ref, taps_ref):
     for r in range(0, KERNEL + 1, 8):
         got = min(8, KERNEL - r)
         block = depth_ref[r : r + got, :].astype(F32)
@@ -293,7 +292,51 @@
         for t in range(8):
             put_rows(taps_ref, r, t, block[:, t * 128 : t * 128 + 128])
 
-    frame0 = first_frame - half
+
+def to_lowered(x_ref, ctx_ref, wao_ref, resid_ref, low_ref):
+    for j in range(4):
+        at = slice(j * 256, j * 256 + 256)
+        joined = x_ref[:, at].astype(F32) + dot(ctx_ref[...], wao_ref[:, at])
+        resid_ref[:, at] = joined.astype(BF16)
+
+    def lower(i, carry):
+        at = pl.ds(pl.multiple_of(i * 16, 16), 16)
+        centred, inverse = moments(resid_ref[at, :].astype(F32))
+        low_ref[at, :] = (centred * inverse).astype(BF16)
+        return carry
+
+    lax.fori_loop(0, x_ref.shape[0] // 16, lower, 0)
+
+
+def to_gated(low_ref, win_ref, g2_ref, frame, length, keep):
+    live = jnp.where((frame >= 0) & (frame < length), 1.0, 0.0)
+    for j in range(4):
+        at = slice(j * 256, j * 256 + 256)
+        gate_at = slice(WIDTH + j * 256, WIDTH + j * 256 + 256)
+        value = dot(low_ref[...], win_ref[:, at])
+        gate = sigmoid(dot(low_ref[...], win_ref[:, gate_at]))
+        if keep is not None:
+            mv_ref, sg_ref = keep
+            mv_ref[:, at] = value[RIM : RIM + ROWS]
+            sg_ref[:, at] = gate[RIM : RIM + ROWS]
+        gated = (value * gate * live).astype(BF16).astype(F32)
+        for t in range(2):
+            put_rows(g2_ref, 0, j * 2 + t, gated[:, t * 128 : t * 128 + 128])
+
+
+def clean_kernel(
+    scal_ref, ctx_in, clean_ref, cot_ref, up_ref, down_ref,
+    wao_ref, win_ref, depth_ref, wout_ref,
+    own_ref, send_ref, gm_ref, go_ref, sw_ref, gs_ref, gg2_ref, g2_ref, resid_ref,
+    ctx_ref, x_ref, low_ref, mv_ref, sg_ref, s2_ref, zed_ref, zinv_ref, gox_ref, gsp2_ref, taps_ref,
+):
+    first_frame, length, core = scal_ref[0], scal_ref[1], scal_ref[2]
+    half = RIM // 2
+    place_context(ctx_in, ctx_ref, 0, False)
+    x_ref[0:RIM, :] = up_ref[0:RIM, :]
+    x_ref[RIM : RIM + ROWS, :] = clean_ref[...]
+    x_ref[RIM + ROWS : CLEAN, :] = down_ref[0:RIM, :]
+    place_taps(depth_ref, taps_ref)
     for piece, row, offset in (
         (up_ref[RIM + half :, :], 0, -half),
         (cot_ref[...], half, 0),
@@ -305,33 +348,9 @@
         gox_ref[row : row + n, :] = (piece.astype(F32) * keep).astype(BF16)
     go_ref[...] = gox_ref[half : half + ROWS, :]
 
-    for j in range(4):
-        at = slice(j * 256, j * 256 + 256)
-        joined = x_ref[:, at].astype(F32) + dot(ctx_ref[...], wao_ref[:, at])
-        resid_ref[:, at] = joined.astype(BF16)
-
-    def lower(i, carry):
-        at = pl.ds(pl.multiple_of(i * 16, 16), 16)
-        centred, inverse = moments(resid_ref[at, :].astype(F32))
-        low_ref[at, :] = (centred * inverse).astype(BF16)
-        return carry
-
-    lax.fori_loop(0, BOTH // 16, lower, 0)
-
-    row = lax.broadcasted_iota(jnp.int32, (BOTH, 1), 0)
-    frame = first_frame + jnp.where(row < CLEAN, row - RIM, row - CLEAN - half)
-    live = jnp.where((frame >= 0) & (frame < length), 1.0, 0.0)
-    for j in range(4):
-        at = slice(j * 256, j * 256 + 256)
-        gate_at = slice(WIDTH + j * 256, WIDTH + j * 256 + 256)
-        value = dot(low_ref[...], win_ref[:, at])
-        gate = sigmoid(dot(low_ref[...], win_ref[:, gate_at]))
-        mv_ref[:, at] = value[RIM : RIM + ROWS]
-        sg_ref[:, at] = gate[RIM : RIM + ROWS]
-        gated = (value * gate * live).astype(BF16).astype(F32)
-        for t in range(2):
-            put_rows(g2_ref, 0, j * 2 + t, gated[:, t * 128 : t * 128 + 128])
-
+    to_lowered(x_ref, ctx_ref, wao_ref, resid_ref, low_ref)
+    frame = first_frame - RIM + lax.broadcasted_iota(jnp.int32, (CLEAN, 1), 0)
+    to_gated(low_ref, win_ref, g2_ref, frame, length, (mv_ref, sg_ref))
     forward = list(range(KERNEL))
     edge = half - KERNEL // 2
     depthwise(g2_ref, edge, taps_ref, forward, s2_ref, INNER)
@@ -346,25 +365,6 @@
         return carry
 
     lax.fori_loop(0, INNER // 16, clean_rows, 0)
-    depthwise(g2_ref, CLEAN + edge, taps_ref, forward, s2_ref, ROWS)
-
-    def patch_rows(i, carry):
-        r = pl.multiple_of(i * 16, 16)
-        centred, inverse = moments(get_rows(s2_ref, r, 16))
-        zed = centred * inverse
-        sw_ref[pl.ds(pl.multiple_of(INNER + r, 16), 16), :] = (zed * sigmoid(zed)).astype(BF16)
-        return carry
-
-    lax.fori_loop(0, ROWS // 16, patch_rows, 0)
-
-    t3 = jnp.zeros((ROWS, 128), F32)
-    for j in range(4):
-        at = slice(j * 256, j * 256 + 256)
-        out = dot(sw_ref[half : INNER + ROWS, :], wout_ref[:, at])
-        out_clean = resid_ref[RIM : RIM + ROWS, at].astype(F32) + out[:ROWS]
-        out_patch = resid_ref[CLEAN + half : CLEAN + half + ROWS, at].astype(F32) + out[ROWS + half :]
-        gap = out_patch.astype(BF16).astype(F32) - out_clean.astype(BF16).astype(F32)
-        t3 = t3 + lane_sum(gap * go_ref[:, at].astype(F32))
 
     for j in range(4):
         at = slice(j * 256, j * 256 + 256)
@@ -387,16 +387,6 @@
         return carry
 
     lax.fori_loop(0, INNER // 16, back_rows, 0)
-
-    def swished_rows(i, carry):
-        r = pl.multiple_of(i * 16, 16)
-        inner = pl.ds(pl.multiple_of(half + r, 16), 16)
-        other = pl.ds(pl.multiple_of(INNER + r, 16), 16)
-        gap = sw_ref[other, :].astype(F32) - sw_ref[inner, :].astype(F32)
-        t2_ref[pl.ds(r, 16), :] = lane_sum(gap * gs_ref[inner, :])
-        return carry
-
-    lax.fori_loop(0, ROWS // 16, swished_rows, 0)
     depthwise(gsp2_ref, edge, taps_ref, forward[::-1], gg2_ref, ROWS)
 
     def mixed_rows(i, carry):
@@ -404,14 +394,69 @@
         at = pl.ds(r, 16)
         frame = first_frame + r + lax.broadcasted_iota(jnp.int32, (16, 1), 0)
         grad = get_rows(gg2_ref, r, 16) * jnp.where(frame < length, 1.0, 0.0)
-        gap = get_rows(g2_ref, CLEAN + half + r, 16) - get_rows(g2_ref, RIM + r, 16)
-        t1_ref[at, :] = lane_sum(gap * grad)
         gate = sg_ref[at, :]
         gm_ref[at, 0:WIDTH] = (grad * gate).astype(BF16)
         gm_ref[at, WIDTH:] = (grad * mv_ref[at, :] * gate * (1.0 - gate)).astype(BF16)
         return carry
 
     lax.fori_loop(0, ROWS // 16, mixed_rows, 0)
+
+    for part in range(4):
+        dest = part * 256
+        source, row = (low_ref, RIM) if part < 2 else (sw_ref, half)
+        lo = (part % 2) * 512
+        first = source[row : row + ROWS, lo : lo + 256].astype(F32)
+        second = source[row : row + ROWS, lo + 256 : lo + 512].astype(F32)
+        own_ref[:, dest : dest + 256] = jnp.where(core == 0, first, second).astype(BF16)
+        send_ref[:, dest : dest + 256] = jnp.where(core == 0, second, first).astype(BF16)
+
+
+def patch_kernel(
+    scal_ref, site_ref, ctx_in, patched_ref, up_ref, down_ref,
+    wao_ref, win_ref, depth_ref, wout_ref,
+    gm_ref, go_ref, swc_ref, gs_ref, gg2_ref, g2c_ref, residc_ref,
+    attr_ref,
+    ctx_ref, x_ref, resid_ref, low_ref, g2_ref, s2_ref, sw_ref, gl_ref, t0_ref, t1_ref, t2_ref, taps_ref,
+):
+    first_frame, length = scal_ref[0], scal_ref[1]
+    half = RIM // 2
+    place_context(ctx_in, ctx_ref, 1, True)
+    x_ref[0:half, :] = up_ref[RIM : RIM + half, :]
+    x_ref[half : half + ROWS, :] = patched_ref[...]
+    x_ref[half + ROWS : PATCH, :] = down_ref[RIM : RIM + half, :]
+    place_taps(depth_ref, taps_ref)
+    to_lowered(x_ref, ctx_ref, wao_ref, resid_ref, low_ref)
+    frame = first_frame - half + lax.broadcasted_iota(jnp.int32, (PATCH, 1), 0)
+    to_gated(low_ref, win_ref, g2_ref, frame, length, None)
+    depthwise(g2_ref, half - KERNEL // 2, taps_ref, list(range(KERNEL)), s2_ref, ROWS)
+    sw_ref[0:ROWS, :] = swc_ref[half : half + ROWS, :]
+
+    def patch_rows(i, carry):
+        r = pl.multiple_of(i * 16, 16)
+        at = pl.ds(r, 16)
+        inner = pl.ds(pl.multiple_of(half + r, 16), 16)
+        centred, inverse = moments(get_rows(s2_ref, r, 16))
+        zed = centred * inverse
+        swished = (zed * sigmoid(zed)).astype(BF16)
+        sw_ref[pl.ds(pl.multiple_of(ROWS + r, 16), 16), :] = swished
+        gap = swished.astype(F32) - sw_ref[at, :].astype(F32)
+        t2_ref[at, :] = lane_sum(gap * gs_ref[inner, :])
+        frame = first_frame + r + lax.broadcasted_iota(jnp.int32, (16, 1), 0)
+        grad = get_rows(gg2_ref, r, 16) * jnp.where(frame < length, 1.0, 0.0)
+        gap = get_rows(g2_ref, half + r, 16) - get_rows(g2c_ref, RIM + r, 16)
+        t1_ref[at, :] = lane_sum(gap * grad)
+        return carry
+
+    lax.fori_loop(0, ROWS // 16, patch_rows, 0)
+
+    t3 = jnp.zeros((ROWS, 128), F32)
+    for j in range(4):
+        at = slice(j * 256, j * 256 + 256)
+        out = dot(sw_ref[...], wout_ref[:, at])
+        out_clean = residc_ref[RIM : RIM + ROWS, at].astype(F32) + out[:ROWS]
+        out_patch = resid_ref[half : half + ROWS, at].astype(F32) + out[ROWS:]
+        gap = out_patch.astype(BF16).astype(F32) - out_clean.astype(BF16).astype(F32)
+        t3 = t3 + lane_sum(gap * go_ref[:, at].astype(F32))
     for j in range(4):
         at = slice(j * 256, j * 256 + 256)
         gl_ref[:, at] = dot_nt(gm_ref[...], win_ref[at, :])
@@ -419,8 +464,8 @@
     def resid_rows(i, carry):
         r = pl.multiple_of(i * 16, 16)
         at = pl.ds(r, 16)
-        clean = resid_ref[pl.ds(pl.multiple_of(RIM + r, 16), 16), :].astype(F32)
-        patch = resid_ref[pl.ds(pl.multiple_of(CLEAN + half + r, 16), 16), :].astype(F32)
+        clean = residc_ref[pl.ds(pl.multiple_of(RIM + r, 16), 16), :].astype(F32)
+        patch = resid_ref[pl.ds(pl.multiple_of(half + r, 16), 16), :].astype(F32)
         centred, inverse = moments(clean)
         normed = centred * inverse
         grad = gl_ref[at, :]
@@ -445,31 +490,27 @@
         chosen = jnp.where(lane == i, column, chosen)
     attr_ref[...] = chosen.T[: attr_ref.shape[0]]
 
-    for part in range(4):
-        lo = (part // 2) * 512
-        dest = part * 256
-        source = low_ref if part < 2 else sw_ref
-        row = RIM if part < 2 else half
-        lo = (part % 2) * 512
-        first = source[row : row + ROWS, lo : lo + 256].astype(F32)
-        second = source[row : row + ROWS, lo + 256 : lo + 512].astype(F32)
-        own_ref[:, dest : dest + 256] = jnp.where(core == 0, first, second).astype(BF16)
-        send_ref[:, dest : dest + 256] = jnp.where(core == 0, second, first).astype(BF16)
-
 
 def weight_kernel(own_ref, other_ref, gm_ref, gm_other, go_ref, go_other, out_ref):
     low = jnp.concatenate([own_ref[:, 0:512], other_ref[:, 0:512]], axis=0)
     swished = jnp.concatenate([own_ref[:, 512:1024], other_ref[:, 512:1024]], axis=0)
+    def put(at, product):
+        half = product.shape[0] // 2
+        lower = product[:half].reshape(half // 8, 8, 256)
+        upper = product[half:].reshape(half // 8, 8, 256)
+        out_ref[:, :, at : at + 256] = jnp.concatenate([lower, upper], axis=1).astype(BF16)
+
     for j in range(0, 2 * WIDTH, 256):
         grads = jnp.concatenate([gm_ref[:, j : j + 256], gm_other[:, j : j + 256]], axis=0)
-        out_ref[:, j : j + 256] = dot_tn(low, grads).astype(BF16)
+        put(j, dot_tn(low, grads))
     for j in range(0, WIDTH, 256):
         grads = jnp.concatenate([go_ref[:, j : j + 256], go_other[:, j : j + 256]], axis=0)
-        out_ref[:, 2 * WIDTH + j : 2 * WIDTH + j + 256] = dot_tn(swished, grads).astype(BF16)
+        put(2 * WIDTH + j, dot_tn(swished, grads))
 
 
 VMEM = pl.BlockSpec(memory_space=pltpu.VMEM)
 SMEM = pl.BlockSpec(memory_space=pltpu.SMEM)
+HBM = pl.BlockSpec(memory_space=pltpu.HBM)
 
 
 def kernel_call(body, out_shape, in_specs, scratch, limit, flops, moved):
@@ -504,15 +545,19 @@
         project_kernel,
         [shape((frames, ROWS + 32, 128), BF16), shape((ROWS, WIDTH), BF16),
          shape((2 * RIM, WIDTH), BF16), shape((2 * RIM, WIDTH), BF16)],
-        [VMEM] * 7,
-        [pltpu.VMEM((2 * ROWS, WIDTH), BF16), pltpu.VMEM((ROWS, ROWS), F32)],
-        24, 8 * 10**8, 6 * 10**6,
+        [HBM] * 3 + [VMEM] + [HBM] * 3,
+        [pltpu.VMEM((2 * ROWS, WIDTH), BF16), pltpu.VMEM((ROWS, ROWS), F32),
+         pltpu.VMEM((ROWS, WIDTH), BF16), pltpu.VMEM((ROWS, WIDTH), BF16),
+         pltpu.VMEM((WIDTH, 512), BF16), pltpu.VMEM((WIDTH, 512), BF16),
+         pltpu.VMEM((WIDTH, 512), BF16), pltpu.SemaphoreType.DMA((7,))],
+        62, 8 * 10**8, 6 * 10**6,
     )(clean, corrupt, cot, patch_mask, w_query, w_key, w_value)
     forward = [(i, i + 1) for i in range(frames - 1)]
     backward = [(i + 1, i) for i in range(frames - 1)]
     from_left = lax.ppermute(up, "frames", forward)
     from_right = lax.ppermute(down, "frames", backward)
     recv = lax.all_to_all(msg, "frames", 0, 0, tiled=True)
+    recv, from_left, from_right = lax.optimization_barrier((recv, from_left, from_right))
     count = frames * ROWS
     (context,) = kernel_call(
         attend_kernel,
@@ -522,26 +567,23 @@
          pltpu.VMEM((256, count), F32), pltpu.VMEM((256, count), F32),
          pltpu.VMEM((256, 128), F32), pltpu.VMEM((256, 128), F32),
          pltpu.VMEM((frames * 32, 128), F32)],
-        40, 8 * 10**9, 10**6,
+        20, 8 * 10**9, 10**6,
     )(scalars, recv)
     contexts = lax.all_to_all(context, "frames", 0, 0, tiled=True)
-    attribution, own, send, grad_mixed, grad_output = kernel_call(
-        block_kernel,
-        [shape((site_ids.shape[0], ROWS), F32), shape((ROWS, 1024), BF16), shape((ROWS, 1024), BF16),
-         shape((ROWS, 2 * WIDTH), BF16), shape((ROWS, WIDTH), BF16)],
-        [SMEM, SMEM] + [VMEM] * 10,
-        [pltpu.VMEM((BOTH, 512), BF16), pltpu.VMEM((BOTH, WIDTH), BF16),
-         pltpu.VMEM((BOTH, WIDTH), BF16), pltpu.VMEM((BOTH, WIDTH), BF16),
+    own, send, grad_mixed, grad_output, swished, grad_swished, grad_gated, gated, resid = kernel_call(
+        clean_kernel,
+        [shape((ROWS, 1024), BF16), shape((ROWS, 1024), BF16), shape((ROWS, 2 * WIDTH), BF16),
+         shape((ROWS, WIDTH), BF16), shape((INNER, WIDTH), BF16), shape((INNER, WIDTH), F32),
+         shape((ROWS * 8, 128), F32), shape((CLEAN * 8, 128), F32), shape((CLEAN, WIDTH), BF16)],
+        [SMEM] + [VMEM] * 9,
+        [pltpu.VMEM((CLEAN, 512), BF16), pltpu.VMEM((CLEAN, WIDTH), BF16),
+         pltpu.VMEM((CLEAN, WIDTH), BF16),
          pltpu.VMEM((ROWS, WIDTH), F32), pltpu.VMEM((ROWS, WIDTH), F32),
-         pltpu.VMEM((BOTH * 8, 128), F32), pltpu.VMEM((INNER * 8, 128), F32),
-         pltpu.VMEM((INNER, WIDTH), F32), pltpu.VMEM((INNER, 128), F32),
-         pltpu.VMEM((INNER + ROWS, WIDTH), BF16), pltpu.VMEM((INNER, WIDTH), BF16),
-         pltpu.VMEM((INNER, WIDTH), F32), pltpu.VMEM((INNER * 8, 128), F32),
-         pltpu.VMEM((ROWS * 8, 128), F32), pltpu.VMEM((ROWS, WIDTH), F32),
-         pltpu.VMEM((ROWS, 128), F32), pltpu.VMEM((ROWS, 128), F32), pltpu.VMEM((ROWS, 128), F32),
-         pltpu.VMEM((32 * 8, 128), F32)],
-        48, 4 * 10**9, 10**7,
-    )(scalars, site_ids, contexts, clean, patched, cot, from_left, from_right,
+         pltpu.VMEM((INNER * 8, 128), F32), pltpu.VMEM((INNER, WIDTH), F32),
+         pltpu.VMEM((INNER, 128), F32), pltpu.VMEM((INNER, WIDTH), BF16),
+         pltpu.VMEM((INNER * 8, 128), F32), pltpu.VMEM((32 * 8, 128), F32)],
+        28, 3 * 10**9, 10**7,
+    )(scalars, contexts, clean, cot, from_left, from_right,
       w_attn_out, w_pointwise_in, depth_kernel, w_pointwise_out)
 
     cores = [(i, i ^ 1) for i in range(lax.axis_size("dp"))]
@@ -550,20 +592,38 @@
     )
     (partial,) = kernel_call(
         weight_kernel,
-        [shape((512, 3 * WIDTH), BF16)],
+        [shape((frames, 16, 3 * WIDTH), BF16)],
         [VMEM] * 6,
         [],
         32, 8 * 10**8, 10**7,
     )(own, other, grad_mixed, gm_other, grad_output, go_other)
-    groups = [
-        [(2 * y + c) * frames + f for y in range(2) for f in range(frames)] for c in range(2)
-    ]
-    pieces = lax.all_to_all(
-        partial.reshape(2 * frames, 8, 3 * WIDTH), ("dp", "frames"), 0, 0,
-        axis_index_groups=groups, tiled=True,
+    pieces = lax.all_to_all(partial, "frames", 0, 0, tiled=True)
+    (attribution,) = kernel_call(
+        patch_kernel,
+        [shape((site_ids.shape[0], ROWS), F32)],
+        [SMEM, SMEM] + [VMEM] * 15,
+        [pltpu.VMEM((PATCH, 512), BF16), pltpu.VMEM((PATCH, WIDTH), BF16),
+         pltpu.VMEM((PATCH, WIDTH), BF16), pltpu.VMEM((PATCH, WIDTH), BF16),
+         pltpu.VMEM((PATCH * 8, 128), F32), pltpu.VMEM((ROWS * 8, 128), F32),
+         pltpu.VMEM((2 * ROWS, WIDTH), BF16), pltpu.VMEM((ROWS, WIDTH), F32),
+         pltpu.VMEM((ROWS, 128), F32), pltpu.VMEM((ROWS, 128), F32), pltpu.VMEM((ROWS, 128), F32),
+         pltpu.VMEM((32 * 8, 128), F32)],
+        28, 3 * 10**9, 10**7,
+    )(scalars, site_ids, contexts, patched, from_left, from_right,
+      w_attn_out, w_pointwise_in, depth_kernel, w_pointwise_out,
+      grad_mixed, grad_output, swished, grad_swished, grad_gated, gated, resid)
+    pieces, attribution = lax.optimization_barrier((pieces, attribution))
+    summed = jnp.sum(pieces.astype(F32), axis=0)
+    upper = lax.axis_index("dp") // 2
+    mine = jnp.where(upper == 0, summed[:8], summed[8:])
+    theirs = jnp.where(upper == 0, summed[8:], summed[:8])
+    half_dp = lax.axis_size("dp") // 2
+    theirs = lax.ppermute(theirs, "dp", [(i, i ^ half_dp) for i in range(2 * half_dp)])
+    return (
+        attribution[None],
+        mine[:, : 2 * WIDTH] + theirs[:, : 2 * WIDTH],
+        mine[:, 2 * WIDTH :] + theirs[:, 2 * WIDTH :],
     )
-    summed = jnp.sum(pieces.astype(F32), axis=0)
-    return attribution[None], summed[:, : 2 * WIDTH], summed[:, 2 * WIDTH :]
 
 
 def solution(mesh):

time: 161 us -> 158 us (0.981); the launches traced: 158 us -> 157 us
  blocking collectives: 52.2 us -> 16 us
  waiting for transfers between devices: 23.8 us -> 39.9 us
  local copies, waits for them, and re-layouts: 10 us -> 20.3 us
  other arithmetic: 0.53 us -> 3.73 us
  starting transfers between devices: 22.3 us -> 25 us
  Pallas kernels: 47.7 us -> 50.3 us
    all_to_all x1, blocking collectives: 52.2 us -> 16 us  [per_device(): contexts = lax.all_to_all(context, 'frames', 0, 0, tiled=True)]
    all_to_all x1, waiting for transfers between devices: 0.01 us -> 21.8 us  [per_device(): pieces = lax.all_to_all(partial, 'frames', 0, 0, tiled=True)]
    all_to_all x1, waiting for transfers between devices: 17.4 us -> 0.28 us  [per_device(): recv = lax.all_to_all(msg, 'frames', 0, 0, tiled=True)]
    unnamed x26 -> x54, local copies, waits for them, and re-layouts: 8.78 us -> 20.3 us
    ppermute x1, waiting for transfers between devices: 1.85 us -> 11 us  [per_device(): from_left = lax.ppermute(up, 'frames', forward)]
    ppermute x0 -> x1, waiting for transfers between devices: none -> 3.84 us  [per_device(): lax.ppermute(theirs, 'dp', [(i, i ^ half_dp) for i in range(2 * half_dp)])]
    ppermute x0 -> x1, starting transfers between devices: none -> 2.36 us  [per_device(): lax.ppermute(theirs, 'dp', [(i, i ^ half_dp) for i in range(2 * half_dp)])]
    reduce_sum x1, other arithmetic: 0.46 us -> 2.38 us  [per_device(): summed = jnp.sum(pieces.astype(F32), axis=0)]
  transfers between devices with their start and end apart: 7 -> 8, of which waited for: 5 -> 7; matrix products, arithmetic and copies ran while one was open for 0% -> 0% of each run, Pallas kernels for 0% -> 8%
where the time goes in v2:
time: 158 us; the launch traced here: 157 us
  Pallas kernels  50.3 us (32%)
  waiting for transfers between devices  39.9 us (25%)
  starting transfers between devices  25 us (16%)
  local copies, waits for them, and re-layouts  20.3 us (13%)
  blocking collectives  16 us (10%)
  other arithmetic  3.73 us (2%)
    all_to_all x1, waiting for transfers between devices, per_device(): pieces = lax.all_to_all(partial, 'frames', 0, 0, tiled=True)  21.8 us
    unnamed x54, local copies, waits for them, and re-layouts  20.3 us
    pallas_call x1, Pallas kernels, per_device(): kernel_call(attend_kernel, [shape((frames, 48, 128), BF16)], [SMEM, VMEM]...  17.6 us
    all_to_all x1, blocking collectives, per_device(): contexts = lax.all_to_all(context, 'frames', 0, 0, tiled=True)  16 us
    pallas_call x1, Pallas kernels, per_device(): kernel_call(patch_kernel, [shape((site_ids.shape[0], ROWS), F32)], [SMEM,...  12.1 us
    pallas_call x1, Pallas kernels, per_device(): kernel_call(clean_kernel, [shape((ROWS, 1024), BF16), shape((ROWS, 1024),...  11.9 us
    ppermute x1, waiting for transfers between devices, per_device(): from_left = lax.ppermute(up, 'frames', forward)  11 us
    all_to_all x1, starting transfers between devices, per_device(): recv = lax.all_to_all(msg, 'frames', 0, 0, tiled=True)  9.42 us
  transfers between devices with their start and end apart: 8, of which 7 were waited for; matrix products, arithmetic and copies ran while one was open for 0% of the time, Pallas kernels for 8%

profile of v2, /device:TPU:10, one launch (start us, length us, event | category | flops | bytes accessed | tf_op | source)
XLA Modules:
  0.0 156.7 jit_solution(3757638680146042290)
XLA Ops:
  0.6 5.9 %shard_map.148 = (bf16[32,160,128]{2,1,0:T(8,128)(2,1)}, bf16[128,1024]{1,0:T(8,128)(2,1)}, bf16[64,1024]{1,0:T(8,128)(2,1)}, bf16[64,1024]{1,0:T(8,128)(2,1)}) custom-call(bf16[128,1024]{1,0:T(8,128)(2,1)} %bitcast.7, bf16[128,1024]{1,0:T(8,128)(2,1)} %bitcast.11, bf16[128,1024]{1,0:T(8,128)(2,1)} %bitcast.9, s32[1,128]{1,0:T(1,128)} %mask_ref.1, ...), custom_call_target="tpu_custom_call" | custom-call | flops 800000000 | bytes 6000000 | tf_op jit(solution)/shard_map/pallas_call | solution.py:544
  6.6 9.4 %all-to-all-start = ((bf16[32,160,128]{2,1,0:T(8,128)(2,1)}), bf16[32,160,128]{2,1,0:T(8,128)(2,1)}, u32[]{:S(2)}, u32[]{:S(2)}) async-start(bf16[32,160,128]{2,1,0:T(8,128)(2,1)} %get-tuple-element.21), calls=%async_computation | async-start | bytes 2621440 | tf_op jit(solution)/shard_map/all_to_all | solution.py:559
  16.0 3.4 %collective-permute-start = (bf16[64,1024]{1,0:T(8,128)(2,1)}, bf16[64,1024]{1,0:T(8,128)(2,1)S(1)}, u32[]{:S(2)}, u32[]{:S(2)}) collective-permute-start(bf16[64,1024]{1,0:T(8,128)(2,1)} %get-tuple-element.22), channel_id=1, source_target_pairs={{0,1},{1,2},{2,3},{3,4},{4,5},{5,6},{6,7},{7,8},{8,9},{9,10},{10,1... | collective-permute-start | bytes 393224 | tf_op jit(solution)/shard_map/ppermute | solution.py:557
  19.4 2.5 %collective-permute-start.1 = (bf16[64,1024]{1,0:T(8,128)(2,1)}, bf16[64,1024]{1,0:T(8,128)(2,1)S(1)}, u32[]{:S(2)}, u32[]{:S(2)}) collective-permute-start(bf16[64,1024]{1,0:T(8,128)(2,1)} %get-tuple-element.23), channel_id=1, source_target_pairs={{1,0},{2,1},{3,2},{4,3},{5,4},{6,5},{7,6},{8,7},{9,8},{10,9},{11,1... | collective-permute-start | bytes 393224 | tf_op jit(solution)/shard_map/ppermute | solution.py:558
  22.5 0.1 pad_add_fusion.scal_ref
  22.6 11.0 %collective-permute-done.up_ref = bf16[64,1024]{1,0:T(8,128)(2,1)S(1)} collective-permute-done((bf16[64,1024]{1,0:T(8,128)(2,1)}, bf16[64,1024]{1,0:T(8,128)(2,1)S(1)}, u32[]{:S(2)}, u32[]{:S(2)}) %collective-permute-start) | collective-permute-done | bytes 131104 | tf_op jit(solution)/shard_map/ppermute | solution.py:557
  33.6 0.9 collective-permute-done.1.down_ref
  34.5 0.3 all-to-all-done.recv_ref
  34.8 17.6 %shard_map.149 = bf16[32,48,128]{2,1,0:T(8,128)(2,1)S(1)} custom-call(s32[4]{0:T(128)S(1)} %pad_add_fusion.scal_ref, bf16[32,160,128]{2,1,0:T(8,128)(2,1)} %all-to-all-done.recv_ref), custom_call_target="tpu_custom_call" | custom-call | flops 8000000000 | bytes 1000000 | tf_op jit(solution)/shard_map/pallas_call | solution.py:562
  52.4 0.0 copy-done.21
  52.4 16.0 %all_to_all.15.ctx_in = bf16[32,48,128]{2,1,0:T(8,128)(2,1)S(1)} all-to-all(bf16[32,48,128]{2,1,0:T(8,128)(2,1)S(1)} %shard_map.149), channel_id=1, replica_groups=mesh['dp'=4,'frames'=32] {'frames'}, dimensions={0} | all-to-all | bytes 786432 | tf_op jit(solution)/shard_map/all_to_all | solution.py:572
  68.5 0.0 copy-start.3
  68.5 1.2 copy-done.3
  69.7 0.9 copy-done.16
  70.7 0.9 copy-done.19
  71.6 0.9 copy-done.22
  72.5 0.8 copy-done.24
  73.3 11.9 %shard_map.150 = (bf16[128,1024]{1,0:T(8,128)(2,1)S(1)}, bf16[128,1024]{1,0:T(8,128)(2,1)S(1)}, bf16[128,2048]{1,0:T(8,128)(2,1)S(1)}, bf16[128,1024]{1,0:T(8,12...) custom-call(s32[4]{0:T(128)S(1)} %pad_add_fusion.scal_ref, ...), custom_call_target="tpu_custom_call" | custom-call | flops 3000000000 | bytes 10000000 | tf_op jit(solution)/shard_map/pallas_call | solution.py:573
  85.3 0.9 copy-done.5
  86.1 0.8 copy-done.7
  87.0 0.9 copy-done.9
  87.8 0.8 copy-done.11
  88.6 0.7 copy-done.13
  89.4 0.5 collective-permute-start.2
  89.9 0.0 collective-permute-start.4
  89.9 1.8 %collective-permute-done.2.other_ref = bf16[128,1024]{1,0:T(8,128)(2,1)S(1)} collective-permute-done((bf16[128,1024]{1,0:T(8,128)(2,1)S(1)}, bf16[128,1024]{1,0:T(8,128)(2,1)S(1)}, u32[]{:S(2)}, u32[]{:S(2)}) %collective-permute-start.2) | collective-permute-done | bytes 262176 | tf_op jit(solution)/shard_map/ppermute | solution.py:591
  91.7 0.4 collective-permute-done.4.go_other
  92.0 0.0 collective-permute-done.3.gm_other
  92.0 2.7 %shard_map.151 = bf16[32,16,3072]{2,1,0:T(8,128)(2,1)} custom-call(bf16[128,1024]{1,0:T(8,128)(2,1)S(1)} %get-tuple-element.27.own_ref, bf16[128,1024]{1,0:T(8,128)(2,1)S(1)} %collective-permute-done.2.other_ref, bf16[128,2048]{1,0:T(8,128)(2,1)S(1)} %get-tuple-element.29.gm_ref, bf16[128,2048]{1,0:T(8,128)(2,1)S(1)} %collective-permute-done.3.gm_other, ...), custom_call_target="tpu_custom_call" | custom-call | flops 800000000 | bytes 10000000 | tf_op jit(solution)/shard_map/pallas_call | solution.py:593
  94.8 6.9 %all-to-all-start.2 = ((bf16[32,16,3072]{2,1,0:T(8,128)(2,1)}), bf16[32,16,3072]{2,1,0:T(8,128)(2,1)}, u32[]{:S(2)}, u32[]{:S(2)}) async-start(bf16[32,16,3072]{2,1,0:T(8,128)(2,1)} %shard_map.151), calls=%async_computation.2 | async-start | bytes 6291456 | tf_op jit(solution)/shard_map/all_to_all | solution.py:600
  101.7 0.0 copy-start.1
  101.7 2.2 %copy-done.1 = bf16[1024,2048]{1,0:T(8,128)(2,1)S(1)} copy-done((bf16[1024,2048]{1,0:T(8,128)(2,1)S(1)}, bf16[1024,2048]{1,0:T(8,128)(2,1)}, u32[]{:S(2)}) %copy-start.1) | copy-done | bytes 4194328
  103.9 1.2 copy-done.4
  105.1 1.1 copy-done.6
  106.2 1.1 copy-done.8
  107.3 1.0 copy-done.10
  108.3 1.0 copy-done.12
  109.3 1.0 copy-done.14
  110.3 0.9 copy-done.20
  111.2 0.9 copy-done.23
  112.1 0.8 copy-done.25
  113.0 12.1 %shard_map.152 = f32[8,128]{1,0:T(8,128)} custom-call(s32[4]{0:T(128)S(1)} %pad_add_fusion.scal_ref, s32[8]{0:T(128)S(1)} %copy-done.26, bf16[32,48,128]{2,1,0:T(8,128)(2,1)S(1)} %all_to_all.15.ctx_in, bf16[128,1024]{1,0:T(8,128)(2,1)S(1)} %copy-done.17, bf16[64,1024]{1,0:T(8,128)(2,1)S(1)} %copy-done.20, bf16[64,1024]{1,0:T(8,128)(2,1)S(1)} %copy-done.23, ...), custom_call_target="tpu_custom_call" | custom-call | flops 3000000000 | bytes 10000000 | tf_op jit(solution)/shard_map/pallas_call | solution.py:601
  125.0 21.8 %all-to-all-done.2 = bf16[32,16,3072]{2,1,0:T(8,128)(2,1)} async-done(((bf16[32,16,3072]{2,1,0:T(8,128)(2,1)}), bf16[32,16,3072]{2,1,0:T(8,128)(2,1)}, u32[]{:S(2)}, u32[]{:S(2)}) %all-to-all-start.2) | async-done | bytes 3145760 | tf_op jit(solution)/shard_map/all_to_all | solution.py:600
  146.8 2.4 %convert_reduce_fusion = f32[16,3072]{1,0:T(8,128)S(1)} fusion(bf16[32,16,3072]{2,1,0:T(8,128)(2,1)} %all-to-all-done.2), kind=kLoop, calls=%fused_computation | loop fusion | flops 3096576 | bytes 3342336 | tf_op jit(solution)/shard_map/reduce_sum | solution.py:616
  149.2 2.4 %collective-permute-start.5 = (f32[8,3072]{1,0:T(8,128)S(1)}, f32[8,3072]{1,0:T(8,128)S(1)}, u32[]{:S(2)}, u32[]{:S(2)}) collective-permute-start(f32[8,3072]{1,0:T(8,128)S(1)} %get-tuple-element.40), channel_id=1, source_target_pairs={{0,64},{32,96},{64,0},{96,32},{1,65},{33,97},{65,1},{97,33},{2,66}... | collective-permute-start | bytes 294920 | tf_op jit(solution)/shard_map/ppermute | solution.py:621
  151.6 3.8 %collective-permute-done.5 = f32[8,3072]{1,0:T(8,128)S(1)} collective-permute-done((f32[8,3072]{1,0:T(8,128)S(1)}, f32[8,3072]{1,0:T(8,128)S(1)}, u32[]{:S(2)}, u32[]{:S(2)}) %collective-permute-start.5) | collective-permute-done | bytes 98336 | tf_op jit(solution)/shard_map/ppermute | solution.py:621
  155.4 0.6 slice_add_fusion.1
  156.0 0.6 slice_add_fusion
  (33 shorter events, 0.1 us)
Async XLA Ops:
  6.6 28.2 %all-to-all-start = ((bf16[32,160,128]{2,1,0:T(8,128)(2,1)}), bf16[32,160,128]{2,1,0:T(8,128)(2,1)}, u32[]{:S(2)}, u32[]{:S(2)}) async-start(bf16[32,160,128]{2,1,0:T(8,128)(2,1)} %get-tuple-element.21), calls=%async_computation | async-start | bytes 2621440 | tf_op jit(solution)/shard_map/all_to_all | solution.py:559
  16.0 17.6 %collective-permute-start = (bf16[64,1024]{1,0:T(8,128)(2,1)}, bf16[64,1024]{1,0:T(8,128)(2,1)S(1)}, u32[]{:S(2)}, u32[]{:S(2)}) collective-permute-start(bf16[64,1024]{1,0:T(8,128)(2,1)} %get-tuple-element.22), channel_id=1, source_target_pairs={{0,1},{1,2},{2,3},{3,4},{4,5},{5,6},{6,7},{7,8},{8,9},{9,10},{10,1... | collective-permute-start | bytes 393224 | tf_op jit(solution)/shard_map/ppermute | solution.py:557
  19.4 15.1 %collective-permute-start.1 = (bf16[64,1024]{1,0:T(8,128)(2,1)}, bf16[64,1024]{1,0:T(8,128)(2,1)S(1)}, u32[]{:S(2)}, u32[]{:S(2)}) collective-permute-start(bf16[64,1024]{1,0:T(8,128)(2,1)} %get-tuple-element.23), channel_id=1, source_target_pairs={{1,0},{2,1},{3,2},{4,3},{5,4},{6,5},{7,6},{8,7},{9,8},{10,9},{11,1... | collective-permute-start | bytes 393224 | tf_op jit(solution)/shard_map/ppermute | solution.py:558
  22.6 45.9 %copy-start.2 = (bf16[1024,1024]{1,0:T(8,128)(2,1)S(1)}, bf16[1024,1024]{1,0:T(8,128)(2,1)}, u32[]{:S(2)}) copy-start(bf16[1024,1024]{1,0:T(8,128)(2,1)} %wout_ref.3) | copy-start | bytes 6291460
  22.6 45.9 %copy-start.15 = (bf16[1,128,1024]{2,1,0:T(8,128)(2,1)S(1)}, bf16[1,128,1024]{2,1,0:T(8,128)(2,1)}, u32[]{:S(2)}) copy-start(bf16[1,128,1024]{2,1,0:T(8,128)(2,1)} %param.13) | copy-start | bytes 786436
  33.6 18.8 %copy-start.18 = (bf16[64,1024]{1,0:T(8,128)(2,1)}, bf16[64,1024]{1,0:T(8,128)(2,1)S(1)}, u32[]{:S(2)}) copy-start(bf16[64,1024]{1,0:T(8,128)(2,1)S(1)} %collective-permute-done.up_ref) | copy-start | bytes 393220
  34.5 17.9 %copy-start.21 = (bf16[64,1024]{1,0:T(8,128)(2,1)}, bf16[64,1024]{1,0:T(8,128)(2,1)S(1)}, u32[]{:S(2)}) copy-start(bf16[64,1024]{1,0:T(8,128)(2,1)S(1)} %collective-permute-done.1.down_ref) | copy-start | bytes 393220
  34.8 33.7 %copy-start = (bf16[1024,2048]{1,0:T(8,128)(2,1)S(1)}, bf16[1024,2048]{1,0:T(8,128)(2,1)}, u32[]{:S(2)}) copy-start(bf16[1024,2048]{1,0:T(8,128)(2,1)} %win_ref.3) | copy-start | bytes 12582916
  68.5 1.2 copy-start.3
  69.7 0.9 copy-start.16
  70.7 0.9 copy-start.19
  71.6 0.9 copy-start.22
  72.5 0.8 copy-start.24
  85.2 0.9 copy-start.5
  86.1 0.8 copy-start.7
  87.0 0.9 copy-start.9
  87.8 0.8 copy-start.11
  88.6 0.7 copy-start.13
  89.4 2.7 %collective-permute-start.3 = (bf16[128,2048]{1,0:T(8,128)(2,1)S(1)}, bf16[128,2048]{1,0:T(8,128)(2,1)S(1)}, u32[]{:S(2)}, u32[]{:S(2)}) collective-permute-start(bf16[128,2048]{1,0:T(8,128)(2,1)S(1)} %get-tuple-element.29.gm_ref), channel_id=1, source_target_pairs={{0,32},{32,0},{64,96},{96,64},{1,33},{33,1},{65,97},{97,65},{2,34}... | collective-permute-start | bytes 1572872 | tf_op jit(solution)/shard_map/ppermute | solution.py:591
  89.4 2.3 %collective-permute-start.2 = (bf16[128,1024]{1,0:T(8,128)(2,1)S(1)}, bf16[128,1024]{1,0:T(8,128)(2,1)S(1)}, u32[]{:S(2)}, u32[]{:S(2)}) collective-permute-start(bf16[128,1024]{1,0:T(8,128)(2,1)S(1)} %get-tuple-element.28), channel_id=1, source_target_pairs={{0,32},{32,0},{64,96},{96,64},{1,33},{33,1},{65,97},{97,65},{2,34}... | collective-permute-start | bytes 786440 | tf_op jit(solution)/shard_map/ppermute | solution.py:591
  89.9 2.1 %collective-permute-start.4 = (bf16[128,1024]{1,0:T(8,128)(2,1)S(1)}, bf16[128,1024]{1,0:T(8,128)(2,1)S(1)}, u32[]{:S(2)}, u32[]{:S(2)}) collective-permute-start(bf16[128,1024]{1,0:T(8,128)(2,1)S(1)} %get-tuple-element.30.go_ref), channel_id=1, source_target_pairs={{0,32},{32,0},{64,96},{96,64},{1,33},{33,1},{65,97},{97,65},{2,34}... | collective-permute-start | bytes 786440 | tf_op jit(solution)/shard_map/ppermute | solution.py:591
  94.8 6.9 %copy-start.17 = (bf16[128,1024]{1,0:T(8,128)(2,1)S(1)}, bf16[128,1024]{1,0:T(8,128)(2,1)}, u32[]{:S(2)}) copy-start(bf16[128,1024]{1,0:T(8,128)(2,1)} %get-tuple-element.31.patched_ref) | copy-start | bytes 786436
  94.8 6.9 %copy-start.26 = (s32[8]{0:T(128)S(1)}, s32[8]{0:T(128)}, u32[]{:S(2)}) copy-start(s32[8]{0:T(128)} %site_ref.1) | copy-start | bytes 100
  94.8 52.0 %all-to-all-start.2 = ((bf16[32,16,3072]{2,1,0:T(8,128)(2,1)}), bf16[32,16,3072]{2,1,0:T(8,128)(2,1)}, u32[]{:S(2)}, u32[]{:S(2)}) async-start(bf16[32,16,3072]{2,1,0:T(8,128)(2,1)} %shard_map.151), calls=%async_computation.2 | async-start | bytes 6291456 | tf_op jit(solution)/shard_map/all_to_all | solution.py:600
  101.7 2.2 %copy-start.1 = (bf16[1024,2048]{1,0:T(8,128)(2,1)S(1)}, bf16[1024,2048]{1,0:T(8,128)(2,1)}, u32[]{:S(2)}) copy-start(bf16[1024,2048]{1,0:T(8,128)(2,1)} %win_ref.3) | copy-start | bytes 12582916
  103.9 1.2 copy-start.4
  105.1 1.1 copy-start.6
  106.2 1.1 copy-start.8
  107.3 1.0 copy-start.10
  108.3 1.0 copy-start.12
  109.3 1.0 copy-start.14
  110.3 0.9 copy-start.20
  111.2 0.9 copy-start.23
  112.1 0.8 copy-start.25
  149.2 6.2 %collective-permute-start.5 = (f32[8,3072]{1,0:T(8,128)S(1)}, f32[8,3072]{1,0:T(8,128)S(1)}, u32[]{:S(2)}, u32[]{:S(2)}) collective-permute-start(f32[8,3072]{1,0:T(8,128)S(1)} %get-tuple-element.40), channel_id=1, source_target_pairs={{0,64},{32,96},{64,0},{96,32},{1,65},{33,97},{65,1},{97,33},{2,66}... | collective-permute-start | bytes 294920 | tf_op jit(solution)/shard_map/ppermute | solution.py:621

commit v3 on v2

--- a/solution.py
+++ b/solution.py
@@ -106,7 +106,7 @@
         copy.wait()
 
     low = lane_of(ROWS) < 64
-    low_q = lane_of(32) < 64
+    low_q = lane_of(64) < 64
     for pair in range(2):
         cols = slice(pair * 256, pair * 256 + 256)
         hidden = hidden_ref[...]
@@ -119,116 +119,135 @@
                 part = slice(run * ROWS, run * ROWS + ROWS)
                 k, v, q = keys[part, tile], values[part, tile], query[part, tile]
                 base = run * 16 + (pair * 2 + sub) * 4
-                even = jnp.where(low, k, swap(v)).astype(BF16)
-                odd = jnp.where(low, swap(k), v).astype(BF16)
-                for side in range(2):
-                    msg_ref[base + side, 0:ROWS, :] = even
-                    msg_ref[base + 2 + side, 0:ROWS, :] = odd
-                    qa = q[side * 64 : side * 64 + 32]
-                    qb = q[side * 64 + 32 : side * 64 + 64]
-                    msg_ref[base + side, ROWS : ROWS + 32, :] = jnp.where(
-                        low_q, qa, swap(qb)
-                    ).astype(BF16)
-                    msg_ref[base + 2 + side, ROWS : ROWS + 32, :] = jnp.where(
-                        low_q, swap(qa), qb
-                    ).astype(BF16)
-
-
-def attend_kernel(scal_ref, recv_ref, out_ref, kt_ref, v_ref, s0_ref, s1_ref, m0_ref, m1_ref, c_ref):
-    length = scal_ref[1]
-    side = scal_ref[3]
+                kv = (jnp.where(low, k, swap(v)).astype(BF16), jnp.where(low, swap(k), v).astype(BF16))
+                early, late = q[:64], q[64:]
+                asked = (
+                    jnp.where(low_q, early, swap(late)).astype(BF16),
+                    jnp.where(low_q, swap(early), late).astype(BF16),
+                )
+                for odd in range(2):
+                    for side in range(2):
+                        dest = base + odd * 2 + side
+                        msg_ref[dest, 0:64, :] = kv[odd][side * 64 : side * 64 + 64]
+                        msg_ref[dest, 64:128, :] = asked[odd]
+
+
+def attend_kernel(
+    scal_ref, recv_ref, out_ref, k_ref, vt_ref, qt_ref, s0_ref, s1_ref, c_ref, r_ref
+):
+    length, side = scal_ref[1], scal_ref[3]
     sources = recv_ref.shape[0]
-    count = sources * ROWS
-    lane = lane_of(ROWS)
+    lane = lane_of(128)
+    row = lax.broadcasted_iota(jnp.int32, (128, 128), 0)
+    scale = DH ** (-0.5) * LOG2E
 
     def load(s, carry):
-        kv = recv_ref[s, 0:ROWS, :].astype(F32)
-        frame = s * ROWS + lax.broadcasted_iota(jnp.int32, (ROWS, 128), 0)
+        at = pl.multiple_of(s * 128, 128)
+        kv = recv_ref[pl.ds(2 * s, 2), 0:64, :].astype(F32).reshape(128, 128)
+        frame = (2 * s + row // 64) * ROWS + side * 64 + row % 64
         bias = jnp.where(frame < length, 0.0, FLOOR)
         keyed = jnp.where(lane < 64, kv, jnp.where(lane == 64, bias, 0.0))
-        at = pl.ds(pl.multiple_of(s * ROWS, ROWS), ROWS)
-        kt_ref[:, at] = keyed.T.astype(BF16)
-        v_ref[at, :] = jnp.where(lane < 64, 1.0, kv).astype(BF16)
-        return carry
-
-    lax.fori_loop(0, sources, load, 0)
-
-    chunk = 512
-    pieces = count // chunk
-    blocks = sources // 4
-    scale = DH ** (-0.5) * LOG2E
+        k_ref[pl.ds(at, 128), :] = keyed.astype(BF16)
+        vt_ref[:, pl.ds(at, 128)] = jnp.where(lane < 64, 1.0, kv).T.astype(BF16)
+        raw = recv_ref[pl.ds(2 * s, 2), 64:128, :].astype(F32).reshape(128, 128).T
+        fill = jnp.where(row == 64, 1.0, 0.0)
+        other = jnp.concatenate([raw[64:], raw[:64]], axis=0)
+        at = pl.multiple_of(s * 256, 256)
+        qt_ref[:, pl.ds(at, 128)] = jnp.where(row < 64, raw, fill).astype(BF16)
+        qt_ref[:, pl.ds(at + 128, 128)] = jnp.where(row < 64, other, fill).astype(BF16)
+        return carry
+
+    lax.fori_loop(0, sources // 2, load, 0, unroll=4)
+
+    many = s0_ref.shape[1]
+    chunk = 256
+    pieces = k_ref.shape[0] // chunk
+    blocks = sources * ROWS // many
+
+    def score_piece(query, s_ref, k, top):
+        at = slice(k * chunk, k * chunk + chunk)
+        scores = dot(k_ref[at, :], query)
+        s_ref[at, :] = scores
+        best = jnp.max(scores.reshape(chunk // 8, 8, many), axis=0)
+        return best if top is None else jnp.maximum(top, best)
+
+    def weigh_piece(s_ref, best, k, accum):
+        at = slice(k * chunk, k * chunk + chunk)
+        weights = jnp.exp2((s_ref[at, :] - best) * scale).astype(BF16)
+        addend = dot(vt_ref[:, at], weights)
+        return addend if accum is None else accum + addend
+
+    def finish(top):
+        return jnp.max(top, axis=0, keepdims=True)
 
     def queries(b):
-        raw = recv_ref[pl.ds(b * 4, 4), ROWS : ROWS + 32, :].astype(F32).reshape(128, 128)
-        fill = jnp.where(lane == 64, 1.0, 0.0)
-        return jnp.concatenate(
-            [jnp.where(lane < 64, raw, fill), jnp.where(lane < 64, swap(raw), fill)], axis=0
-        ).astype(BF16)
-
-    def score_piece(query, s_ref, k, top):
-        scores = dot(query, kt_ref[:, k * chunk : (k + 1) * chunk])
-        s_ref[:, k * chunk : (k + 1) * chunk] = scores
-        for j in range(chunk // 128):
-            tile = scores[:, j * 128 : (j + 1) * 128]
-            top = tile if top is None else jnp.maximum(top, tile)
-        return top
-
-    def finish_top(m_ref, top):
-        m_ref[...] = jnp.broadcast_to(jnp.max(top, axis=1, keepdims=True), (256, 128))
-
-    def weigh_piece(s_ref, top, k, accum):
-        scores = s_ref[:, k * chunk : (k + 1) * chunk]
-        weights = jnp.exp2((scores - top) * scale).astype(BF16)
-        addend = dot(weights, v_ref[k * chunk : (k + 1) * chunk, :])
-        return addend if accum is None else accum + addend
-
-    def store(b, accum):
-        first, second = accum[:128], accum[128:]
-        result = jnp.where(lane < 64, swap(first) / first, second / swap(second))
-        c_ref[pl.ds(b * 128, 128), :] = result
-
-    def step(b, s_ref, m_ref, next_b, next_s, next_m):
+        return qt_ref[:, pl.ds(pl.multiple_of(b * many, many), many)]
+
+    low8 = lane_of(8) < 64
+
+    def store(b, accum, best):
+        total = accum[0:1, :]
+        result = accum[64:128, :] / total
+        level = jnp.broadcast_to(best * scale + jnp.log2(total), (8, many))
+        for g in range(many // 256):
+            first = slice(g * 256, g * 256 + 128)
+            second = slice(g * 256 + 128, g * 256 + 256)
+            both = jnp.concatenate([result[:, first], result[:, second]], axis=0)
+            at = b * (many // 256) + g
+            c_ref[pl.ds(pl.multiple_of(at * 128, 128), 128), :] = both.T
+            early, late = level[:, first], level[:, second]
+            r_ref[pl.ds(pl.multiple_of(at * 16, 16), 8), :] = jnp.where(low8, early, swap(late))
+            r_ref[pl.ds(pl.multiple_of(at * 16 + 8, 8), 8), :] = jnp.where(low8, swap(early), late)
+
+    def step(b, s_ref, best, next_b, next_s):
         query = None if next_s is None else queries(next_b)
         top, accum = None, None
-        best = jnp.tile(m_ref[...], (1, chunk // 128))
         for k in range(pieces):
             if query is not None:
                 top = score_piece(query, next_s, k, top)
             accum = weigh_piece(s_ref, best, k, accum)
-        if query is not None:
-            finish_top(next_m, top)
-        store(b, accum)
+        store(b, accum, best)
+        return None if query is None else finish(top)
 
     query, top = queries(0), None
     for k in range(pieces):
         top = score_piece(query, s0_ref, k, top)
-    finish_top(m0_ref, top)
-
-    def pair(i, carry):
-        step(2 * i, s0_ref, m0_ref, 2 * i + 1, s1_ref, m1_ref)
-        step(2 * i + 1, s1_ref, m1_ref, 2 * i + 2, s0_ref, m0_ref)
-        return carry
-
-    lax.fori_loop(0, blocks // 2 - 1, pair, 0)
-    step(blocks - 2, s0_ref, m0_ref, blocks - 1, s1_ref, m1_ref)
-    step(blocks - 1, s1_ref, m1_ref, None, None, None)
-
-    low = lane_of(16) < 64
+
+    def pair(i, best):
+        best = step(2 * i, s0_ref, best, 2 * i + 1, s1_ref)
+        return step(2 * i + 1, s1_ref, best, 2 * i + 2, s0_ref)
+
+    best = lax.fori_loop(0, blocks // 2 - 1, pair, finish(top))
+    best = step(blocks - 2, s0_ref, best, blocks - 1, s1_ref)
+    step(blocks - 1, s1_ref, best, None, None)
+
+    low32 = lane_of(32) < 64
+    row8 = lax.broadcasted_iota(jnp.int32, (8, 128), 0)
 
     def pack(d, carry):
-        own = c_ref[pl.ds(pl.multiple_of(d * 32, 32), 32), :]
         after = lax.rem(d + 1, sources)
         before = lax.rem(d + sources - 1, sources)
-        other = jnp.where(side == 0, after, before)
-        rim = c_ref[pl.ds(pl.multiple_of(other * 32, 32), 32), :]
-        first, second = rim[:16], rim[16:]
-        rim_a = jnp.where(low, first, swap(second))
-        rim_b = jnp.where(low, swap(first), second)
-        out_ref[d, 0:32, :] = own.astype(BF16)
-        out_ref[d, 32:48, :] = jnp.where(side == 0, rim_a, rim_b).astype(BF16)
-        return carry
-
-    lax.fori_loop(0, sources, pack, 0)
+        out_ref[d, 0:64, :] = c_ref[pl.ds(pl.multiple_of(d * 64, 64), 64), :].astype(BF16)
+        right = c_ref[pl.ds(pl.multiple_of(after * 64, 64), 32), :]
+        left = c_ref[pl.ds(pl.multiple_of(before * 64 + 32, 32), 32), :]
+        out_ref[d, 64:96, :] = jnp.where(low32, right, left).astype(BF16)
+        own = r_ref[pl.ds(pl.multiple_of(d * 8, 8), 8), :]
+        rim = jnp.where(
+            low8,
+            r_ref[pl.ds(pl.multiple_of(after * 8, 8), 8), :],
+            r_ref[pl.ds(pl.multiple_of(before * 8, 8), 8), :],
+        )
+        rows = jnp.where(row8 < 3, own, rim)
+        high = rows.astype(BF16).astype(F32)
+        rest = rows - high
+        middle = rest.astype(BF16).astype(F32)
+        last = rest - middle
+        level = row8 % 3
+        rows = jnp.where(level == 0, high, jnp.where(level == 1, middle, last))
+        out_ref[d, 96:112, :] = jnp.concatenate([rows, rows], axis=0).astype(BF16)
+        return carry
+
+    lax.fori_loop(0, sources, pack, 0, unroll=2)
 
 
 def depthwise(source, source_row, taps_ref, order, target, count):
@@ -262,25 +281,47 @@
     return jnp.concatenate(groups, axis=0) if len(groups) > 1 else groups[0]
 
 
-def place_context(ctx_in, ctx_ref, run, trimmed):
-    low = lane_of(48) < 64
+def place_context(ctx_in, base, ctx_ref, rim):
+    row8 = lax.broadcasted_iota(jnp.int32, (8, 128), 0)
+    zero = jnp.zeros((8, 128), F32)
+    levels = [[zero, zero], [zero, zero]]
+    for h in range(HEADS):
+        for side in range(2):
+            block = ctx_in[base + h * 2 + side, 96:112, :].astype(F32)
+            for kind in range(2):
+                at = kind * 3
+                level = block[at : at + 1] + block[at + 1 : at + 2] + block[at + 2 : at + 3]
+                levels[kind][side] = jnp.where(row8 == h, level, levels[kind][side])
+    shares = []
+    for first, second in levels:
+        shares.append(1.0 / (1.0 + jnp.exp2(second - first)))
+        shares.append(1.0 / (1.0 + jnp.exp2(first - second)))
+    share = jnp.concatenate(shares + [jnp.zeros((96, 128), F32)], axis=0).T
+    low = lane_of(96) < 64
+    low_rows = lane_of(ROWS) < 64
     for t in range(HEADS // 2):
         at = slice(t * 128, t * 128 + 128)
-        base = run * 16 + t * 4
-        halves = []
+        own = left = right = None
         for side in range(2):
-            even = ctx_in[base + side].astype(F32)
-            odd = ctx_in[base + 2 + side].astype(F32)
-            halves.append((
-                jnp.where(low, even, swap(odd)).astype(BF16),
-                jnp.where(low, swap(even), odd).astype(BF16),
-            ))
-        (lo0, hi0), (lo1, hi1) = halves
-        parts = [lo1[32:48], hi1[32:48], lo0[:32], hi0[:32], lo1[:32], hi1[:32], lo0[32:48], hi0[32:48]]
-        row = 0
-        for part in parts[1:-1] if trimmed else parts:
-            ctx_ref[row : row + part.shape[0], at] = part
-            row += part.shape[0]
+            even = ctx_in[base + t * 4 + side, 0:96, :].astype(F32)
+            odd = ctx_in[base + t * 4 + 2 + side, 0:96, :].astype(F32)
+            first = jnp.where(low, even, swap(odd))
+            second = jnp.where(low, swap(even), odd)
+            scale = []
+            for kind in range(2):
+                column = kind * 16 + side * 8 + 2 * t
+                scale.append(jnp.where(
+                    low_rows, share[:, column : column + 1], share[:, column + 1 : column + 2]
+                ))
+            part = jnp.concatenate([first[:64], second[:64]], axis=0) * scale[0]
+            after = first[64:96] * scale[1][0:32]
+            before = second[64:96] * scale[1][96:128]
+            own = part if own is None else own + part
+            left = before if left is None else left + before
+            right = after if right is None else right + after
+        ctx_ref[0:rim, at] = left[RIM - rim :].astype(BF16)
+        ctx_ref[rim : rim + ROWS, at] = own.astype(BF16)
+        ctx_ref[rim + ROWS :, at] = right[:rim].astype(BF16)
 
 
 def place_taps(depth_ref, taps_ref):
@@ -325,32 +366,61 @@
 
 
 def clean_kernel(
-    scal_ref, ctx_in, clean_ref, cot_ref, up_ref, down_ref,
-    wao_ref, win_ref, depth_ref, wout_ref,
+    scal_ref, ctx_hbm, clean_hbm, cot_hbm, up_hbm, down_hbm,
+    wao_hbm, win_hbm, depth_hbm, wout_hbm,
+    own_out, send_out, gm_out, go_out, sw_out, gs_out, gg2_out, g2_out, resid_out,
+    ctx_in, wao_ref, win_ref, depth_ref, wout_ref,
     own_ref, send_ref, gm_ref, go_ref, sw_ref, gs_ref, gg2_ref, g2_ref, resid_ref,
     ctx_ref, x_ref, low_ref, mv_ref, sg_ref, s2_ref, zed_ref, zinv_ref, gox_ref, gsp2_ref, taps_ref,
+    in_sems, out_sems,
 ):
     first_frame, length, core = scal_ref[0], scal_ref[1], scal_ref[2]
     half = RIM // 2
-    place_context(ctx_in, ctx_ref, 0, False)
-    x_ref[0:RIM, :] = up_ref[0:RIM, :]
-    x_ref[RIM : RIM + ROWS, :] = clean_ref[...]
-    x_ref[RIM + ROWS : CLEAN, :] = down_ref[0:RIM, :]
+    copies = [
+        pltpu.make_async_copy(source, target, in_sems.at[i])
+        for i, (source, target) in enumerate((
+            (ctx_hbm.at[pl.ds(0, 16)], ctx_in),
+            (up_hbm.at[pl.ds(0, RIM)], x_ref.at[pl.ds(0, RIM)]),
+            (clean_hbm, x_ref.at[pl.ds(RIM, ROWS)]),
+            (down_hbm.at[pl.ds(0, RIM)], x_ref.at[pl.ds(RIM + ROWS, RIM)]),
+            (wao_hbm, wao_ref),
+            (depth_hbm, depth_ref),
+            (up_hbm.at[pl.ds(RIM + half, half)], gox_ref.at[pl.ds(0, half)]),
+            (cot_hbm, gox_ref.at[pl.ds(half, ROWS)]),
+            (down_hbm.at[pl.ds(RIM + half, half)], gox_ref.at[pl.ds(half + ROWS, half)]),
+            (win_hbm, win_ref),
+            (wout_hbm, wout_ref),
+        ))
+    ]
+    for copy in copies:
+        copy.start()
+    results = [
+        pltpu.make_async_copy(source, target, out_sems.at[i])
+        for i, (source, target) in enumerate((
+            (own_ref, own_out), (send_ref, send_out), (gm_ref, gm_out), (go_ref, go_out),
+            (sw_ref, sw_out), (gs_ref, gs_out), (gg2_ref, gg2_out), (g2_ref, g2_out),
+            (resid_ref, resid_out),
+        ))
+    ]
+    own_copy, send_copy, gm_copy, go_copy, sw_copy, gs_copy, gg2_copy, g2_copy, resid_copy = results
+    copies[0].wait()
+    place_context(ctx_in, 0, ctx_ref, RIM)
+    for copy in copies[1:9]:
+        copy.wait()
     place_taps(depth_ref, taps_ref)
-    for piece, row, offset in (
-        (up_ref[RIM + half :, :], 0, -half),
-        (cot_ref[...], half, 0),
-        (down_ref[RIM + half :, :], half + ROWS, ROWS),
-    ):
-        n = piece.shape[0]
-        frame = first_frame + offset + lax.broadcasted_iota(jnp.int32, (n, 1), 0)
-        keep = jnp.where(frame < length, 1.0, 0.0)
-        gox_ref[row : row + n, :] = (piece.astype(F32) * keep).astype(BF16)
+    for row in range(0, INNER, 16):
+        at = slice(row, row + 16)
+        frame = first_frame - half + row + lax.broadcasted_iota(jnp.int32, (16, 1), 0)
+        gox_ref[at, :] = (gox_ref[at, :].astype(F32) * jnp.where(frame < length, 1.0, 0.0)).astype(BF16)
     go_ref[...] = gox_ref[half : half + ROWS, :]
+    go_copy.start()
 
     to_lowered(x_ref, ctx_ref, wao_ref, resid_ref, low_ref)
+    resid_copy.start()
     frame = first_frame - RIM + lax.broadcasted_iota(jnp.int32, (CLEAN, 1), 0)
+    copies[9].wait()
     to_gated(low_ref, win_ref, g2_ref, frame, length, (mv_ref, sg_ref))
+    g2_copy.start()
     forward = list(range(KERNEL))
     edge = half - KERNEL // 2
     depthwise(g2_ref, edge, taps_ref, forward, s2_ref, INNER)
@@ -365,10 +435,24 @@
         return carry
 
     lax.fori_loop(0, INNER // 16, clean_rows, 0)
-
+    sw_copy.start()
+
+    for part in range(4):
+        dest = part * 256
+        source, row = (low_ref, RIM) if part < 2 else (sw_ref, half)
+        lo = (part % 2) * 512
+        first = source[row : row + ROWS, lo : lo + 256].astype(F32)
+        second = source[row : row + ROWS, lo + 256 : lo + 512].astype(F32)
+        own_ref[:, dest : dest + 256] = jnp.where(core == 0, first, second).astype(BF16)
+        send_ref[:, dest : dest + 256] = jnp.where(core == 0, second, first).astype(BF16)
+    own_copy.start()
+    send_copy.start()
+
+    copies[10].wait()
     for j in range(4):
         at = slice(j * 256, j * 256 + 256)
         gs_ref[:, at] = dot_nt(gox_ref[...], wout_ref[at, :])
+    gs_copy.start()
 
     def back_rows(i, carry):
         r = pl.multiple_of(i * 16, 16)
@@ -388,6 +472,7 @@
 
     lax.fori_loop(0, INNER // 16, back_rows, 0)
     depthwise(gsp2_ref, edge, taps_ref, forward[::-1], gg2_ref, ROWS)
+    gg2_copy.start()
 
     def mixed_rows(i, carry):
         r = pl.multiple_of(i * 16, 16)
@@ -401,14 +486,9 @@
 
     lax.fori_loop(0, ROWS // 16, mixed_rows, 0)
 
-    for part in range(4):
-        dest = part * 256
-        source, row = (low_ref, RIM) if part < 2 else (sw_ref, half)
-        lo = (part % 2) * 512
-        first = source[row : row + ROWS, lo : lo + 256].astype(F32)
-        second = source[row : row + ROWS, lo + 256 : lo + 512].astype(F32)
-        own_ref[:, dest : dest + 256] = jnp.where(core == 0, first, second).astype(BF16)
-        send_ref[:, dest : dest + 256] = jnp.where(core == 0, second, first).astype(BF16)
+    gm_copy.start()
+    for copy in results:
+        copy.wait()
 
 
 def patch_kernel(
@@ -420,7 +500,7 @@
 ):
     first_frame, length = scal_ref[0], scal_ref[1]
     half = RIM // 2
-    place_context(ctx_in, ctx_ref, 1, True)
+    place_context(ctx_in, 16, ctx_ref, half)
     x_ref[0:half, :] = up_ref[RIM : RIM + half, :]
     x_ref[half : half + ROWS, :] = patched_ref[...]
     x_ref[half + ROWS : PATCH, :] = down_ref[RIM : RIM + half, :]
@@ -513,12 +593,12 @@
 HBM = pl.BlockSpec(memory_space=pltpu.HBM)
 
 
-def kernel_call(body, out_shape, in_specs, scratch, limit, flops, moved):
+def kernel_call(body, out_shape, in_specs, scratch, limit, flops, moved, out_spec=VMEM):
     return pl.pallas_call(
         body,
         out_shape=out_shape,
         in_specs=in_specs,
-        out_specs=[VMEM] * len(out_shape),
+        out_specs=[out_spec] * len(out_shape),
         scratch_shapes=scratch,
         compiler_params=pltpu.CompilerParams(vmem_limit_bytes=limit << 20),
         cost_estimate=pl.CostEstimate(flops=flops, bytes_accessed=moved, transcendentals=0),
@@ -543,7 +623,7 @@
 
     msg, patched, up, down = kernel_call(
         project_kernel,
-        [shape((frames, ROWS + 32, 128), BF16), shape((ROWS, WIDTH), BF16),
+        [shape((frames, ROWS, 128), BF16), shape((ROWS, WIDTH), BF16),
          shape((2 * RIM, WIDTH), BF16), shape((2 * RIM, WIDTH), BF16)],
         [HBM] * 3 + [VMEM] + [HBM] * 3,
         [pltpu.VMEM((2 * ROWS, WIDTH), BF16), pltpu.VMEM((ROWS, ROWS), F32),
@@ -558,15 +638,15 @@
     from_right = lax.ppermute(down, "frames", backward)
     recv = lax.all_to_all(msg, "frames", 0, 0, tiled=True)
     recv, from_left, from_right = lax.optimization_barrier((recv, from_left, from_right))
-    count = frames * ROWS
+    keys = frames * ROWS // 2
     (context,) = kernel_call(
         attend_kernel,
-        [shape((frames, 48, 128), BF16)],
+        [shape((frames, 112, 128), BF16)],
         [SMEM, VMEM],
-        [pltpu.VMEM((128, count), BF16), pltpu.VMEM((count, 128), BF16),
-         pltpu.VMEM((256, count), F32), pltpu.VMEM((256, count), F32),
-         pltpu.VMEM((256, 128), F32), pltpu.VMEM((256, 128), F32),
-         pltpu.VMEM((frames * 32, 128), F32)],
+        [pltpu.VMEM((keys, 128), BF16), pltpu.VMEM((128, keys), BF16),
+         pltpu.VMEM((128, 2 * keys), BF16),
+         pltpu.VMEM((keys, 512), F32), pltpu.VMEM((keys, 512), F32),
+         pltpu.VMEM((frames * 64, 128), F32), pltpu.VMEM((frames * 8, 128), F32)],
         20, 8 * 10**9, 10**6,
     )(scalars, recv)
     contexts = lax.all_to_all(context, "frames", 0, 0, tiled=True)
@@ -575,14 +655,23 @@
         [shape((ROWS, 1024), BF16), shape((ROWS, 1024), BF16), shape((ROWS, 2 * WIDTH), BF16),
          shape((ROWS, WIDTH), BF16), shape((INNER, WIDTH), BF16), shape((INNER, WIDTH), F32),
          shape((ROWS * 8, 128), F32), shape((CLEAN * 8, 128), F32), shape((CLEAN, WIDTH), BF16)],
-        [SMEM] + [VMEM] * 9,
-        [pltpu.VMEM((CLEAN, 512), BF16), pltpu.VMEM((CLEAN, WIDTH), BF16),
+        [SMEM] + [HBM] * 9,
+        [pltpu.VMEM((16, 112, 128), BF16), pltpu.VMEM((512, WIDTH), BF16),
+         pltpu.VMEM((WIDTH, 2 * WIDTH), BF16), pltpu.VMEM((KERNEL, WIDTH), BF16),
+         pltpu.VMEM((WIDTH, WIDTH), BF16),
+         pltpu.VMEM((ROWS, 1024), BF16), pltpu.VMEM((ROWS, 1024), BF16),
+         pltpu.VMEM((ROWS, 2 * WIDTH), BF16), pltpu.VMEM((ROWS, WIDTH), BF16),
+         pltpu.VMEM((INNER, WIDTH), BF16), pltpu.VMEM((INNER, WIDTH), F32),
+         pltpu.VMEM((ROWS * 8, 128), F32), pltpu.VMEM((CLEAN * 8, 128), F32),
+         pltpu.VMEM((CLEAN, WIDTH), BF16),
+         pltpu.VMEM((CLEAN, 512), BF16), pltpu.VMEM((CLEAN, WIDTH), BF16),
          pltpu.VMEM((CLEAN, WIDTH), BF16),
          pltpu.VMEM((ROWS, WIDTH), F32), pltpu.VMEM((ROWS, WIDTH), F32),
          pltpu.VMEM((INNER * 8, 128), F32), pltpu.VMEM((INNER, WIDTH), F32),
          pltpu.VMEM((INNER, 128), F32), pltpu.VMEM((INNER, WIDTH), BF16),
-         pltpu.VMEM((INNER * 8, 128), F32), pltpu.VMEM((32 * 8, 128), F32)],
-        28, 3 * 10**9, 10**7,
+         pltpu.VMEM((INNER * 8, 128), F32), pltpu.VMEM((32 * 8, 128), F32),
+         pltpu.SemaphoreType.DMA((11,)), pltpu.SemaphoreType.DMA((9,))],
+        62, 3 * 10**9, 10**7, HBM,
     )(scalars, contexts, clean, cot, from_left, from_right,
       w_attn_out, w_pointwise_in, depth_kernel, w_pointwise_out)
 
@@ -618,7 +707,9 @@
     mine = jnp.where(upper == 0, summed[:8], summed[8:])
     theirs = jnp.where(upper == 0, summed[8:], summed[:8])
     half_dp = lax.axis_size("dp") // 2
-    theirs = lax.ppermute(theirs, "dp", [(i, i ^ half_dp) for i in range(2 * half_dp)])
+    theirs = lax.ppermute(
+        theirs.astype(BF16), "dp", [(i, i ^ half_dp) for i in range(2 * half_dp)]
+    ).astype(F32)
     return (
         attribution[None],
         mine[:, : 2 * WIDTH] + theirs[:, : 2 * WIDTH],

time: 158 us -> 147 us (0.930)
  waiting for transfers between devices: 39.9 us -> 32.8 us
  blocking collectives: 16 us -> 20.6 us
  local copies, waits for them, and re-layouts: 20.3 us -> 16.2 us
  Pallas kernels: 50.3 us -> 46.7 us
    pallas_call x2, Pallas kernels: 23.6 us -> 16.6 us  [the longest x1 10.8 us: per_device(): kernel_call(attend_kernel, [shape((frames, 112, 128), BF16)], [SMEM, VMEM...]
    all_to_all x1, blocking collectives: 16 us -> 20.6 us  [per_device(): contexts = lax.all_to_all(context, 'frames', 0, 0, tiled=True)]
    unnamed x54 -> x46, local copies, waits for them, and re-layouts: 20.3 us -> 16.2 us
    all_to_all x1, waiting for transfers between devices: 21.8 us -> 17.9 us  [per_device(): pieces = lax.all_to_all(partial, 'frames', 0, 0, tiled=True)]
    pallas_call x1, Pallas kernels: 11.9 us -> 14.8 us  [per_device(): kernel_call(clean_kernel, [shape((ROWS, 1024), BF16), shape((ROWS, 1024),...]
    ppermute x1, waiting for transfers between devices: 11 us -> 8.23 us  [per_device(): from_left = lax.ppermute(up, 'frames', forward)]
  transfers between devices with their start and end apart: 8 -> 8, of which waited for: 7 -> 7; matrix products, arithmetic and copies ran while one was open for 0% -> 0% of each run, Pallas kernels for 8% -> 9%
where the time goes in v3:
time: 147 us
  Pallas kernels  46.7 us (32%)
  waiting for transfers between devices  32.8 us (22%)
  starting transfers between devices  25.1 us (17%)
  blocking collectives  20.6 us (14%)
  local copies, waits for them, and re-layouts  16.2 us (11%)
  other arithmetic  3.75 us (3%)
  between operations  1.49 us (1%)
    all_to_all x1, blocking collectives, per_device(): contexts = lax.all_to_all(context, 'frames', 0, 0, tiled=True)  20.6 us
    all_to_all x1, waiting for transfers between devices, per_device(): pieces = lax.all_to_all(partial, 'frames', 0, 0, tiled=True)  17.9 us
    unnamed x46, local copies, waits for them, and re-layouts  16.2 us
    pallas_call x1, Pallas kernels, per_device(): kernel_call(clean_kernel, [shape((ROWS, 1024), BF16), shape((ROWS, 1024),...  14.8 us
    pallas_call x1, Pallas kernels, per_device(): kernel_call(patch_kernel, [shape((site_ids.shape[0], ROWS), F32)], [SMEM,...  12.6 us
    pallas_call x1, Pallas kernels, per_device(): kernel_call(attend_kernel, [shape((frames, 112, 128), BF16)], [SMEM, VMEM...  10.8 us
    all_to_all x1, starting transfers between devices, per_device(): recv = lax.all_to_all(msg, 'frames', 0, 0, tiled=True)  9.37 us
    ppermute x1, waiting for transfers between devices, per_device(): from_left = lax.ppermute(up, 'frames', forward)  8.23 us
  transfers between devices with their start and end apart: 8, of which 7 were waited for; matrix products, arithmetic and copies ran while one was open for 0% of the time, Pallas kernels for 9%

profile of v3, /device:TPU:10, one launch (start us, length us, event | category | flops | bytes accessed | tf_op | source)
XLA Modules:
  0.0 146.5 jit_solution(9455006290879644925)
XLA Ops:
  0.6 5.8 %shard_map.148 = (bf16[32,128,128]{2,1,0:T(8,128)(2,1)}, bf16[128,1024]{1,0:T(8,128)(2,1)}, bf16[64,1024]{1,0:T(8,128)(2,1)}, bf16[64,1024]{1,0:T(8,128)(2,1)}) custom-call(bf16[128,1024]{1,0:T(8,128)(2,1)} %bitcast.8, bf16[128,1024]{1,0:T(8,128)(2,1)} %bitcast.7, bf16[128,1024]{1,0:T(8,128)(2,1)} %bitcast.10, s32[1,128]{1,0:T(1,128)} %mask_ref.1, ...), custom_call_target="tpu_custom_call" | custom-call | flops 800000000 | bytes 6000000 | tf_op jit(solution)/shard_map/pallas_call | solution.py:624
  6.5 9.4 %all-to-all-start = ((bf16[32,128,128]{2,1,0:T(8,128)(2,1)}), bf16[32,128,128]{2,1,0:T(8,128)(2,1)S(1)}, u32[]{:S(2)}, u32[]{:S(2)}) async-start(bf16[32,128,128]{2,1,0:T(8,128)(2,1)} %get-tuple-element.21), calls=%async_computation | async-start | bytes 2097152 | tf_op jit(solution)/shard_map/all_to_all | solution.py:639
  15.8 3.4 %collective-permute-start = (bf16[64,1024]{1,0:T(8,128)(2,1)}, bf16[64,1024]{1,0:T(8,128)(2,1)S(1)}, u32[]{:S(2)}, u32[]{:S(2)}) collective-permute-start(bf16[64,1024]{1,0:T(8,128)(2,1)} %get-tuple-element.22), channel_id=1, source_target_pairs={{0,1},{1,2},{2,3},{3,4},{4,5},{5,6},{6,7},{7,8},{8,9},{9,10},{10,1... | collective-permute-start | bytes 393224 | tf_op jit(solution)/shard_map/ppermute | solution.py:637
  19.2 2.5 %collective-permute-start.1 = (bf16[64,1024]{1,0:T(8,128)(2,1)}, bf16[64,1024]{1,0:T(8,128)(2,1)S(1)}, u32[]{:S(2)}, u32[]{:S(2)}) collective-permute-start(bf16[64,1024]{1,0:T(8,128)(2,1)} %get-tuple-element.23), channel_id=1, source_target_pairs={{1,0},{2,1},{3,2},{4,3},{5,4},{6,5},{7,6},{8,7},{9,8},{10,9},{11,1... | collective-permute-start | bytes 393224 | tf_op jit(solution)/shard_map/ppermute | solution.py:638
  22.4 0.1 pad_add_fusion.scal_ref
  22.4 8.2 %collective-permute-done.up_hbm.up_ref = bf16[64,1024]{1,0:T(8,128)(2,1)S(1)} collective-permute-done((bf16[64,1024]{1,0:T(8,128)(2,1)}, bf16[64,1024]{1,0:T(8,128)(2,1)S(1)}, u32[]{:S(2)}, u32[]{:S(2)}) %collective-permute-start) | collective-permute-done | bytes 131104 | tf_op jit(solution)/shard_map/ppermute | solution.py:637
  30.7 0.9 collective-permute-done.1.down_hbm.down_ref
  31.6 0.1 all-to-all-done.recv_ref
  31.7 10.8 %shard_map.149 = bf16[32,112,128]{2,1,0:T(8,128)(2,1)S(1)} custom-call(s32[4]{0:T(128)S(1)} %pad_add_fusion.scal_ref, bf16[32,128,128]{2,1,0:T(8,128)(2,1)S(1)} %all-to-all-done.recv_ref), custom_call_target="tpu_custom_call" | custom-call | flops 8000000000 | bytes 1000000 | tf_op jit(solution)/shard_map/pallas_call | solution.py:642
  42.5 0.0 copy-done.20
  42.5 0.0 copy-done.15
  42.5 0.0 copy-done.17
  42.5 20.6 %all_to_all.15.ctx_hbm.ctx_in = bf16[32,112,128]{2,1,0:T(8,128)(2,1)} all-to-all(bf16[32,112,128]{2,1,0:T(8,128)(2,1)S(1)} %shard_map.149), channel_id=1, replica_groups=mesh['dp'=4,'frames'=32] {'frames'}, dimensions={0} | all-to-all | bytes 1835008 | tf_op jit(solution)/shard_map/all_to_all | solution.py:652
  63.1 14.8 %shard_map.150 = (bf16[128,1024]{1,0:T(8,128)(2,1)}, bf16[128,1024]{1,0:T(8,128)(2,1)}, bf16[128,2048]{1,0:T(8,128)(2,1)}, bf16[128,1024]{1,0:T(8,128)(2,1)}, bf...) custom-call(s32[4]{0:T(128)} %copy-done.20, ...), custom_call_target="tpu_custom_call" | custom-call | flops 3000000000 | bytes 10000000 | tf_op jit(solution)/shard_map/pallas_call | solution.py:653
  77.9 0.1 collective-permute-start.3
  78.0 0.5 collective-permute-start.2
  78.5 0.1 collective-permute-start.4
  78.6 1.9 %collective-permute-done.2.other_ref = bf16[128,1024]{1,0:T(8,128)(2,1)S(1)} collective-permute-done((bf16[128,1024]{1,0:T(8,128)(2,1)}, bf16[128,1024]{1,0:T(8,128)(2,1)S(1)}, u32[]{:S(2)}, u32[]{:S(2)}) %collective-permute-start.2) | collective-permute-done | bytes 262176 | tf_op jit(solution)/shard_map/ppermute | solution.py:680
  80.5 0.4 collective-permute-done.4.go_other
  80.8 0.0 collective-permute-done.3.gm_other
  80.9 1.0 copy-done.2
  81.9 0.9 copy-done.6
  82.8 0.9 copy-done.14
  83.8 2.7 %shard_map.151 = bf16[32,16,3072]{2,1,0:T(8,128)(2,1)} custom-call(bf16[128,1024]{1,0:T(8,128)(2,1)S(1)} %copy-done.14, bf16[128,1024]{1,0:T(8,128)(2,1)S(1)} %collective-permute-done.2.other_ref, bf16[128,2048]{1,0:T(8,128)(2,1)S(1)} %copy-done.2, bf16[128,2048]{1,0:T(8,128)(2,1)S(1)} %collective-permute-done.3.gm_other, bf16[128,1024]{1,0:T(8,128)(2,1)S(1)} %copy-done.6, ...), custom_call_target="tpu_custom_call" | custom-call | flops 800000000 | bytes 10000000 | tf_op jit(solution)/shard_map/pallas_call | solution.py:682
  86.5 0.0 copy-start.22
  86.5 6.9 %all-to-all-start.2 = ((bf16[32,16,3072]{2,1,0:T(8,128)(2,1)}), bf16[32,16,3072]{2,1,0:T(8,128)(2,1)}, u32[]{:S(2)}, u32[]{:S(2)}) async-start(bf16[32,16,3072]{2,1,0:T(8,128)(2,1)} %shard_map.151), calls=%async_computation.2 | async-start | bytes 6291456 | tf_op jit(solution)/shard_map/all_to_all | solution.py:689
  93.4 0.0 copy-done.1
  93.4 0.0 copy-done.3
  93.5 0.0 copy-start
  93.5 2.2 %copy-done = bf16[1024,2048]{1,0:T(8,128)(2,1)S(1)} copy-done((bf16[1024,2048]{1,0:T(8,128)(2,1)S(1)}, bf16[1024,2048]{1,0:T(8,128)(2,1)}, u32[]{:S(2)}) %copy-start) | copy-done | bytes 4194328
  95.7 1.2 copy-done.5
  96.9 0.9 copy-done.7
  97.8 1.1 copy-done.8
  99.0 1.1 copy-done.9
  100.1 1.0 copy-done.10
  101.1 1.0 copy-done.11
  102.1 1.0 copy-done.12
  103.1 0.9 copy-done.13
  104.0 0.9 copy-done.16
  104.9 0.9 copy-done.18
  105.8 0.8 copy-done.19
  106.7 12.6 %shard_map.152 = f32[8,128]{1,0:T(8,128)} custom-call(s32[4]{0:T(128)S(1)} %copy-done.21, s32[8]{0:T(128)S(1)} %copy-done.22, bf16[32,112,128]{2,1,0:T(8,128)(2,1)S(1)} %copy-done.1, bf16[128,1024]{1,0:T(8,128)(2,1)S(1)} %copy-done.13, bf16[64,1024]{1,0:T(8,128)(2,1)S(1)} %copy-done.16, bf16[64,1024]{1,0:T(8,128)(2,1)S(1)} %copy-done.18, ...), custom_call_target="tpu_custom_call" | custom-call | flops 3000000000 | bytes 10000000 | tf_op jit(solution)/shard_map/pallas_call | solution.py:690
  119.3 17.9 %all-to-all-done.2 = bf16[32,16,3072]{2,1,0:T(8,128)(2,1)} async-done(((bf16[32,16,3072]{2,1,0:T(8,128)(2,1)}), bf16[32,16,3072]{2,1,0:T(8,128)(2,1)}, u32[]{:S(2)}, u32[]{:S(2)}) %all-to-all-start.2) | async-done | bytes 3145760 | tf_op jit(solution)/shard_map/all_to_all | solution.py:689
  137.2 2.4 %convert_reduce_fusion = f32[16,3072]{1,0:T(8,128)S(1)} fusion(bf16[32,16,3072]{2,1,0:T(8,128)(2,1)} %all-to-all-done.2), kind=kLoop, calls=%fused_computation | loop fusion | flops 3096576 | bytes 3342336 | tf_op jit(solution)/shard_map/reduce_sum | solution.py:705
  139.6 2.3 %collective-permute-start.5 = (bf16[8,3072]{1,0:T(8,128)(2,1)S(1)}, bf16[8,3072]{1,0:T(8,128)(2,1)S(1)}, u32[]{:S(2)}, u32[]{:S(2)}) collective-permute-start(bf16[8,3072]{1,0:T(8,128)(2,1)S(1)} %select_convert_fusion), channel_id=1, source_target_pairs={{0,64},{32,96},{64,0},{96,32},{1,65},{33,97},{65,1},{97,33},{2,66}... | collective-permute-start | bytes 147464 | tf_op jit(solution)/shard_map/ppermute | solution.py:710
  141.9 3.3 %collective-permute-done.5 = bf16[8,3072]{1,0:T(8,128)(2,1)S(1)} collective-permute-done((bf16[8,3072]{1,0:T(8,128)(2,1)S(1)}, bf16[8,3072]{1,0:T(8,128)(2,1)S(1)}, u32[]{:S(2)}, u32[]{:S(2)}) %collective-permute-start.5) | collective-permute-done | bytes 49184 | tf_op jit(solution)/shard_map/ppermute | solution.py:710
  145.3 0.6 slice_add_fusion.1
  145.9 0.6 slice_add_fusion
  (27 shorter events, 0.1 us)
Async XLA Ops:
  6.5 25.2 %all-to-all-start = ((bf16[32,128,128]{2,1,0:T(8,128)(2,1)}), bf16[32,128,128]{2,1,0:T(8,128)(2,1)S(1)}, u32[]{:S(2)}, u32[]{:S(2)}) async-start(bf16[32,128,128]{2,1,0:T(8,128)(2,1)} %get-tuple-element.21), calls=%async_computation | async-start | bytes 2097152 | tf_op jit(solution)/shard_map/all_to_all | solution.py:639
  15.8 14.8 %collective-permute-start = (bf16[64,1024]{1,0:T(8,128)(2,1)}, bf16[64,1024]{1,0:T(8,128)(2,1)S(1)}, u32[]{:S(2)}, u32[]{:S(2)}) collective-permute-start(bf16[64,1024]{1,0:T(8,128)(2,1)} %get-tuple-element.22), channel_id=1, source_target_pairs={{0,1},{1,2},{2,3},{3,4},{4,5},{5,6},{6,7},{7,8},{8,9},{9,10},{10,1... | collective-permute-start | bytes 393224 | tf_op jit(solution)/shard_map/ppermute | solution.py:637
  19.2 12.3 %collective-permute-start.1 = (bf16[64,1024]{1,0:T(8,128)(2,1)}, bf16[64,1024]{1,0:T(8,128)(2,1)S(1)}, u32[]{:S(2)}, u32[]{:S(2)}) collective-permute-start(bf16[64,1024]{1,0:T(8,128)(2,1)} %get-tuple-element.23), channel_id=1, source_target_pairs={{1,0},{2,1},{3,2},{4,3},{5,4},{6,5},{7,6},{8,7},{9,8},{10,9},{11,1... | collective-permute-start | bytes 393224 | tf_op jit(solution)/shard_map/ppermute | solution.py:638
  22.4 20.1 %copy-start.20 = (s32[4]{0:T(128)}, s32[4]{0:T(128)S(1)}, u32[]{:S(2)}) copy-start(s32[4]{0:T(128)S(1)} %pad_add_fusion.scal_ref) | copy-start | bytes 52
  30.7 11.8 %copy-start.15 = (bf16[64,1024]{1,0:T(8,128)(2,1)}, bf16[64,1024]{1,0:T(8,128)(2,1)S(1)}, u32[]{:S(2)}) copy-start(bf16[64,1024]{1,0:T(8,128)(2,1)S(1)} %collective-permute-done.up_hbm.up_ref) | copy-start | bytes 393220
  31.6 10.9 %copy-start.17 = (bf16[64,1024]{1,0:T(8,128)(2,1)}, bf16[64,1024]{1,0:T(8,128)(2,1)S(1)}, u32[]{:S(2)}) copy-start(bf16[64,1024]{1,0:T(8,128)(2,1)S(1)} %collective-permute-done.1.down_hbm.down_ref) | copy-start | bytes 393220
  77.9 3.0 %collective-permute-start.3 = (bf16[128,2048]{1,0:T(8,128)(2,1)}, bf16[128,2048]{1,0:T(8,128)(2,1)S(1)}, u32[]{:S(2)}, u32[]{:S(2)}) collective-permute-start(bf16[128,2048]{1,0:T(8,128)(2,1)} %get-tuple-element.29.gm_ref), channel_id=1, source_target_pairs={{0,32},{32,0},{64,96},{96,64},{1,33},{33,1},{65,97},{97,65},{2,34}... | collective-permute-start | bytes 1572872 | tf_op jit(solution)/shard_map/ppermute | solution.py:680
  78.0 2.5 %collective-permute-start.2 = (bf16[128,1024]{1,0:T(8,128)(2,1)}, bf16[128,1024]{1,0:T(8,128)(2,1)S(1)}, u32[]{:S(2)}, u32[]{:S(2)}) collective-permute-start(bf16[128,1024]{1,0:T(8,128)(2,1)} %get-tuple-element.28), channel_id=1, source_target_pairs={{0,32},{32,0},{64,96},{96,64},{1,33},{33,1},{65,97},{97,65},{2,34}... | collective-permute-start | bytes 786440 | tf_op jit(solution)/shard_map/ppermute | solution.py:680
  78.5 2.4 %collective-permute-start.4 = (bf16[128,1024]{1,0:T(8,128)(2,1)}, bf16[128,1024]{1,0:T(8,128)(2,1)S(1)}, u32[]{:S(2)}, u32[]{:S(2)}) collective-permute-start(bf16[128,1024]{1,0:T(8,128)(2,1)} %get-tuple-element.30.go_ref), channel_id=1, source_target_pairs={{0,32},{32,0},{64,96},{96,64},{1,33},{33,1},{65,97},{97,65},{2,34}... | collective-permute-start | bytes 786440 | tf_op jit(solution)/shard_map/ppermute | solution.py:680
  80.8 1.0 copy-start.2
  81.9 0.9 copy-start.6
  82.8 0.9 copy-start.14
  86.5 6.9 %copy-start.1 = (bf16[32,112,128]{2,1,0:T(8,128)(2,1)S(1)}, bf16[32,112,128]{2,1,0:T(8,128)(2,1)}, u32[]{:S(2)}) copy-start(bf16[32,112,128]{2,1,0:T(8,128)(2,1)} %all_to_all.15.ctx_hbm.ctx_in) | copy-start | bytes 2752516
  86.5 6.9 %copy-start.3 = (bf16[128,2048]{1,0:T(8,128)(2,1)S(1)}, bf16[128,2048]{1,0:T(8,128)(2,1)}, u32[]{:S(2)}) copy-start(bf16[128,2048]{1,0:T(8,128)(2,1)} %get-tuple-element.29.gm_ref) | copy-start | bytes 1572868
  86.5 6.9 %copy-start.4 = (bf16[1024,1024]{1,0:T(8,128)(2,1)S(1)}, bf16[1024,1024]{1,0:T(8,128)(2,1)}, u32[]{:S(2)}) copy-start(bf16[1024,1024]{1,0:T(8,128)(2,1)} %wout_ref.1) | copy-start | bytes 6291460
  86.5 7.0 %copy-start.21 = (s32[4]{0:T(128)S(1)}, s32[4]{0:T(128)}, u32[]{:S(2)}) copy-start(s32[4]{0:T(128)} %copy-done.20) | copy-start | bytes 52
  86.5 7.0 %copy-start.22 = (s32[8]{0:T(128)S(1)}, s32[8]{0:T(128)}, u32[]{:S(2)}) copy-start(s32[8]{0:T(128)} %site_ref.1) | copy-start | bytes 100
  86.5 50.7 %all-to-all-start.2 = ((bf16[32,16,3072]{2,1,0:T(8,128)(2,1)}), bf16[32,16,3072]{2,1,0:T(8,128)(2,1)}, u32[]{:S(2)}, u32[]{:S(2)}) async-start(bf16[32,16,3072]{2,1,0:T(8,128)(2,1)} %shard_map.151), calls=%async_computation.2 | async-start | bytes 6291456 | tf_op jit(solution)/shard_map/all_to_all | solution.py:689
  93.5 2.2 %copy-start = (bf16[1024,2048]{1,0:T(8,128)(2,1)S(1)}, bf16[1024,2048]{1,0:T(8,128)(2,1)}, u32[]{:S(2)}) copy-start(bf16[1024,2048]{1,0:T(8,128)(2,1)} %win_ref.1) | copy-start | bytes 12582916
  95.7 1.2 copy-start.5
  96.9 0.9 copy-start.7
  97.8 1.1 copy-start.8
  99.0 1.1 copy-start.9
  100.1 1.0 copy-start.10
  101.1 1.0 copy-start.11
  102.1 1.0 copy-start.12
  103.1 0.9 copy-start.13
  104.0 0.9 copy-start.16
  104.9 0.9 copy-start.18
  105.8 0.8 copy-start.19
  139.6 5.7 %collective-permute-start.5 = (bf16[8,3072]{1,0:T(8,128)(2,1)S(1)}, bf16[8,3072]{1,0:T(8,128)(2,1)S(1)}, u32[]{:S(2)}, u32[]{:S(2)}) collective-permute-start(bf16[8,3072]{1,0:T(8,128)(2,1)S(1)} %select_convert_fusion), channel_id=1, source_target_pairs={{0,64},{32,96},{64,0},{96,32},{1,65},{33,97},{65,1},{97,33},{2,66}... | collective-permute-start | bytes 147464 | tf_op jit(solution)/shard_map/ppermute | solution.py:710

commit v4 on v3

--- a/solution.py
+++ b/solution.py
@@ -20,6 +20,8 @@
 PATCH = ROWS + RIM
 BOTH = CLEAN + PATCH
 INNER = ROWS + RIM
+UNROLL = 5
+TAP_UNROLL = 2
 
 
 def lane_of(rows):
@@ -97,7 +99,7 @@
             hidden_ref[dest, :] = (centred * inverse).astype(BF16)
         return carry
 
-    lax.fori_loop(0, ROWS // 16, rows, 0)
+    lax.fori_loop(0, ROWS // 16, rows, 0, unroll=UNROLL)
     up_ref[0:RIM, :] = clean_ref[ROWS - RIM : ROWS, :]
     up_ref[RIM : RIM + half, :] = patched_ref[ROWS - half : ROWS, :]
     down_ref[0:RIM, :] = clean_ref[0:RIM, :]
@@ -265,7 +267,7 @@
             target[pl.ds(pl.multiple_of((i * 8 + o) * 8, 8), 8), :] = sums[o]
         return carry
 
-    lax.fori_loop(0, count // 8, rows, 0)
+    lax.fori_loop(0, count // 8, rows, 0, unroll=TAP_UNROLL)
 
 
 def put_rows(ref, row, tile, values):
@@ -346,7 +348,7 @@
         low_ref[at, :] = (centred * inverse).astype(BF16)
         return carry
 
-    lax.fori_loop(0, x_ref.shape[0] // 16, lower, 0)
+    lax.fori_loop(0, x_ref.shape[0] // 16, lower, 0, unroll=UNROLL)
 
 
 def to_gated(low_ref, win_ref, g2_ref, frame, length, keep):
@@ -434,7 +436,7 @@
         sw_ref[pl.ds(r, 16), :] = (zed * sigmoid(zed)).astype(BF16)
         return carry
 
-    lax.fori_loop(0, INNER // 16, clean_rows, 0)
+    lax.fori_loop(0, INNER // 16, clean_rows, 0, unroll=UNROLL)
     sw_copy.start()
 
     for part in range(4):
@@ -470,7 +472,7 @@
                 ]
         return carry
 
-    lax.fori_loop(0, INNER // 16, back_rows, 0)
+    lax.fori_loop(0, INNER // 16, back_rows, 0, unroll=UNROLL)
     depthwise(gsp2_ref, edge, taps_ref, forward[::-1], gg2_ref, ROWS)
     gg2_copy.start()
 
@@ -484,7 +486,7 @@
         gm_ref[at, WIDTH:] = (grad * mv_ref[at, :] * gate * (1.0 - gate)).astype(BF16)
         return carry
 
-    lax.fori_loop(0, ROWS // 16, mixed_rows, 0)
+    lax.fori_loop(0, ROWS // 16, mixed_rows, 0, unroll=UNROLL)
 
     gm_copy.start()
     for copy in results:
@@ -527,7 +529,7 @@
         t1_ref[at, :] = lane_sum(gap * grad)
         return carry
 
-    lax.fori_loop(0, ROWS // 16, patch_rows, 0)
+    lax.fori_loop(0, ROWS // 16, patch_rows, 0, unroll=UNROLL)
 
     t3 = jnp.zeros((ROWS, 128), F32)
     for j in range(4):
@@ -555,7 +557,7 @@
         t0_ref[at, :] = lane_sum((patch - clean) * grad_resid)
         return carry
 
-    lax.fori_loop(0, ROWS // 16, resid_rows, 0)
+    lax.fori_loop(0, ROWS // 16, resid_rows, 0, unroll=UNROLL)
 
     columns = [
         jnp.sum(part, axis=1, keepdims=True) for part in (t0_ref[...], t1_ref[...], t2_ref[...], t3)
@@ -571,21 +573,47 @@
     attr_ref[...] = chosen.T[: attr_ref.shape[0]]
 
 
-def weight_kernel(own_ref, other_ref, gm_ref, gm_other, go_ref, go_other, out_ref):
-    low = jnp.concatenate([own_ref[:, 0:512], other_ref[:, 0:512]], axis=0)
-    swished = jnp.concatenate([own_ref[:, 512:1024], other_ref[:, 512:1024]], axis=0)
+def weight_kernel(
+    own_hbm, other_hbm, gm_hbm, gm_other_hbm, go_hbm, go_other_hbm, out_hbm,
+    left_ref, gm_ref, go_ref, out_ref, in_sems, out_sems,
+):
+    pairs = (
+        (own_hbm, left_ref, 0), (other_hbm, left_ref, ROWS), (go_hbm, go_ref, 0),
+        (go_other_hbm, go_ref, ROWS), (gm_hbm, gm_ref, 0), (gm_other_hbm, gm_ref, ROWS),
+    )
+    copies = [
+        pltpu.make_async_copy(source, target.at[pl.ds(row, ROWS)], in_sems.at[i])
+        for i, (source, target, row) in enumerate(pairs)
+    ]
+    for copy in copies:
+        copy.start()
+
+    def send(i):
+        at = pl.ds(i * WIDTH, WIDTH)
+        return pltpu.make_async_copy(out_ref.at[:, :, at], out_hbm.at[:, :, at], out_sems.at[i])
+
     def put(at, product):
         half = product.shape[0] // 2
         lower = product[:half].reshape(half // 8, 8, 256)
         upper = product[half:].reshape(half // 8, 8, 256)
         out_ref[:, :, at : at + 256] = jnp.concatenate([lower, upper], axis=1).astype(BF16)
 
+    for copy in copies[:4]:
+        copy.wait()
+    swished = left_ref[:, 512:1024].T
+    for j in range(0, WIDTH, 256):
+        put(2 * WIDTH + j, dot(swished, go_ref[:, j : j + 256]))
+    send(2).start()
+    for copy in copies[4:]:
+        copy.wait()
+    low = left_ref[:, 0:512].T
     for j in range(0, 2 * WIDTH, 256):
-        grads = jnp.concatenate([gm_ref[:, j : j + 256], gm_other[:, j : j + 256]], axis=0)
-        put(j, dot_tn(low, grads))
-    for j in range(0, WIDTH, 256):
-        grads = jnp.concatenate([go_ref[:, j : j + 256], go_other[:, j : j + 256]], axis=0)
-        put(2 * WIDTH + j, dot_tn(swished, grads))
+        put(j, dot(low, gm_ref[:, j : j + 256]))
+        if j + 256 == WIDTH:
+            send(0).start()
+    send(1).start()
+    for i in range(3):
+        send(i).wait()
 
 
 VMEM = pl.BlockSpec(memory_space=pltpu.VMEM)
@@ -637,7 +665,6 @@
     from_left = lax.ppermute(up, "frames", forward)
     from_right = lax.ppermute(down, "frames", backward)
     recv = lax.all_to_all(msg, "frames", 0, 0, tiled=True)
-    recv, from_left, from_right = lax.optimization_barrier((recv, from_left, from_right))
     keys = frames * ROWS // 2
     (context,) = kernel_call(
         attend_kernel,
@@ -671,7 +698,7 @@
          pltpu.VMEM((INNER, 128), F32), pltpu.VMEM((INNER, WIDTH), BF16),
          pltpu.VMEM((INNER * 8, 128), F32), pltpu.VMEM((32 * 8, 128), F32),
          pltpu.SemaphoreType.DMA((11,)), pltpu.SemaphoreType.DMA((9,))],
-        62, 3 * 10**9, 10**7, HBM,
+        59, 3 * 10**9, 10**7, HBM,
     )(scalars, contexts, clean, cot, from_left, from_right,
       w_attn_out, w_pointwise_in, depth_kernel, w_pointwise_out)
 
@@ -682,9 +709,11 @@
     (partial,) = kernel_call(
         weight_kernel,
         [shape((frames, 16, 3 * WIDTH), BF16)],
-        [VMEM] * 6,
-        [],
-        32, 8 * 10**8, 10**7,
+        [HBM] * 6,
+        [pltpu.VMEM((2 * ROWS, WIDTH), BF16), pltpu.VMEM((2 * ROWS, 2 * WIDTH), BF16),
+         pltpu.VMEM((2 * ROWS, WIDTH), BF16), pltpu.VMEM((frames, 16, 3 * WIDTH), BF16),
+         pltpu.SemaphoreType.DMA((6,)), pltpu.SemaphoreType.DMA((3,))],
+        59, 8 * 10**8, 10**7, HBM,
     )(own, other, grad_mixed, gm_other, grad_output, go_other)
     pieces = lax.all_to_all(partial, "frames", 0, 0, tiled=True)
     (attribution,) = kernel_call(

time: 147 us -> 143 us (0.973)
  blocking collectives: 20.6 us -> 0 us
  waiting for transfers between devices: 32.8 us -> 48.9 us
  starting transfers between devices: 25.1 us -> 33.2 us
  Pallas kernels: 46.7 us -> 40 us
    all_to_all x1 -> x0, blocking collectives: 20.6 us -> none  [per_device(): contexts = lax.all_to_all(context, 'frames', 0, 0, tiled=True)]
    all_to_all x1, waiting for transfers between devices: 0.13 us -> 14.7 us  [per_device(): recv = lax.all_to_all(msg, 'frames', 0, 0, tiled=True)]
    all_to_all x0 -> x1, starting transfers between devices: none -> 6.13 us  [per_device(): contexts = lax.all_to_all(context, 'frames', 0, 0, tiled=True)]
    pallas_call x1, Pallas kernels: 14.8 us -> 10.8 us  [per_device(): kernel_call(clean_kernel, [shape((ROWS, 1024), BF16), shape((ROWS, 1024),...]
    pallas_call x1, Pallas kernels: 12.6 us -> 9.13 us  [per_device(): kernel_call(patch_kernel, [shape((site_ids.shape[0], ROWS), F32)], [SMEM,...]
    all_to_all x1, waiting for transfers between devices: 17.9 us -> 20.5 us  [per_device(): pieces = lax.all_to_all(partial, 'frames', 0, 0, tiled=True)]
    all_to_all x1, starting transfers between devices: 6.88 us -> 8.79 us  [per_device(): pieces = lax.all_to_all(partial, 'frames', 0, 0, tiled=True)]
    ppermute x1, waiting for transfers between devices: 8.23 us -> 6.45 us  [per_device(): from_left = lax.ppermute(up, 'frames', forward)]
  transfers between devices with their start and end apart: 8 -> 9, of which waited for: 7 -> 8; matrix products, arithmetic and copies ran while one was open for 0% -> 0% of each run, Pallas kernels for 9% -> 6%
where the time goes in v4:
time: 143 us; the launch traced here: 142 us
  waiting for transfers between devices  48.9 us (34%)
  Pallas kernels  40 us (28%)
  starting transfers between devices  33.2 us (23%)
  local copies, waits for them, and re-layouts  15 us (10%)
  other arithmetic  3.75 us (3%)
  between operations  1.52 us (1%)
    all_to_all x1, waiting for transfers between devices, per_device(): pieces = lax.all_to_all(partial, 'frames', 0, 0, tiled=True)  20.5 us
    unnamed x52, local copies, waits for them, and re-layouts  15 us
    all_to_all x1, waiting for transfers between devices, per_device(): recv = lax.all_to_all(msg, 'frames', 0, 0, tiled=True)  14.7 us
    pallas_call x1, Pallas kernels, per_device(): kernel_call(attend_kernel, [shape((frames, 112, 128), BF16)], [SMEM, VMEM...  11.7 us
    pallas_call x1, Pallas kernels, per_device(): kernel_call(clean_kernel, [shape((ROWS, 1024), BF16), shape((ROWS, 1024),...  10.8 us
    all_to_all x1, starting transfers between devices, per_device(): recv = lax.all_to_all(msg, 'frames', 0, 0, tiled=True)  9.37 us
    pallas_call x1, Pallas kernels, per_device(): kernel_call(patch_kernel, [shape((site_ids.shape[0], ROWS), F32)], [SMEM,...  9.13 us
    all_to_all x1, starting transfers between devices, per_device(): pieces = lax.all_to_all(partial, 'frames', 0, 0, tiled=True)  8.79 us
  transfers between devices with their start and end apart: 9, of which 8 were waited for; matrix products, arithmetic and copies ran while one was open for 0% of the time, Pallas kernels for 6%

profile of v4, /device:TPU:10, one launch (start us, length us, event | category | flops | bytes accessed | tf_op | source)
XLA Modules:
  0.0 142.4 jit_solution(9000315841731006322)
XLA Ops:
  0.6 4.8 %shard_map.148 = (bf16[32,128,128]{2,1,0:T(8,128)(2,1)}, bf16[128,1024]{1,0:T(8,128)(2,1)}, bf16[64,1024]{1,0:T(8,128)(2,1)}, bf16[64,1024]{1,0:T(8,128)(2,1)}) custom-call(bf16[128,1024]{1,0:T(8,128)(2,1)} %bitcast.8, bf16[128,1024]{1,0:T(8,128)(2,1)} %bitcast.7, bf16[128,1024]{1,0:T(8,128)(2,1)} %bitcast.10, s32[1,128]{1,0:T(1,128)} %mask_ref.1, ...), custom_call_target="tpu_custom_call" | custom-call | flops 800000000 | bytes 6000000 | tf_op jit(solution)/shard_map/pallas_call | solution.py:652
  5.5 9.4 %all-to-all-start = ((bf16[32,128,128]{2,1,0:T(8,128)(2,1)}), bf16[32,128,128]{2,1,0:T(8,128)(2,1)S(1)}, u32[]{:S(2)}, u32[]{:S(2)}) async-start(bf16[32,128,128]{2,1,0:T(8,128)(2,1)} %get-tuple-element.18), calls=%async_computation | async-start | bytes 2097152 | tf_op jit(solution)/shard_map/all_to_all | solution.py:667
  15.5 0.1 pad_add_fusion.scal_ref
  15.6 14.7 %all-to-all-done.recv_ref = bf16[32,128,128]{2,1,0:T(8,128)(2,1)S(1)} async-done(((bf16[32,128,128]{2,1,0:T(8,128)(2,1)}), bf16[32,128,128]{2,1,0:T(8,128)(2,1)S(1)}, u32[]{:S(2)}, u32[]{:S(2)}) %all-to-all-start) | async-done | bytes 1048608 | tf_op jit(solution)/shard_map/all_to_all | solution.py:667
  30.3 11.7 %shard_map.149 = bf16[32,112,128]{2,1,0:T(8,128)(2,1)} custom-call(s32[4]{0:T(128)S(1)} %pad_add_fusion.scal_ref, bf16[32,128,128]{2,1,0:T(8,128)(2,1)S(1)} %all-to-all-done.recv_ref), custom_call_target="tpu_custom_call" | custom-call | flops 8000000000 | bytes 1000000 | tf_op jit(solution)/shard_map/pallas_call | solution.py:669
  42.0 6.1 %all-to-all-start.1 = ((bf16[32,112,128]{2,1,0:T(8,128)(2,1)}), bf16[32,112,128]{2,1,0:T(8,128)(2,1)S(1)}, u32[]{:S(2)}, u32[]{:S(2)}) async-start(bf16[32,112,128]{2,1,0:T(8,128)(2,1)} %shard_map.149), calls=%async_computation.1 | async-start | bytes 1835008 | tf_op jit(solution)/shard_map/all_to_all | solution.py:679
  48.2 0.0 copy-done.25
  48.2 3.4 %collective-permute-start = (bf16[64,1024]{1,0:T(8,128)(2,1)S(1)}, bf16[64,1024]{1,0:T(8,128)(2,1)S(1)}, u32[]{:S(2)}, u32[]{:S(2)}) collective-permute-start(bf16[64,1024]{1,0:T(8,128)(2,1)S(1)} %copy-done.25), channel_id=1, source_target_pairs={{0,1},{1,2},{2,3},{3,4},{4,5},{5,6},{6,7},{7,8},{8,9},{9,10},{10,1... | collective-permute-start | bytes 393224 | tf_op jit(solution)/shard_map/ppermute | solution.py:665
  51.6 2.5 %collective-permute-start.1 = (bf16[64,1024]{1,0:T(8,128)(2,1)S(1)}, bf16[64,1024]{1,0:T(8,128)(2,1)S(1)}, u32[]{:S(2)}, u32[]{:S(2)}) collective-permute-start(bf16[64,1024]{1,0:T(8,128)(2,1)S(1)} %copy-done.24), channel_id=1, source_target_pairs={{1,0},{2,1},{3,2},{4,3},{5,4},{6,5},{7,6},{8,7},{9,8},{10,9},{11,1... | collective-permute-start | bytes 393224 | tf_op jit(solution)/shard_map/ppermute | solution.py:666
  54.1 6.5 %collective-permute-done.up_hbm.up_ref = bf16[64,1024]{1,0:T(8,128)(2,1)S(1)} collective-permute-done((bf16[64,1024]{1,0:T(8,128)(2,1)S(1)}, bf16[64,1024]{1,0:T(8,128)(2,1)S(1)}, u32[]{:S(2)}, u32[]{:S(2)}) %collective-permute-start) | collective-permute-done | bytes 131104 | tf_op jit(solution)/shard_map/ppermute | solution.py:665
  60.5 0.9 collective-permute-done.1.down_hbm.down_ref
  61.4 0.8 all-to-all-done.1.ctx_hbm.ctx_in
  62.2 0.9 copy-done.1
  63.1 10.8 %shard_map.150 = (bf16[128,1024]{1,0:T(8,128)(2,1)}, bf16[128,1024]{1,0:T(8,128)(2,1)}, bf16[128,2048]{1,0:T(8,128)(2,1)}, bf16[128,1024]{1,0:T(8,128)(2,1)}, bf...) custom-call(s32[4]{0:T(128)} %copy-done.18, ...), custom_call_target="tpu_custom_call" | custom-call | flops 3000000000 | bytes 10000000 | tf_op jit(solution)/shard_map/pallas_call | solution.py:680
  73.9 0.1 collective-permute-start.3
  74.0 0.5 collective-permute-start.2
  74.5 0.1 collective-permute-start.4
  74.6 1.9 %collective-permute-done.2.other_hbm = bf16[128,1024]{1,0:T(8,128)(2,1)S(1)} collective-permute-done((bf16[128,1024]{1,0:T(8,128)(2,1)}, bf16[128,1024]{1,0:T(8,128)(2,1)S(1)}, u32[]{:S(2)}, u32[]{:S(2)}) %collective-permute-start.2) | collective-permute-done | bytes 262176 | tf_op jit(solution)/shard_map/ppermute | solution.py:707
  76.5 0.4 collective-permute-done.4.go_other_hbm
  76.9 0.0 collective-permute-done.3.gm_other_hbm
  76.9 0.3 copy-done.22
  77.2 0.4 copy-done.23
  77.6 0.2 copy-done.21
  77.8 3.5 %shard_map.151 = bf16[32,16,3072]{2,1,0:T(8,128)(2,1)} custom-call(bf16[128,1024]{1,0:T(8,128)(2,1)} %get-tuple-element.21.own_hbm, bf16[128,1024]{1,0:T(8,128)(2,1)} %copy-done.22, bf16[128,2048]{1,0:T(8,128)(2,1)} %get-tuple-element.23.gm_hbm.gm_ref, bf16[128,2048]{1,0:T(8,128)(2,1)} %copy-done.21, bf16[128,1024]{1,0:T(8,128)(2,1)} %get-tuple-element.24.go_hbm.go_ref, ...), custom_call_target="tpu_custom_call" | custom-call | flops 800000000 | bytes 10000000 | tf_op jit(solution)/shard_map/pallas_call | solution.py:709
  81.4 0.0 copy-start.4
  81.4 0.0 copy-start.19
  81.4 0.0 copy-start.20
  81.4 8.8 %all-to-all-start.2 = ((bf16[32,16,3072]{2,1,0:T(8,128)(2,1)}), bf16[32,16,3072]{2,1,0:T(8,128)(2,1)}, u32[]{:S(2)}, u32[]{:S(2)}) async-start(bf16[32,16,3072]{2,1,0:T(8,128)(2,1)} %shard_map.151), calls=%async_computation.2 | async-start | bytes 6291456 | tf_op jit(solution)/shard_map/all_to_all | solution.py:718
  90.3 0.0 copy-start
  90.3 2.2 %copy-done = bf16[1024,2048]{1,0:T(8,128)(2,1)S(1)} copy-done((bf16[1024,2048]{1,0:T(8,128)(2,1)S(1)}, bf16[1024,2048]{1,0:T(8,128)(2,1)}, u32[]{:S(2)}) %copy-start) | copy-done | bytes 4194328
  92.4 1.2 copy-done.5
  93.7 0.9 copy-done.6
  94.6 1.1 copy-done.7
  95.8 1.1 copy-done.8
  96.8 1.0 copy-done.9
  97.9 1.0 copy-done.10
  98.9 1.0 copy-done.11
  99.9 0.9 copy-done.12
  100.8 0.9 copy-done.14
  101.7 0.9 copy-done.16
  102.6 0.8 copy-done.17
  103.5 9.1 %shard_map.152 = f32[8,128]{1,0:T(8,128)} custom-call(s32[4]{0:T(128)S(1)} %copy-done.19, s32[8]{0:T(128)S(1)} %copy-done.20, bf16[32,112,128]{2,1,0:T(8,128)(2,1)S(1)} %copy-done.2, bf16[128,1024]{1,0:T(8,128)(2,1)S(1)} %copy-done.12, bf16[64,1024]{1,0:T(8,128)(2,1)S(1)} %copy-done.14, bf16[64,1024]{1,0:T(8,128)(2,1)S(1)} %copy-done.16, ...), custom_call_target="tpu_custom_call" | custom-call | flops 3000000000 | bytes 10000000 | tf_op jit(solution)/shard_map/pallas_call | solution.py:719
  112.6 20.5 %all-to-all-done.2 = bf16[32,16,3072]{2,1,0:T(8,128)(2,1)} async-done(((bf16[32,16,3072]{2,1,0:T(8,128)(2,1)}), bf16[32,16,3072]{2,1,0:T(8,128)(2,1)}, u32[]{:S(2)}, u32[]{:S(2)}) %all-to-all-start.2) | async-done | bytes 3145760 | tf_op jit(solution)/shard_map/all_to_all | solution.py:718
  133.1 2.4 %convert_reduce_fusion = f32[16,3072]{1,0:T(8,128)S(1)} fusion(bf16[32,16,3072]{2,1,0:T(8,128)(2,1)} %all-to-all-done.2), kind=kLoop, calls=%fused_computation | loop fusion | flops 3096576 | bytes 3342336 | tf_op jit(solution)/shard_map/reduce_sum | solution.py:734
  135.5 2.4 %collective-permute-start.5 = (bf16[8,3072]{1,0:T(8,128)(2,1)S(1)}, bf16[8,3072]{1,0:T(8,128)(2,1)S(1)}, u32[]{:S(2)}, u32[]{:S(2)}) collective-permute-start(bf16[8,3072]{1,0:T(8,128)(2,1)S(1)} %select_convert_fusion), channel_id=1, source_target_pairs={{0,64},{32,96},{64,0},{96,32},{1,65},{33,97},{65,1},{97,33},{2,66}... | collective-permute-start | bytes 147464 | tf_op jit(solution)/shard_map/ppermute | solution.py:739
  137.9 3.3 %collective-permute-done.5 = bf16[8,3072]{1,0:T(8,128)(2,1)S(1)} collective-permute-done((bf16[8,3072]{1,0:T(8,128)(2,1)S(1)}, bf16[8,3072]{1,0:T(8,128)(2,1)S(1)}, u32[]{:S(2)}, u32[]{:S(2)}) %collective-permute-start.5) | collective-permute-done | bytes 49184 | tf_op jit(solution)/shard_map/ppermute | solution.py:739
  141.2 0.6 slice_add_fusion.1
  141.8 0.6 slice_add_fusion
  (34 shorter events, 0.1 us)
Async XLA Ops:
  5.5 24.9 %all-to-all-start = ((bf16[32,128,128]{2,1,0:T(8,128)(2,1)}), bf16[32,128,128]{2,1,0:T(8,128)(2,1)S(1)}, u32[]{:S(2)}, u32[]{:S(2)}) async-start(bf16[32,128,128]{2,1,0:T(8,128)(2,1)} %get-tuple-element.18), calls=%async_computation | async-start | bytes 2097152 | tf_op jit(solution)/shard_map/all_to_all | solution.py:667
  15.6 26.5 %copy-start.18 = (s32[4]{0:T(128)}, s32[4]{0:T(128)S(1)}, u32[]{:S(2)}) copy-start(s32[4]{0:T(128)S(1)} %pad_add_fusion.scal_ref) | copy-start | bytes 52
  15.6 32.6 %copy-start.25 = (bf16[64,1024]{1,0:T(8,128)(2,1)S(1)}, bf16[64,1024]{1,0:T(8,128)(2,1)}, u32[]{:S(2)}) copy-start(bf16[64,1024]{1,0:T(8,128)(2,1)} %get-tuple-element.19) | copy-start | bytes 393220
  15.6 36.0 %copy-start.24 = (bf16[64,1024]{1,0:T(8,128)(2,1)S(1)}, bf16[64,1024]{1,0:T(8,128)(2,1)}, u32[]{:S(2)}) copy-start(bf16[64,1024]{1,0:T(8,128)(2,1)} %get-tuple-element.20) | copy-start | bytes 393220
  42.0 20.2 %all-to-all-start.1 = ((bf16[32,112,128]{2,1,0:T(8,128)(2,1)}), bf16[32,112,128]{2,1,0:T(8,128)(2,1)S(1)}, u32[]{:S(2)}, u32[]{:S(2)}) async-start(bf16[32,112,128]{2,1,0:T(8,128)(2,1)} %shard_map.149), calls=%async_computation.1 | async-start | bytes 1835008 | tf_op jit(solution)/shard_map/all_to_all | solution.py:679
  48.2 12.3 %collective-permute-start = (bf16[64,1024]{1,0:T(8,128)(2,1)S(1)}, bf16[64,1024]{1,0:T(8,128)(2,1)S(1)}, u32[]{:S(2)}, u32[]{:S(2)}) collective-permute-start(bf16[64,1024]{1,0:T(8,128)(2,1)S(1)} %copy-done.25), channel_id=1, source_target_pairs={{0,1},{1,2},{2,3},{3,4},{4,5},{5,6},{6,7},{7,8},{8,9},{9,10},{10,1... | collective-permute-start | bytes 393224 | tf_op jit(solution)/shard_map/ppermute | solution.py:665
  51.6 9.8 %collective-permute-start.1 = (bf16[64,1024]{1,0:T(8,128)(2,1)S(1)}, bf16[64,1024]{1,0:T(8,128)(2,1)S(1)}, u32[]{:S(2)}, u32[]{:S(2)}) collective-permute-start(bf16[64,1024]{1,0:T(8,128)(2,1)S(1)} %copy-done.24), channel_id=1, source_target_pairs={{1,0},{2,1},{3,2},{4,3},{5,4},{6,5},{7,6},{8,7},{9,8},{10,9},{11,1... | collective-permute-start | bytes 393224 | tf_op jit(solution)/shard_map/ppermute | solution.py:666
  60.5 1.7 %copy-start.13 = (bf16[64,1024]{1,0:T(8,128)(2,1)}, bf16[64,1024]{1,0:T(8,128)(2,1)S(1)}, u32[]{:S(2)}) copy-start(bf16[64,1024]{1,0:T(8,128)(2,1)S(1)} %collective-permute-done.up_hbm.up_ref) | copy-start | bytes 393220
  61.4 0.8 copy-start.15
  62.2 0.9 copy-start.1
  73.9 3.0 %collective-permute-start.3 = (bf16[128,2048]{1,0:T(8,128)(2,1)}, bf16[128,2048]{1,0:T(8,128)(2,1)S(1)}, u32[]{:S(2)}, u32[]{:S(2)}) collective-permute-start(bf16[128,2048]{1,0:T(8,128)(2,1)} %get-tuple-element.23.gm_hbm.gm_ref), channel_id=1, source_target_pairs={{0,32},{32,0},{64,96},{96,64},{1,33},{33,1},{65,97},{97,65},{2,34}... | collective-permute-start | bytes 1572872 | tf_op jit(solution)/shard_map/ppermute | solution.py:707
  74.0 2.5 %collective-permute-start.2 = (bf16[128,1024]{1,0:T(8,128)(2,1)}, bf16[128,1024]{1,0:T(8,128)(2,1)S(1)}, u32[]{:S(2)}, u32[]{:S(2)}) collective-permute-start(bf16[128,1024]{1,0:T(8,128)(2,1)} %get-tuple-element.22), channel_id=1, source_target_pairs={{0,32},{32,0},{64,96},{96,64},{1,33},{33,1},{65,97},{97,65},{2,34}... | collective-permute-start | bytes 786440 | tf_op jit(solution)/shard_map/ppermute | solution.py:707
  74.5 2.4 %collective-permute-start.4 = (bf16[128,1024]{1,0:T(8,128)(2,1)}, bf16[128,1024]{1,0:T(8,128)(2,1)S(1)}, u32[]{:S(2)}, u32[]{:S(2)}) collective-permute-start(bf16[128,1024]{1,0:T(8,128)(2,1)} %get-tuple-element.24.go_hbm.go_ref), channel_id=1, source_target_pairs={{0,32},{32,0},{64,96},{96,64},{1,33},{33,1},{65,97},{97,65},{2,34}... | collective-permute-start | bytes 786440 | tf_op jit(solution)/shard_map/ppermute | solution.py:707
  76.5 0.7 copy-start.22
  76.9 0.7 copy-start.23
  76.9 0.9 copy-start.21
  81.3 8.9 %copy-start.2 = (bf16[32,112,128]{2,1,0:T(8,128)(2,1)S(1)}, bf16[32,112,128]{2,1,0:T(8,128)(2,1)}, u32[]{:S(2)}) copy-start(bf16[32,112,128]{2,1,0:T(8,128)(2,1)} %copy-done.1) | copy-start | bytes 2752516
  81.3 8.9 %copy-start.3 = (bf16[128,2048]{1,0:T(8,128)(2,1)S(1)}, bf16[128,2048]{1,0:T(8,128)(2,1)}, u32[]{:S(2)}) copy-start(bf16[128,2048]{1,0:T(8,128)(2,1)} %get-tuple-element.23.gm_hbm.gm_ref) | copy-start | bytes 1572868
  81.4 8.9 %copy-start.4 = (bf16[1024,1024]{1,0:T(8,128)(2,1)S(1)}, bf16[1024,1024]{1,0:T(8,128)(2,1)}, u32[]{:S(2)}) copy-start(bf16[1024,1024]{1,0:T(8,128)(2,1)} %wout_ref.1) | copy-start | bytes 6291460
  81.4 8.9 %copy-start.19 = (s32[4]{0:T(128)S(1)}, s32[4]{0:T(128)}, u32[]{:S(2)}) copy-start(s32[4]{0:T(128)} %copy-done.18) | copy-start | bytes 52
  81.4 8.9 %copy-start.20 = (s32[8]{0:T(128)S(1)}, s32[8]{0:T(128)}, u32[]{:S(2)}) copy-start(s32[8]{0:T(128)} %site_ref.1) | copy-start | bytes 100
  81.4 51.7 %all-to-all-start.2 = ((bf16[32,16,3072]{2,1,0:T(8,128)(2,1)}), bf16[32,16,3072]{2,1,0:T(8,128)(2,1)}, u32[]{:S(2)}, u32[]{:S(2)}) async-start(bf16[32,16,3072]{2,1,0:T(8,128)(2,1)} %shard_map.151), calls=%async_computation.2 | async-start | bytes 6291456 | tf_op jit(solution)/shard_map/all_to_all | solution.py:718
  90.3 2.2 %copy-start = (bf16[1024,2048]{1,0:T(8,128)(2,1)S(1)}, bf16[1024,2048]{1,0:T(8,128)(2,1)}, u32[]{:S(2)}) copy-start(bf16[1024,2048]{1,0:T(8,128)(2,1)} %win_ref.1) | copy-start | bytes 12582916
  92.4 1.2 copy-start.5
  93.7 0.9 copy-start.6
  94.6 1.1 copy-start.7
  95.8 1.1 copy-start.8
  96.8 1.0 copy-start.9
  97.9 1.0 copy-start.10
  98.9 1.0 copy-start.11
  99.9 0.9 copy-start.12
  100.8 0.9 copy-start.14
  101.7 0.9 copy-start.16
  102.6 0.8 copy-start.17
  135.5 5.7 %collective-permute-start.5 = (bf16[8,3072]{1,0:T(8,128)(2,1)S(1)}, bf16[8,3072]{1,0:T(8,128)(2,1)S(1)}, u32[]{:S(2)}, u32[]{:S(2)}) collective-permute-start(bf16[8,3072]{1,0:T(8,128)(2,1)S(1)} %select_convert_fusion), channel_id=1, source_target_pairs={{0,64},{32,96},{64,0},{96,32},{1,65},{33,97},{65,1},{97,33},{2,66}... | collective-permute-start | bytes 147464 | tf_op jit(solution)/shard_map/ppermute | solution.py:739

commit v5 on v4

--- a/solution.py
+++ b/solution.py
@@ -20,8 +20,11 @@
 PATCH = ROWS + RIM
 BOTH = CLEAN + PATCH
 INNER = ROWS + RIM
-UNROLL = 5
-TAP_UNROLL = 2
+UNROLL = True
+TAP_UNROLL = 4
+LOAD_UNROLL = 4
+PACK_UNROLL = 4
+CHUNK = 256
 
 
 def lane_of(rows):
@@ -159,10 +162,10 @@
         qt_ref[:, pl.ds(at + 128, 128)] = jnp.where(row < 64, other, fill).astype(BF16)
         return carry
 
-    lax.fori_loop(0, sources // 2, load, 0, unroll=4)
+    lax.fori_loop(0, sources // 2, load, 0, unroll=LOAD_UNROLL)
 
     many = s0_ref.shape[1]
-    chunk = 256
+    chunk = CHUNK
     pieces = k_ref.shape[0] // chunk
     blocks = sources * ROWS // many
 
@@ -249,7 +252,7 @@
         out_ref[d, 96:112, :] = jnp.concatenate([rows, rows], axis=0).astype(BF16)
         return carry
 
-    lax.fori_loop(0, sources, pack, 0, unroll=2)
+    lax.fori_loop(0, sources, pack, 0, unroll=PACK_UNROLL)
 
 
 def depthwise(source, source_row, taps_ref, order, target, count):
@@ -351,11 +354,14 @@
     lax.fori_loop(0, x_ref.shape[0] // 16, lower, 0, unroll=UNROLL)
 
 
-def to_gated(low_ref, win_ref, g2_ref, frame, length, keep):
+def to_gated(low_ref, win_ref, g2_ref, frame, length, keep, arrivals=None):
     live = jnp.where((frame >= 0) & (frame < length), 1.0, 0.0)
     for j in range(4):
         at = slice(j * 256, j * 256 + 256)
         gate_at = slice(WIDTH + j * 256, WIDTH + j * 256 + 256)
+        if arrivals is not None:
+            arrivals[2 * j].wait()
+            arrivals[2 * j + 1].wait()
         value = dot(low_ref[...], win_ref[:, at])
         gate = sigmoid(dot(low_ref[...], win_ref[:, gate_at]))
         if keep is not None:
@@ -390,7 +396,11 @@
             (up_hbm.at[pl.ds(RIM + half, half)], gox_ref.at[pl.ds(0, half)]),
             (cot_hbm, gox_ref.at[pl.ds(half, ROWS)]),
             (down_hbm.at[pl.ds(RIM + half, half)], gox_ref.at[pl.ds(half + ROWS, half)]),
-            (win_hbm, win_ref),
+            *(
+                (win_hbm.at[:, pl.ds(at, 256)], win_ref.at[:, pl.ds(at, 256)])
+                for j in range(0, WIDTH, 256)
+                for at in (j, WIDTH + j)
+            ),
             (wout_hbm, wout_ref),
         ))
     ]
@@ -420,8 +430,7 @@
     to_lowered(x_ref, ctx_ref, wao_ref, resid_ref, low_ref)
     resid_copy.start()
     frame = first_frame - RIM + lax.broadcasted_iota(jnp.int32, (CLEAN, 1), 0)
-    copies[9].wait()
-    to_gated(low_ref, win_ref, g2_ref, frame, length, (mv_ref, sg_ref))
+    to_gated(low_ref, win_ref, g2_ref, frame, length, (mv_ref, sg_ref), copies[9:17])
     g2_copy.start()
     forward = list(range(KERNEL))
     edge = half - KERNEL // 2
@@ -450,7 +459,7 @@
     own_copy.start()
     send_copy.start()
 
-    copies[10].wait()
+    copies[17].wait()
     for j in range(4):
         at = slice(j * 256, j * 256 + 256)
         gs_ref[:, at] = dot_nt(gox_ref[...], wout_ref[at, :])
@@ -616,6 +625,28 @@
         send(i).wait()
 
 
+def fold_kernel(scal_ref, pieces_ref, mine_ref, theirs_ref):
+    upper = scal_ref[4]
+
+    def columns(j, carry):
+        at = pl.ds(pl.multiple_of(j * 256, 256), 256)
+        total = pieces_ref[0, :, at].astype(F32)
+        for k in range(1, pieces_ref.shape[0]):
+            total = total + pieces_ref[k, :, at].astype(F32)
+        first, second = total[:8], total[8:]
+        mine_ref[:, at] = jnp.where(upper == 0, first, second)
+        theirs_ref[:, at] = jnp.where(upper == 0, second, first)
+        return carry
+
+    lax.fori_loop(0, mine_ref.shape[1] // 256, columns, 0, unroll=2)
+
+
+def join_kernel(mine_ref, theirs_ref, in_ref, out_ref):
+    whole = mine_ref[...] + theirs_ref[...]
+    in_ref[...] = whole[:, : 2 * WIDTH]
+    out_ref[...] = whole[:, 2 * WIDTH :]
+
+
 VMEM = pl.BlockSpec(memory_space=pltpu.VMEM)
 SMEM = pl.BlockSpec(memory_space=pltpu.SMEM)
 HBM = pl.BlockSpec(memory_space=pltpu.HBM)
@@ -645,7 +676,7 @@
     position = lax.axis_index("frames")
     core = lax.rem(lax.axis_index("dp"), 2)
     scalars = jnp.stack(
-        [position * ROWS, lengths[0], core, lax.rem(position, 2)]
+        [position * ROWS, lengths[0], core, lax.rem(position, 2), lax.axis_index("dp") // 2]
     ).astype(jnp.int32)
     clean, corrupt, cot = clean_input[0], corrupt_input[0], cotangent[0]
 
@@ -665,6 +696,7 @@
     from_left = lax.ppermute(up, "frames", forward)
     from_right = lax.ppermute(down, "frames", backward)
     recv = lax.all_to_all(msg, "frames", 0, 0, tiled=True)
+    recv, from_left, from_right = lax.optimization_barrier((recv, from_left, from_right))
     keys = frames * ROWS // 2
     (context,) = kernel_call(
         attend_kernel,
@@ -697,7 +729,7 @@
          pltpu.VMEM((INNER * 8, 128), F32), pltpu.VMEM((INNER, WIDTH), F32),
          pltpu.VMEM((INNER, 128), F32), pltpu.VMEM((INNER, WIDTH), BF16),
          pltpu.VMEM((INNER * 8, 128), F32), pltpu.VMEM((32 * 8, 128), F32),
-         pltpu.SemaphoreType.DMA((11,)), pltpu.SemaphoreType.DMA((9,))],
+         pltpu.SemaphoreType.DMA((18,)), pltpu.SemaphoreType.DMA((9,))],
         59, 3 * 10**9, 10**7, HBM,
     )(scalars, contexts, clean, cot, from_left, from_right,
       w_attn_out, w_pointwise_in, depth_kernel, w_pointwise_out)
@@ -731,19 +763,23 @@
       w_attn_out, w_pointwise_in, depth_kernel, w_pointwise_out,
       grad_mixed, grad_output, swished, grad_swished, grad_gated, gated, resid)
     pieces, attribution = lax.optimization_barrier((pieces, attribution))
-    summed = jnp.sum(pieces.astype(F32), axis=0)
-    upper = lax.axis_index("dp") // 2
-    mine = jnp.where(upper == 0, summed[:8], summed[8:])
-    theirs = jnp.where(upper == 0, summed[8:], summed[:8])
+    mine, theirs = kernel_call(
+        fold_kernel,
+        [shape((8, 3 * WIDTH), F32), shape((8, 3 * WIDTH), F32)],
+        [SMEM, VMEM],
+        [],
+        16, 10**8, 3 * 10**6,
+    )(scalars, pieces)
     half_dp = lax.axis_size("dp") // 2
-    theirs = lax.ppermute(
-        theirs.astype(BF16), "dp", [(i, i ^ half_dp) for i in range(2 * half_dp)]
-    ).astype(F32)
-    return (
-        attribution[None],
-        mine[:, : 2 * WIDTH] + theirs[:, : 2 * WIDTH],
-        mine[:, 2 * WIDTH :] + theirs[:, 2 * WIDTH :],
-    )
+    theirs = lax.ppermute(theirs, "dp", [(i, i ^ half_dp) for i in range(2 * half_dp)])
+    grad_in, grad_out = kernel_call(
+        join_kernel,
+        [shape((8, 2 * WIDTH), F32), shape((8, WIDTH), F32)],
+        [VMEM] * 2,
+        [],
+        16, 10**6, 10**6,
+    )(mine, theirs)
+    return attribution[None], grad_in, grad_out
 
 
 def solution(mesh):

time: 143 us -> 138 us (0.965)
  blocking collectives: 0 us -> 20.6 us
  waiting for transfers between devices: 48.9 us -> 35.5 us
  starting transfers between devices: 33.2 us -> 25.1 us
  other arithmetic: 3.75 us -> 0 us
  Pallas kernels: 40 us -> 38.3 us
    all_to_all x0 -> x1, blocking collectives: none -> 20.6 us  [per_device(): contexts = lax.all_to_all(context, 'frames', 0, 0, tiled=True)]
    all_to_all x1, waiting for transfers between devices: 14.7 us -> 0.13 us  [per_device(): recv = lax.all_to_all(msg, 'frames', 0, 0, tiled=True)]
    all_to_all x1 -> x0, starting transfers between devices: 6.13 us -> none  [per_device(): contexts = lax.all_to_all(context, 'frames', 0, 0, tiled=True)]
    reduce_sum x1 -> x0, other arithmetic: 2.38 us -> none  [per_device(): summed = jnp.sum(pieces.astype(F32), axis=0)]
    all_to_all x1, starting transfers between devices: 8.79 us -> 6.7 us  [per_device(): pieces = lax.all_to_all(partial, 'frames', 0, 0, tiled=True)]
    pallas_call x1, Pallas kernels: 9.13 us -> 7.34 us  [per_device(): kernel_call(patch_kernel, [shape((site_ids.shape[0], ROWS), F32)], [SMEM,...]
    pallas_call x0 -> x2, Pallas kernels: none -> 1.77 us  [the longest x1 1.13 us: per_device(): kernel_call(fold_kernel, [shape((8, 3 * WIDTH), F32), shape((8, 3 * WIDTH...]
    ppermute x1, waiting for transfers between devices: 6.45 us -> 8.22 us  [per_device(): from_left = lax.ppermute(up, 'frames', forward)]
  transfers between devices with their start and end apart: 9 -> 8, of which waited for: 8 -> 7; matrix products, arithmetic and copies ran while one was open for 0% -> 0% of each run, Pallas kernels for 6% -> 5%
where the time goes in v5:
time: 138 us; the launch traced here: 137 us
  Pallas kernels  38.3 us (28%)
  waiting for transfers between devices  35.5 us (26%)
  starting transfers between devices  25.1 us (18%)
  blocking collectives  20.6 us (15%)
  local copies, waits for them, and re-layouts  16.1 us (12%)
  between operations  1.48 us (1%)
    all_to_all x1, blocking collectives, per_device(): contexts = lax.all_to_all(context, 'frames', 0, 0, tiled=True)  20.6 us
    all_to_all x1, waiting for transfers between devices, per_device(): pieces = lax.all_to_all(partial, 'frames', 0, 0, tiled=True)  20.3 us
    unnamed x46, local copies, waits for them, and re-layouts  16 us
    pallas_call x1, Pallas kernels, per_device(): kernel_call(attend_kernel, [shape((frames, 112, 128), BF16)], [SMEM, VMEM...  10.7 us
    pallas_call x1, Pallas kernels, per_device(): kernel_call(clean_kernel, [shape((ROWS, 1024), BF16), shape((ROWS, 1024),...  10.1 us
    all_to_all x1, starting transfers between devices, per_device(): recv = lax.all_to_all(msg, 'frames', 0, 0, tiled=True)  9.37 us
    ppermute x1, waiting for transfers between devices, per_device(): from_left = lax.ppermute(up, 'frames', forward)  8.22 us
    pallas_call x1, Pallas kernels, per_device(): kernel_call(patch_kernel, [shape((site_ids.shape[0], ROWS), F32)], [SMEM,...  7.34 us
  transfers between devices with their start and end apart: 8, of which 7 were waited for; matrix products, arithmetic and copies ran while one was open for 0% of the time, Pallas kernels for 5%

profile of v5, /device:TPU:10, one launch (start us, length us, event | category | flops | bytes accessed | tf_op | source)
XLA Modules:
  0.0 137.1 jit_solution(9820112251306587848)
XLA Ops:
  0.6 4.8 %shard_map.148 = (bf16[32,128,128]{2,1,0:T(8,128)(2,1)}, bf16[128,1024]{1,0:T(8,128)(2,1)}, bf16[64,1024]{1,0:T(8,128)(2,1)}, bf16[64,1024]{1,0:T(8,128)(2,1)}) custom-call(bf16[128,1024]{1,0:T(8,128)(2,1)} %bitcast.9, bf16[128,1024]{1,0:T(8,128)(2,1)} %bitcast.8, bf16[128,1024]{1,0:T(8,128)(2,1)} %bitcast.11, s32[1,128]{1,0:T(1,128)} %mask_ref.1, ...), custom_call_target="tpu_custom_call" | custom-call | flops 800000000 | bytes 6000000 | tf_op jit(solution)/shard_map/pallas_call | solution.py:683
  5.4 9.4 %all-to-all-start = ((bf16[32,128,128]{2,1,0:T(8,128)(2,1)}), bf16[32,128,128]{2,1,0:T(8,128)(2,1)S(1)}, u32[]{:S(2)}, u32[]{:S(2)}) async-start(bf16[32,128,128]{2,1,0:T(8,128)(2,1)} %get-tuple-element.25), calls=%async_computation | async-start | bytes 2097152 | tf_op jit(solution)/shard_map/all_to_all | solution.py:698
  14.8 3.4 %collective-permute-start = (bf16[64,1024]{1,0:T(8,128)(2,1)}, bf16[64,1024]{1,0:T(8,128)(2,1)S(1)}, u32[]{:S(2)}, u32[]{:S(2)}) collective-permute-start(bf16[64,1024]{1,0:T(8,128)(2,1)} %get-tuple-element.26), channel_id=1, source_target_pairs={{0,1},{1,2},{2,3},{3,4},{4,5},{5,6},{6,7},{7,8},{8,9},{9,10},{10,1... | collective-permute-start | bytes 393224 | tf_op jit(solution)/shard_map/ppermute | solution.py:696
  18.2 2.5 %collective-permute-start.1 = (bf16[64,1024]{1,0:T(8,128)(2,1)}, bf16[64,1024]{1,0:T(8,128)(2,1)S(1)}, u32[]{:S(2)}, u32[]{:S(2)}) collective-permute-start(bf16[64,1024]{1,0:T(8,128)(2,1)} %get-tuple-element.27), channel_id=1, source_target_pairs={{1,0},{2,1},{3,2},{4,3},{5,4},{6,5},{7,6},{8,7},{9,8},{10,9},{11,1... | collective-permute-start | bytes 393224 | tf_op jit(solution)/shard_map/ppermute | solution.py:697
  21.3 0.1 stack.19.scal_ref
  21.4 8.2 %collective-permute-done.up_hbm.up_ref = bf16[64,1024]{1,0:T(8,128)(2,1)S(1)} collective-permute-done((bf16[64,1024]{1,0:T(8,128)(2,1)}, bf16[64,1024]{1,0:T(8,128)(2,1)S(1)}, u32[]{:S(2)}, u32[]{:S(2)}) %collective-permute-start) | collective-permute-done | bytes 131104 | tf_op jit(solution)/shard_map/ppermute | solution.py:696
  29.6 0.9 collective-permute-done.1.down_hbm.down_ref
  30.5 0.1 all-to-all-done.recv_ref
  30.7 10.7 %shard_map.149 = bf16[32,112,128]{2,1,0:T(8,128)(2,1)S(1)} custom-call(s32[5]{0:T(128)S(1)} %stack.19.scal_ref, bf16[32,128,128]{2,1,0:T(8,128)(2,1)S(1)} %all-to-all-done.recv_ref), custom_call_target="tpu_custom_call" | custom-call | flops 8000000000 | bytes 1000000 | tf_op jit(solution)/shard_map/pallas_call | solution.py:701
  41.4 0.0 copy-done.17
  41.4 0.0 copy-done.12
  41.4 20.6 %all_to_all.15.ctx_hbm.ctx_in = bf16[32,112,128]{2,1,0:T(8,128)(2,1)} all-to-all(bf16[32,112,128]{2,1,0:T(8,128)(2,1)S(1)} %shard_map.149), channel_id=1, replica_groups=mesh['dp'=4,'frames'=32] {'frames'}, dimensions={0} | all-to-all | bytes 1835008 | tf_op jit(solution)/shard_map/all_to_all | solution.py:711
  62.0 10.1 %shard_map.150 = (bf16[128,1024]{1,0:T(8,128)(2,1)}, bf16[128,1024]{1,0:T(8,128)(2,1)}, bf16[128,2048]{1,0:T(8,128)(2,1)}, bf16[128,1024]{1,0:T(8,128)(2,1)}, bf...) custom-call(s32[5]{0:T(128)} %copy-done.17, ...), custom_call_target="tpu_custom_call" | custom-call | flops 3000000000 | bytes 10000000 | tf_op jit(solution)/shard_map/pallas_call | solution.py:712
  72.1 0.1 collective-permute-start.3
  72.2 0.5 collective-permute-start.2
  72.7 0.3 collective-permute-start.4
  73.0 1.7 %collective-permute-done.2.other_hbm = bf16[128,1024]{1,0:T(8,128)(2,1)S(1)} collective-permute-done((bf16[128,1024]{1,0:T(8,128)(2,1)}, bf16[128,1024]{1,0:T(8,128)(2,1)S(1)}, u32[]{:S(2)}, u32[]{:S(2)}) %collective-permute-start.2) | collective-permute-done | bytes 262176 | tf_op jit(solution)/shard_map/ppermute | solution.py:739
  74.7 0.4 collective-permute-done.4.go_other_hbm
  75.1 0.0 collective-permute-done.3.gm_other_hbm
  75.1 0.3 copy-done.21
  75.4 0.4 copy-done.22
  75.8 0.2 copy-done.20
  75.9 3.6 %shard_map.151 = bf16[32,16,3072]{2,1,0:T(8,128)(2,1)} custom-call(bf16[128,1024]{1,0:T(8,128)(2,1)} %get-tuple-element.31.own_hbm, bf16[128,1024]{1,0:T(8,128)(2,1)} %copy-done.21, bf16[128,2048]{1,0:T(8,128)(2,1)} %get-tuple-element.33.gm_hbm.gm_ref, bf16[128,2048]{1,0:T(8,128)(2,1)} %copy-done.20, bf16[128,1024]{1,0:T(8,128)(2,1)} %get-tuple-element.34.go_hbm.go_ref, ...), custom_call_target="tpu_custom_call" | custom-call | flops 800000000 | bytes 10000000 | tf_op jit(solution)/shard_map/pallas_call | solution.py:741
  79.6 0.0 copy-start.5
  79.6 0.0 copy-start.13
  79.6 0.0 copy-start.18
  79.6 0.0 copy-start.19
  79.6 6.7 %all-to-all-start.2 = ((bf16[32,16,3072]{2,1,0:T(8,128)(2,1)}), bf16[32,16,3072]{2,1,0:T(8,128)(2,1)S(1)}, u32[]{:S(2)}, u32[]{:S(2)}) async-start(bf16[32,16,3072]{2,1,0:T(8,128)(2,1)} %shard_map.151), calls=%async_computation.2 | async-start | bytes 6291456 | tf_op jit(solution)/shard_map/all_to_all | solution.py:750
  86.4 0.0 copy-start
  86.4 2.2 %copy-done = bf16[1024,2048]{1,0:T(8,128)(2,1)S(1)} copy-done((bf16[1024,2048]{1,0:T(8,128)(2,1)S(1)}, bf16[1024,2048]{1,0:T(8,128)(2,1)}, u32[]{:S(2)}) %copy-start) | copy-done | bytes 4194328
  88.5 1.2 copy-done.1
  89.7 1.0 copy-done.2
  90.8 1.6 %copy-done.3 = bf16[1024,1024]{1,0:T(8,128)(2,1)S(1)} copy-done((bf16[1024,1024]{1,0:T(8,128)(2,1)S(1)}, bf16[1024,1024]{1,0:T(8,128)(2,1)}, u32[]{:S(2)}) %copy-start.3) | copy-done | bytes 2097176
  92.4 1.2 copy-done.4
  93.6 1.1 copy-done.6
  94.7 1.1 copy-done.7
  95.8 1.0 copy-done.8
  96.8 1.0 copy-done.9
  97.8 1.0 copy-done.10
  98.8 0.9 copy-done.11
  99.8 0.9 copy-done.15
  100.7 0.8 copy-done.16
  101.5 7.3 %shard_map.152 = f32[8,128]{1,0:T(8,128)} custom-call(s32[5]{0:T(128)S(1)} %copy-done.18, s32[8]{0:T(128)S(1)} %copy-done.19, bf16[32,112,128]{2,1,0:T(8,128)(2,1)S(1)} %copy-done.1, bf16[128,1024]{1,0:T(8,128)(2,1)S(1)} %copy-done.11, bf16[64,1024]{1,0:T(8,128)(2,1)S(1)} %copy-done.13, bf16[64,1024]{1,0:T(8,128)(2,1)S(1)} %copy-done.15, ...), custom_call_target="tpu_custom_call" | custom-call | flops 3000000000 | bytes 10000000 | tf_op jit(solution)/shard_map/pallas_call | solution.py:751
  108.9 20.3 %all-to-all-done.2.pieces_ref = bf16[32,16,3072]{2,1,0:T(8,128)(2,1)S(1)} async-done(((bf16[32,16,3072]{2,1,0:T(8,128)(2,1)}), bf16[32,16,3072]{2,1,0:T(8,128)(2,1)S(1)}, u32[]{:S(2)}, u32[]{:S(2)}) %all-to-all-start.2) | async-done | bytes 3145760 | tf_op jit(solution)/shard_map/all_to_all | solution.py:750
  129.2 1.1 shard_map.153
  130.3 2.4 %collective-permute-start.5 = (f32[8,3072]{1,0:T(8,128)S(1)}, f32[8,3072]{1,0:T(8,128)S(1)}, u32[]{:S(2)}, u32[]{:S(2)}) collective-permute-start(f32[8,3072]{1,0:T(8,128)S(1)} %get-tuple-element.44), channel_id=1, source_target_pairs={{0,64},{32,96},{64,0},{96,32},{1,65},{33,97},{65,1},{97,33},{2,66}... | collective-permute-start | bytes 294920 | tf_op jit(solution)/shard_map/ppermute | solution.py:774
  132.7 3.8 %collective-permute-done.5.theirs_ref = f32[8,3072]{1,0:T(8,128)S(1)} collective-permute-done((f32[8,3072]{1,0:T(8,128)S(1)}, f32[8,3072]{1,0:T(8,128)S(1)}, u32[]{:S(2)}, u32[]{:S(2)}) %collective-permute-start.5) | collective-permute-done | bytes 98336 | tf_op jit(solution)/shard_map/ppermute | solution.py:774
  136.5 0.6 shard_map.154
  (23 shorter events, 0.0 us)
Async XLA Ops:
  5.4 25.2 %all-to-all-start = ((bf16[32,128,128]{2,1,0:T(8,128)(2,1)}), bf16[32,128,128]{2,1,0:T(8,128)(2,1)S(1)}, u32[]{:S(2)}, u32[]{:S(2)}) async-start(bf16[32,128,128]{2,1,0:T(8,128)(2,1)} %get-tuple-element.25), calls=%async_computation | async-start | bytes 2097152 | tf_op jit(solution)/shard_map/all_to_all | solution.py:698
  14.8 14.8 %collective-permute-start = (bf16[64,1024]{1,0:T(8,128)(2,1)}, bf16[64,1024]{1,0:T(8,128)(2,1)S(1)}, u32[]{:S(2)}, u32[]{:S(2)}) collective-permute-start(bf16[64,1024]{1,0:T(8,128)(2,1)} %get-tuple-element.26), channel_id=1, source_target_pairs={{0,1},{1,2},{2,3},{3,4},{4,5},{5,6},{6,7},{7,8},{8,9},{9,10},{10,1... | collective-permute-start | bytes 393224 | tf_op jit(solution)/shard_map/ppermute | solution.py:696
  18.2 12.3 %collective-permute-start.1 = (bf16[64,1024]{1,0:T(8,128)(2,1)}, bf16[64,1024]{1,0:T(8,128)(2,1)S(1)}, u32[]{:S(2)}, u32[]{:S(2)}) collective-permute-start(bf16[64,1024]{1,0:T(8,128)(2,1)} %get-tuple-element.27), channel_id=1, source_target_pairs={{1,0},{2,1},{3,2},{4,3},{5,4},{6,5},{7,6},{8,7},{9,8},{10,9},{11,1... | collective-permute-start | bytes 393224 | tf_op jit(solution)/shard_map/ppermute | solution.py:697
  21.4 20.0 %copy-start.17 = (s32[5]{0:T(128)}, s32[5]{0:T(128)S(1)}, u32[]{:S(2)}) copy-start(s32[5]{0:T(128)S(1)} %stack.19.scal_ref) | copy-start | bytes 64
  29.6 11.7 %copy-start.12 = (bf16[64,1024]{1,0:T(8,128)(2,1)}, bf16[64,1024]{1,0:T(8,128)(2,1)S(1)}, u32[]{:S(2)}) copy-start(bf16[64,1024]{1,0:T(8,128)(2,1)S(1)} %collective-permute-done.up_hbm.up_ref) | copy-start | bytes 393220
  30.5 10.9 %copy-start.14 = (bf16[64,1024]{1,0:T(8,128)(2,1)}, bf16[64,1024]{1,0:T(8,128)(2,1)S(1)}, u32[]{:S(2)}) copy-start(bf16[64,1024]{1,0:T(8,128)(2,1)S(1)} %collective-permute-done.1.down_hbm.down_ref) | copy-start | bytes 393220
  72.1 3.0 %collective-permute-start.3 = (bf16[128,2048]{1,0:T(8,128)(2,1)}, bf16[128,2048]{1,0:T(8,128)(2,1)S(1)}, u32[]{:S(2)}, u32[]{:S(2)}) collective-permute-start(bf16[128,2048]{1,0:T(8,128)(2,1)} %get-tuple-element.33.gm_hbm.gm_ref), channel_id=1, source_target_pairs={{0,32},{32,0},{64,96},{96,64},{1,33},{33,1},{65,97},{97,65},{2,34}... | collective-permute-start | bytes 1572872 | tf_op jit(solution)/shard_map/ppermute | solution.py:739
  72.2 2.5 %collective-permute-start.2 = (bf16[128,1024]{1,0:T(8,128)(2,1)}, bf16[128,1024]{1,0:T(8,128)(2,1)S(1)}, u32[]{:S(2)}, u32[]{:S(2)}) collective-permute-start(bf16[128,1024]{1,0:T(8,128)(2,1)} %get-tuple-element.32), channel_id=1, source_target_pairs={{0,32},{32,0},{64,96},{96,64},{1,33},{33,1},{65,97},{97,65},{2,34}... | collective-permute-start | bytes 786440 | tf_op jit(solution)/shard_map/ppermute | solution.py:739
  72.7 2.4 %collective-permute-start.4 = (bf16[128,1024]{1,0:T(8,128)(2,1)}, bf16[128,1024]{1,0:T(8,128)(2,1)S(1)}, u32[]{:S(2)}, u32[]{:S(2)}) collective-permute-start(bf16[128,1024]{1,0:T(8,128)(2,1)} %get-tuple-element.34.go_hbm.go_ref), channel_id=1, source_target_pairs={{0,32},{32,0},{64,96},{96,64},{1,33},{33,1},{65,97},{97,65},{2,34}... | collective-permute-start | bytes 786440 | tf_op jit(solution)/shard_map/ppermute | solution.py:739
  74.7 0.7 copy-start.21
  75.1 0.7 copy-start.22
  75.1 0.9 copy-start.20
  79.6 6.8 %copy-start.5 = (bf16[128,1024]{1,0:T(8,128)(2,1)S(1)}, bf16[128,1024]{1,0:T(8,128)(2,1)}, u32[]{:S(2)}) copy-start(bf16[128,1024]{1,0:T(8,128)(2,1)} %get-tuple-element.34.go_hbm.go_ref) | copy-start | bytes 786436
  79.6 6.8 %copy-start.13 = (bf16[64,1024]{1,0:T(8,128)(2,1)S(1)}, bf16[64,1024]{1,0:T(8,128)(2,1)}, u32[]{:S(2)}) copy-start(bf16[64,1024]{1,0:T(8,128)(2,1)} %copy-done.12) | copy-start | bytes 393220
  79.6 6.8 %copy-start.18 = (s32[5]{0:T(128)S(1)}, s32[5]{0:T(128)}, u32[]{:S(2)}) copy-start(s32[5]{0:T(128)} %copy-done.17) | copy-start | bytes 64
  79.6 6.8 %copy-start.19 = (s32[8]{0:T(128)S(1)}, s32[8]{0:T(128)}, u32[]{:S(2)}) copy-start(s32[8]{0:T(128)} %site_ref.1) | copy-start | bytes 100
  79.6 49.6 %all-to-all-start.2 = ((bf16[32,16,3072]{2,1,0:T(8,128)(2,1)}), bf16[32,16,3072]{2,1,0:T(8,128)(2,1)S(1)}, u32[]{:S(2)}, u32[]{:S(2)}) async-start(bf16[32,16,3072]{2,1,0:T(8,128)(2,1)} %shard_map.151), calls=%async_computation.2 | async-start | bytes 6291456 | tf_op jit(solution)/shard_map/all_to_all | solution.py:750
  86.4 2.2 %copy-start = (bf16[1024,2048]{1,0:T(8,128)(2,1)S(1)}, bf16[1024,2048]{1,0:T(8,128)(2,1)}, u32[]{:S(2)}) copy-start(bf16[1024,2048]{1,0:T(8,128)(2,1)} %win_ref.1) | copy-start | bytes 12582916
  88.5 1.2 copy-start.1
  89.7 1.0 copy-start.2
  90.8 1.6 %copy-start.3 = (bf16[1024,1024]{1,0:T(8,128)(2,1)S(1)}, bf16[1024,1024]{1,0:T(8,128)(2,1)}, u32[]{:S(2)}) copy-start(bf16[1024,1024]{1,0:T(8,128)(2,1)} %wout_ref.1) | copy-start | bytes 6291460
  92.4 1.2 copy-start.4
  93.6 1.1 copy-start.6
  94.7 1.1 copy-start.7
  95.8 1.0 copy-start.8
  96.8 1.0 copy-start.9
  97.8 1.0 copy-start.10
  98.8 0.9 copy-start.11
  99.8 0.9 copy-start.15
  100.7 0.8 copy-start.16
  130.3 6.2 %collective-permute-start.5 = (f32[8,3072]{1,0:T(8,128)S(1)}, f32[8,3072]{1,0:T(8,128)S(1)}, u32[]{:S(2)}, u32[]{:S(2)}) collective-permute-start(f32[8,3072]{1,0:T(8,128)S(1)} %get-tuple-element.44), channel_id=1, source_target_pairs={{0,64},{32,96},{64,0},{96,32},{1,65},{33,97},{65,1},{97,33},{2,66}... | collective-permute-start | bytes 294920 | tf_op jit(solution)/shard_map/ppermute | solution.py:774

commit v6 on v5

--- a/solution.py
+++ b/solution.py
@@ -20,6 +20,8 @@
 PATCH = ROWS + RIM
 BOTH = CLEAN + PATCH
 INNER = ROWS + RIM
+GM = WIDTH
+GO = 3 * WIDTH
 UNROLL = True
 TAP_UNROLL = 4
 LOAD_UNROLL = 4
@@ -153,7 +155,8 @@
         bias = jnp.where(frame < length, 0.0, FLOOR)
         keyed = jnp.where(lane < 64, kv, jnp.where(lane == 64, bias, 0.0))
         k_ref[pl.ds(at, 128), :] = keyed.astype(BF16)
-        vt_ref[:, pl.ds(at, 128)] = jnp.where(lane < 64, 1.0, kv).T.astype(BF16)
+        vt_ref[0:64, pl.ds(at, 128)] = kv.T[64:128].astype(BF16)
+        vt_ref[64:80, pl.ds(at, 128)] = jnp.ones((16, 128), BF16)
         raw = recv_ref[pl.ds(2 * s, 2), 64:128, :].astype(F32).reshape(128, 128).T
         fill = jnp.where(row == 64, 1.0, 0.0)
         other = jnp.concatenate([raw[64:], raw[:64]], axis=0)
@@ -191,8 +194,8 @@
     low8 = lane_of(8) < 64
 
     def store(b, accum, best):
-        total = accum[0:1, :]
-        result = accum[64:128, :] / total
+        total = accum[64:65, :]
+        result = accum[0:64, :] / total
         level = jnp.broadcast_to(best * scale + jnp.log2(total), (8, many))
         for g in range(many // 256):
             first = slice(g * 256, g * 256 + 128)
@@ -376,9 +379,9 @@
 def clean_kernel(
     scal_ref, ctx_hbm, clean_hbm, cot_hbm, up_hbm, down_hbm,
     wao_hbm, win_hbm, depth_hbm, wout_hbm,
-    own_out, send_out, gm_out, go_out, sw_out, gs_out, gg2_out, g2_out, resid_out,
+    own_out, pack_out, sw_out, gs_out, gg2_out, g2_out, resid_out,
     ctx_in, wao_ref, win_ref, depth_ref, wout_ref,
-    own_ref, send_ref, gm_ref, go_ref, sw_ref, gs_ref, gg2_ref, g2_ref, resid_ref,
+    own_ref, pack_ref, sw_ref, gs_ref, gg2_ref, g2_ref, resid_ref,
     ctx_ref, x_ref, low_ref, mv_ref, sg_ref, s2_ref, zed_ref, zinv_ref, gox_ref, gsp2_ref, taps_ref,
     in_sems, out_sems,
 ):
@@ -409,7 +412,11 @@
     results = [
         pltpu.make_async_copy(source, target, out_sems.at[i])
         for i, (source, target) in enumerate((
-            (own_ref, own_out), (send_ref, send_out), (gm_ref, gm_out), (go_ref, go_out),
+            (own_ref, own_out),
+            *(
+                (pack_ref.at[:, pl.ds(at, size)], pack_out.at[:, pl.ds(at, size)])
+                for at, size in ((0, WIDTH), (GM, 2 * WIDTH), (GO, WIDTH))
+            ),
             (sw_ref, sw_out), (gs_ref, gs_out), (gg2_ref, gg2_out), (g2_ref, g2_out),
             (resid_ref, resid_out),
         ))
@@ -424,7 +431,7 @@
         at = slice(row, row + 16)
         frame = first_frame - half + row + lax.broadcasted_iota(jnp.int32, (16, 1), 0)
         gox_ref[at, :] = (gox_ref[at, :].astype(F32) * jnp.where(frame < length, 1.0, 0.0)).astype(BF16)
-    go_ref[...] = gox_ref[half : half + ROWS, :]
+    pack_ref[:, GO:] = gox_ref[half : half + ROWS, :]
     go_copy.start()
 
     to_lowered(x_ref, ctx_ref, wao_ref, resid_ref, low_ref)
@@ -455,7 +462,7 @@
         first = source[row : row + ROWS, lo : lo + 256].astype(F32)
         second = source[row : row + ROWS, lo + 256 : lo + 512].astype(F32)
         own_ref[:, dest : dest + 256] = jnp.where(core == 0, first, second).astype(BF16)
-        send_ref[:, dest : dest + 256] = jnp.where(core == 0, second, first).astype(BF16)
+        pack_ref[:, dest : dest + 256] = jnp.where(core == 0, second, first).astype(BF16)
     own_copy.start()
     send_copy.start()
 
@@ -491,8 +498,8 @@
         frame = first_frame + r + lax.broadcasted_iota(jnp.int32, (16, 1), 0)
         grad = get_rows(gg2_ref, r, 16) * jnp.where(frame < length, 1.0, 0.0)
         gate = sg_ref[at, :]
-        gm_ref[at, 0:WIDTH] = (grad * gate).astype(BF16)
-        gm_ref[at, WIDTH:] = (grad * mv_ref[at, :] * gate * (1.0 - gate)).astype(BF16)
+        pack_ref[at, GM : GM + WIDTH] = (grad * gate).astype(BF16)
+        pack_ref[at, GM + WIDTH : GO] = (grad * mv_ref[at, :] * gate * (1.0 - gate)).astype(BF16)
         return carry
 
     lax.fori_loop(0, ROWS // 16, mixed_rows, 0, unroll=UNROLL)
@@ -505,7 +512,7 @@
 def patch_kernel(
     scal_ref, site_ref, ctx_in, patched_ref, up_ref, down_ref,
     wao_ref, win_ref, depth_ref, wout_ref,
-    gm_ref, go_ref, swc_ref, gs_ref, gg2_ref, g2c_ref, residc_ref,
+    pack_ref, swc_ref, gs_ref, gg2_ref, g2c_ref, residc_ref,
     attr_ref,
     ctx_ref, x_ref, resid_ref, low_ref, g2_ref, s2_ref, sw_ref, gl_ref, t0_ref, t1_ref, t2_ref, taps_ref,
 ):
@@ -547,10 +554,10 @@
         out_clean = residc_ref[RIM : RIM + ROWS, at].astype(F32) + out[:ROWS]
         out_patch = resid_ref[half : half + ROWS, at].astype(F32) + out[ROWS:]
         gap = out_patch.astype(BF16).astype(F32) - out_clean.astype(BF16).astype(F32)
-        t3 = t3 + lane_sum(gap * go_ref[:, at].astype(F32))
+        t3 = t3 + lane_sum(gap * pack_ref[:, GO + j * 256 : GO + j * 256 + 256].astype(F32))
     for j in range(4):
         at = slice(j * 256, j * 256 + 256)
-        gl_ref[:, at] = dot_nt(gm_ref[...], win_ref[at, :])
+        gl_ref[:, at] = dot_nt(pack_ref[:, GM:GO], win_ref[at, :])
 
     def resid_rows(i, carry):
         r = pl.multiple_of(i * 16, 16)
@@ -562,7 +569,7 @@
         grad = gl_ref[at, :]
         mean = jnp.mean(grad, axis=-1, keepdims=True)
         along = jnp.mean(grad * normed, axis=-1, keepdims=True)
-        grad_resid = go_ref[at, :].astype(F32) + (grad - mean - normed * along) * inverse
+        grad_resid = pack_ref[at, GO:].astype(F32) + (grad - mean - normed * along) * inverse
         t0_ref[at, :] = lane_sum((patch - clean) * grad_resid)
         return carry
 
@@ -583,12 +590,16 @@
 
 
 def weight_kernel(
-    own_hbm, other_hbm, gm_hbm, gm_other_hbm, go_hbm, go_other_hbm, out_hbm,
+    own_hbm, pack_hbm, other_hbm, out_hbm,
     left_ref, gm_ref, go_ref, out_ref, in_sems, out_sems,
 ):
     pairs = (
-        (own_hbm, left_ref, 0), (other_hbm, left_ref, ROWS), (go_hbm, go_ref, 0),
-        (go_other_hbm, go_ref, ROWS), (gm_hbm, gm_ref, 0), (gm_other_hbm, gm_ref, ROWS),
+        (own_hbm, left_ref, 0),
+        (other_hbm.at[:, pl.ds(0, WIDTH)], left_ref, ROWS),
+        (pack_hbm.at[:, pl.ds(GO, WIDTH)], go_ref, 0),
+        (other_hbm.at[:, pl.ds(GO, WIDTH)], go_ref, ROWS),
+        (pack_hbm.at[:, pl.ds(GM, 2 * WIDTH)], gm_ref, 0),
+        (other_hbm.at[:, pl.ds(GM, 2 * WIDTH)], gm_ref, ROWS),
     )
     copies = [
         pltpu.make_async_copy(source, target.at[pl.ds(row, ROWS)], in_sems.at[i])
@@ -628,21 +639,24 @@
 def fold_kernel(scal_ref, pieces_ref, mine_ref, theirs_ref):
     upper = scal_ref[4]
 
-    def columns(j, carry):
-        at = pl.ds(pl.multiple_of(j * 256, 256), 256)
+    def fold(at):
         total = pieces_ref[0, :, at].astype(F32)
         for k in range(1, pieces_ref.shape[0]):
             total = total + pieces_ref[k, :, at].astype(F32)
         first, second = total[:8], total[8:]
         mine_ref[:, at] = jnp.where(upper == 0, first, second)
-        theirs_ref[:, at] = jnp.where(upper == 0, second, first)
-        return carry
-
-    lax.fori_loop(0, mine_ref.shape[1] // 256, columns, 0, unroll=2)
+        return jnp.where(upper == 0, second, first)
+
+    middle = theirs_ref.shape[1]
+    for j in range(0, middle, 256):
+        low = fold(slice(j, j + 256))
+        high = fold(slice(middle + j, middle + j + 256))
+        theirs_ref[:, j : j + 256] = jnp.concatenate([low, high], axis=0).astype(BF16)
 
 
 def join_kernel(mine_ref, theirs_ref, in_ref, out_ref):
-    whole = mine_ref[...] + theirs_ref[...]
+    theirs = theirs_ref[...].astype(F32)
+    whole = mine_ref[...] + jnp.concatenate([theirs[:8], theirs[8:]], axis=1)
     in_ref[...] = whole[:, : 2 * WIDTH]
     out_ref[...] = whole[:, 2 * WIDTH :]
 
@@ -702,24 +716,23 @@
         attend_kernel,
         [shape((frames, 112, 128), BF16)],
         [SMEM, VMEM],
-        [pltpu.VMEM((keys, 128), BF16), pltpu.VMEM((128, keys), BF16),
+        [pltpu.VMEM((keys, 128), BF16), pltpu.VMEM((80, keys), BF16),
          pltpu.VMEM((128, 2 * keys), BF16),
          pltpu.VMEM((keys, 512), F32), pltpu.VMEM((keys, 512), F32),
          pltpu.VMEM((frames * 64, 128), F32), pltpu.VMEM((frames * 8, 128), F32)],
         20, 8 * 10**9, 10**6,
     )(scalars, recv)
     contexts = lax.all_to_all(context, "frames", 0, 0, tiled=True)
-    own, send, grad_mixed, grad_output, swished, grad_swished, grad_gated, gated, resid = kernel_call(
+    own, pack, swished, grad_swished, grad_gated, gated, resid = kernel_call(
         clean_kernel,
-        [shape((ROWS, 1024), BF16), shape((ROWS, 1024), BF16), shape((ROWS, 2 * WIDTH), BF16),
-         shape((ROWS, WIDTH), BF16), shape((INNER, WIDTH), BF16), shape((INNER, WIDTH), F32),
+        [shape((ROWS, WIDTH), BF16), shape((ROWS, 4 * WIDTH), BF16),
+         shape((INNER, WIDTH), BF16), shape((INNER, WIDTH), F32),
          shape((ROWS * 8, 128), F32), shape((CLEAN * 8, 128), F32), shape((CLEAN, WIDTH), BF16)],
         [SMEM] + [HBM] * 9,
         [pltpu.VMEM((16, 112, 128), BF16), pltpu.VMEM((512, WIDTH), BF16),
          pltpu.VMEM((WIDTH, 2 * WIDTH), BF16), pltpu.VMEM((KERNEL, WIDTH), BF16),
          pltpu.VMEM((WIDTH, WIDTH), BF16),
-         pltpu.VMEM((ROWS, 1024), BF16), pltpu.VMEM((ROWS, 1024), BF16),
-         pltpu.VMEM((ROWS, 2 * WIDTH), BF16), pltpu.VMEM((ROWS, WIDTH), BF16),
+         pltpu.VMEM((ROWS, WIDTH), BF16), pltpu.VMEM((ROWS, 4 * WIDTH), BF16),
          pltpu.VMEM((INNER, WIDTH), BF16), pltpu.VMEM((INNER, WIDTH), F32),
          pltpu.VMEM((ROWS * 8, 128), F32), pltpu.VMEM((CLEAN * 8, 128), F32),
          pltpu.VMEM((CLEAN, WIDTH), BF16),
@@ -735,23 +748,21 @@
       w_attn_out, w_pointwise_in, depth_kernel, w_pointwise_out)
 
     cores = [(i, i ^ 1) for i in range(lax.axis_size("dp"))]
-    other, gm_other, go_other = (
-        lax.ppermute(part, "dp", cores) for part in (send, grad_mixed, grad_output)
-    )
+    other = lax.ppermute(pack, "dp", cores)
     (partial,) = kernel_call(
         weight_kernel,
         [shape((frames, 16, 3 * WIDTH), BF16)],
-        [HBM] * 6,
+        [HBM] * 3,
         [pltpu.VMEM((2 * ROWS, WIDTH), BF16), pltpu.VMEM((2 * ROWS, 2 * WIDTH), BF16),
          pltpu.VMEM((2 * ROWS, WIDTH), BF16), pltpu.VMEM((frames, 16, 3 * WIDTH), BF16),
          pltpu.SemaphoreType.DMA((6,)), pltpu.SemaphoreType.DMA((3,))],
         59, 8 * 10**8, 10**7, HBM,
-    )(own, other, grad_mixed, gm_other, grad_output, go_other)
+    )(own, pack, other)
     pieces = lax.all_to_all(partial, "frames", 0, 0, tiled=True)
     (attribution,) = kernel_call(
         patch_kernel,
         [shape((site_ids.shape[0], ROWS), F32)],
-        [SMEM, SMEM] + [VMEM] * 15,
+        [SMEM, SMEM] + [VMEM] * 14,
         [pltpu.VMEM((PATCH, 512), BF16), pltpu.VMEM((PATCH, WIDTH), BF16),
          pltpu.VMEM((PATCH, WIDTH), BF16), pltpu.VMEM((PATCH, WIDTH), BF16),
          pltpu.VMEM((PATCH * 8, 128), F32), pltpu.VMEM((ROWS * 8, 128), F32),
@@ -761,11 +772,11 @@
         28, 3 * 10**9, 10**7,
     )(scalars, site_ids, contexts, patched, from_left, from_right,
       w_attn_out, w_pointwise_in, depth_kernel, w_pointwise_out,
-      grad_mixed, grad_output, swished, grad_swished, grad_gated, gated, resid)
+      pack, swished, grad_swished, grad_gated, gated, resid)
     pieces, attribution = lax.optimization_barrier((pieces, attribution))
     mine, theirs = kernel_call(
         fold_kernel,
-        [shape((8, 3 * WIDTH), F32), shape((8, 3 * WIDTH), F32)],
+        [shape((8, 3 * WIDTH), F32), shape((16, 3 * WIDTH // 2), BF16)],
         [SMEM, VMEM],
         [],
         16, 10**8, 3 * 10**6,

time: 138 us -> 137 us (level)
    ppermute x3 -> x1, waiting for transfers between devices: 2.09 us -> 2.86 us  [per_device(): other = lax.ppermute(pack, 'dp', cores)]
    unnamed x46 -> x40, local copies, waits for them, and re-layouts: 16 us -> 16.3 us
  transfers between devices with their start and end apart: 8 -> 6, of which waited for: 7 -> 6; matrix products, arithmetic and copies ran while one was open for 0% -> 0% of each run, Pallas kernels for 5% -> 5%
where the time goes in v6:
time: 137 us; the launch traced here: 136 us
  Pallas kernels  37.5 us (27%)
  waiting for transfers between devices  35.7 us (26%)
  starting transfers between devices  24.6 us (18%)
  blocking collectives  20.6 us (15%)
  local copies, waits for them, and re-layouts  16.4 us (12%)
  between operations  1.46 us (1%)
    all_to_all x1, blocking collectives, per_device(): contexts = lax.all_to_all(context, 'frames', 0, 0, tiled=True)  20.6 us
    all_to_all x1, waiting for transfers between devices, per_device(): pieces = lax.all_to_all(partial, 'frames', 0, 0, tiled=True)  20.3 us
    unnamed x40, local copies, waits for them, and re-layouts  16.3 us
    pallas_call x1, Pallas kernels, per_device(): kernel_call(clean_kernel, [shape((ROWS, WIDTH), BF16), shape((ROWS, 4 * W...  10.1 us
    pallas_call x1, Pallas kernels, per_device(): kernel_call(attend_kernel, [shape((frames, 112, 128), BF16)], [SMEM, VMEM...  10.1 us
    all_to_all x1, starting transfers between devices, per_device(): recv = lax.all_to_all(msg, 'frames', 0, 0, tiled=True)  9.37 us
    ppermute x1, waiting for transfers between devices, per_device(): from_left = lax.ppermute(up, 'frames', forward)  8.22 us
    pallas_call x1, Pallas kernels, per_device(): kernel_call(patch_kernel, [shape((site_ids.shape[0], ROWS), F32)], [SMEM,...  7.33 us
  transfers between devices with their start and end apart: 6, of which 6 were waited for; matrix products, arithmetic and copies ran while one was open for 0% of the time, Pallas kernels for 5%

profile of v6, /device:TPU:10, one launch (start us, length us, event | category | flops | bytes accessed | tf_op | source)
XLA Modules:
  0.0 136.1 jit_solution(12152142926938935642)
XLA Ops:
  0.6 4.8 %shard_map.148 = (bf16[32,128,128]{2,1,0:T(8,128)(2,1)}, bf16[128,1024]{1,0:T(8,128)(2,1)}, bf16[64,1024]{1,0:T(8,128)(2,1)}, bf16[64,1024]{1,0:T(8,128)(2,1)}) custom-call(bf16[128,1024]{1,0:T(8,128)(2,1)} %bitcast.9, bf16[128,1024]{1,0:T(8,128)(2,1)} %bitcast.8, bf16[128,1024]{1,0:T(8,128)(2,1)} %bitcast.11, s32[1,128]{1,0:T(1,128)} %mask_ref.1, ...), custom_call_target="tpu_custom_call" | custom-call | flops 800000000 | bytes 6000000 | tf_op jit(solution)/shard_map/pallas_call | solution.py:697
  5.4 9.4 %all-to-all-start = ((bf16[32,128,128]{2,1,0:T(8,128)(2,1)}), bf16[32,128,128]{2,1,0:T(8,128)(2,1)S(1)}, u32[]{:S(2)}, u32[]{:S(2)}) async-start(bf16[32,128,128]{2,1,0:T(8,128)(2,1)} %get-tuple-element.23), calls=%async_computation | async-start | bytes 2097152 | tf_op jit(solution)/shard_map/all_to_all | solution.py:712
  14.8 3.4 %collective-permute-start = (bf16[64,1024]{1,0:T(8,128)(2,1)}, bf16[64,1024]{1,0:T(8,128)(2,1)S(1)}, u32[]{:S(2)}, u32[]{:S(2)}) collective-permute-start(bf16[64,1024]{1,0:T(8,128)(2,1)} %get-tuple-element.24), channel_id=1, source_target_pairs={{0,1},{1,2},{2,3},{3,4},{4,5},{5,6},{6,7},{7,8},{8,9},{9,10},{10,1... | collective-permute-start | bytes 393224 | tf_op jit(solution)/shard_map/ppermute | solution.py:710
  18.2 2.5 %collective-permute-start.1 = (bf16[64,1024]{1,0:T(8,128)(2,1)}, bf16[64,1024]{1,0:T(8,128)(2,1)S(1)}, u32[]{:S(2)}, u32[]{:S(2)}) collective-permute-start(bf16[64,1024]{1,0:T(8,128)(2,1)} %get-tuple-element.25), channel_id=1, source_target_pairs={{1,0},{2,1},{3,2},{4,3},{5,4},{6,5},{7,6},{8,7},{9,8},{10,9},{11,1... | collective-permute-start | bytes 393224 | tf_op jit(solution)/shard_map/ppermute | solution.py:711
  21.3 0.1 stack.19.scal_ref
  21.4 0.0 copy-start.16
  21.4 8.2 %collective-permute-done.up_hbm.up_ref = bf16[64,1024]{1,0:T(8,128)(2,1)S(1)} collective-permute-done((bf16[64,1024]{1,0:T(8,128)(2,1)}, bf16[64,1024]{1,0:T(8,128)(2,1)S(1)}, u32[]{:S(2)}, u32[]{:S(2)}) %collective-permute-start) | collective-permute-done | bytes 131104 | tf_op jit(solution)/shard_map/ppermute | solution.py:710
  29.6 0.0 copy-start.11
  29.6 0.9 collective-permute-done.1.down_hbm.down_ref
  30.5 0.1 all-to-all-done.recv_ref
  30.7 10.1 %shard_map.149 = bf16[32,112,128]{2,1,0:T(8,128)(2,1)S(1)} custom-call(s32[5]{0:T(128)S(1)} %stack.19.scal_ref, bf16[32,128,128]{2,1,0:T(8,128)(2,1)S(1)} %all-to-all-done.recv_ref), custom_call_target="tpu_custom_call" | custom-call | flops 8000000000 | bytes 1000000 | tf_op jit(solution)/shard_map/pallas_call | solution.py:715
  40.8 0.0 copy-done.16
  40.8 0.0 copy-done.11
  40.8 0.0 copy-done.13
  40.8 20.6 %all_to_all.15.ctx_hbm.ctx_in = bf16[32,112,128]{2,1,0:T(8,128)(2,1)} all-to-all(bf16[32,112,128]{2,1,0:T(8,128)(2,1)S(1)} %shard_map.149), channel_id=1, replica_groups=mesh['dp'=4,'frames'=32] {'frames'}, dimensions={0} | all-to-all | bytes 1835008 | tf_op jit(solution)/shard_map/all_to_all | solution.py:725
  61.4 10.1 %shard_map.150 = (bf16[128,1024]{1,0:T(8,128)(2,1)}, bf16[128,4096]{1,0:T(8,128)(2,1)}, bf16[160,1024]{1,0:T(8,128)(2,1)}, f32[160,1024]{1,0:T(8,128)}, f32[1024...) custom-call(s32[5]{0:T(128)} %copy-done.16, bf16[32,112,128]{2,1,0:T(8,128)(2,1)} %all_to_all.15.ctx_hbm.ctx_in, ...), custom_call_target="tpu_custom_call" | custom-call | flops 3000000000 | bytes 10000000 | tf_op jit(solution)/shard_map/pallas_call | solution.py:726
  71.5 0.3 collective-permute-start.2
  71.8 2.9 %collective-permute-done.2.other_hbm = bf16[128,4096]{1,0:T(8,128)(2,1)S(1)} collective-permute-done((bf16[128,4096]{1,0:T(8,128)(2,1)}, bf16[128,4096]{1,0:T(8,128)(2,1)S(1)}, u32[]{:S(2)}, u32[]{:S(2)}) %collective-permute-start.2) | collective-permute-done | bytes 1048608 | tf_op jit(solution)/shard_map/ppermute | solution.py:751
  74.6 0.0 copy-start.19
  74.6 1.0 copy-done.19
  75.6 3.5 %shard_map.151 = bf16[32,16,3072]{2,1,0:T(8,128)(2,1)} custom-call(bf16[128,1024]{1,0:T(8,128)(2,1)} %get-tuple-element.29.own_hbm, bf16[128,4096]{1,0:T(8,128)(2,1)} %get-tuple-element.30.pack_hbm.pack_ref, bf16[128,4096]{1,0:T(8,128)(2,1)} %copy-done.19), custom_call_target="tpu_custom_call" | custom-call | flops 800000000 | bytes 10000000 | tf_op jit(solution)/shard_map/pallas_call | solution.py:752
  79.2 0.0 copy-start.8
  79.2 0.0 copy-start.17
  79.2 0.0 copy-start.18
  79.2 6.7 %all-to-all-start.2 = ((bf16[32,16,3072]{2,1,0:T(8,128)(2,1)}), bf16[32,16,3072]{2,1,0:T(8,128)(2,1)S(1)}, u32[]{:S(2)}, u32[]{:S(2)}) async-start(bf16[32,16,3072]{2,1,0:T(8,128)(2,1)} %shard_map.151), calls=%async_computation.2 | async-start | bytes 6291456 | tf_op jit(solution)/shard_map/all_to_all | solution.py:761
  85.9 0.0 copy-done.8
  85.9 0.0 copy-done.17
  86.0 0.0 copy-done.18
  86.0 0.0 copy-start
  86.0 2.2 %copy-done = bf16[1024,2048]{1,0:T(8,128)(2,1)S(1)} copy-done((bf16[1024,2048]{1,0:T(8,128)(2,1)S(1)}, bf16[1024,2048]{1,0:T(8,128)(2,1)}, u32[]{:S(2)}) %copy-start) | copy-done | bytes 4194328
  88.2 1.2 copy-done.1
  89.4 1.2 copy-done.2
  90.6 1.6 %copy-done.3 = bf16[1024,1024]{1,0:T(8,128)(2,1)S(1)} copy-done((bf16[1024,1024]{1,0:T(8,128)(2,1)S(1)}, bf16[1024,1024]{1,0:T(8,128)(2,1)}, u32[]{:S(2)}) %copy-start.3) | copy-done | bytes 2097176
  92.2 1.2 copy-done.4
  93.4 1.1 copy-done.5
  94.5 1.1 copy-done.6
  95.6 1.0 copy-done.7
  96.6 1.0 copy-done.9
  97.6 0.9 copy-done.10
  98.6 0.9 copy-done.12
  99.5 0.9 copy-done.14
  100.4 0.8 copy-done.15
  101.2 7.3 %shard_map.152 = f32[8,128]{1,0:T(8,128)} custom-call(s32[5]{0:T(128)S(1)} %copy-done.17, s32[8]{0:T(128)S(1)} %copy-done.18, bf16[32,112,128]{2,1,0:T(8,128)(2,1)S(1)} %copy-done.2, bf16[128,1024]{1,0:T(8,128)(2,1)S(1)} %copy-done.10, bf16[64,1024]{1,0:T(8,128)(2,1)S(1)} %copy-done.12, bf16[64,1024]{1,0:T(8,128)(2,1)S(1)} %copy-done.14, ...), custom_call_target="tpu_custom_call" | custom-call | flops 3000000000 | bytes 10000000 | tf_op jit(solution)/shard_map/pallas_call | solution.py:762
  108.5 20.3 %all-to-all-done.2.pieces_ref = bf16[32,16,3072]{2,1,0:T(8,128)(2,1)S(1)} async-done(((bf16[32,16,3072]{2,1,0:T(8,128)(2,1)}), bf16[32,16,3072]{2,1,0:T(8,128)(2,1)S(1)}, u32[]{:S(2)}, u32[]{:S(2)}) %all-to-all-start.2) | async-done | bytes 3145760 | tf_op jit(solution)/shard_map/all_to_all | solution.py:761
  128.8 1.0 shard_map.153
  129.8 2.4 %collective-permute-start.3 = (bf16[16,1536]{1,0:T(8,128)(2,1)S(1)}, bf16[16,1536]{1,0:T(8,128)(2,1)S(1)}, u32[]{:S(2)}, u32[]{:S(2)}) collective-permute-start(bf16[16,1536]{1,0:T(8,128)(2,1)S(1)} %get-tuple-element.40), channel_id=1, source_target_pairs={{0,64},{32,96},{64,0},{96,32},{1,65},{33,97},{65,1},{97,33},{2,66}... | collective-permute-start | bytes 147464 | tf_op jit(solution)/shard_map/ppermute | solution.py:785
  132.2 3.3 %collective-permute-done.3.theirs_ref = bf16[16,1536]{1,0:T(8,128)(2,1)S(1)} collective-permute-done((bf16[16,1536]{1,0:T(8,128)(2,1)S(1)}, bf16[16,1536]{1,0:T(8,128)(2,1)S(1)}, u32[]{:S(2)}, u32[]{:S(2)}) %collective-permute-start.3) | collective-permute-done | bytes 49184 | tf_op jit(solution)/shard_map/ppermute | solution.py:785
  135.5 0.6 shard_map.154
  (13 shorter events, 0.0 us)
Async XLA Ops:
  5.4 25.2 %all-to-all-start = ((bf16[32,128,128]{2,1,0:T(8,128)(2,1)}), bf16[32,128,128]{2,1,0:T(8,128)(2,1)S(1)}, u32[]{:S(2)}, u32[]{:S(2)}) async-start(bf16[32,128,128]{2,1,0:T(8,128)(2,1)} %get-tuple-element.23), calls=%async_computation | async-start | bytes 2097152 | tf_op jit(solution)/shard_map/all_to_all | solution.py:712
  14.8 14.8 %collective-permute-start = (bf16[64,1024]{1,0:T(8,128)(2,1)}, bf16[64,1024]{1,0:T(8,128)(2,1)S(1)}, u32[]{:S(2)}, u32[]{:S(2)}) collective-permute-start(bf16[64,1024]{1,0:T(8,128)(2,1)} %get-tuple-element.24), channel_id=1, source_target_pairs={{0,1},{1,2},{2,3},{3,4},{4,5},{5,6},{6,7},{7,8},{8,9},{9,10},{10,1... | collective-permute-start | bytes 393224 | tf_op jit(solution)/shard_map/ppermute | solution.py:710
  18.2 12.3 %collective-permute-start.1 = (bf16[64,1024]{1,0:T(8,128)(2,1)}, bf16[64,1024]{1,0:T(8,128)(2,1)S(1)}, u32[]{:S(2)}, u32[]{:S(2)}) collective-permute-start(bf16[64,1024]{1,0:T(8,128)(2,1)} %get-tuple-element.25), channel_id=1, source_target_pairs={{1,0},{2,1},{3,2},{4,3},{5,4},{6,5},{7,6},{8,7},{9,8},{10,9},{11,1... | collective-permute-start | bytes 393224 | tf_op jit(solution)/shard_map/ppermute | solution.py:711
  21.4 19.3 %copy-start.16 = (s32[5]{0:T(128)}, s32[5]{0:T(128)S(1)}, u32[]{:S(2)}) copy-start(s32[5]{0:T(128)S(1)} %stack.19.scal_ref) | copy-start | bytes 64
  29.6 11.1 %copy-start.11 = (bf16[64,1024]{1,0:T(8,128)(2,1)}, bf16[64,1024]{1,0:T(8,128)(2,1)S(1)}, u32[]{:S(2)}) copy-start(bf16[64,1024]{1,0:T(8,128)(2,1)S(1)} %collective-permute-done.up_hbm.up_ref) | copy-start | bytes 393220
  30.5 10.2 %copy-start.13 = (bf16[64,1024]{1,0:T(8,128)(2,1)}, bf16[64,1024]{1,0:T(8,128)(2,1)S(1)}, u32[]{:S(2)}) copy-start(bf16[64,1024]{1,0:T(8,128)(2,1)S(1)} %collective-permute-done.1.down_hbm.down_ref) | copy-start | bytes 393220
  71.5 3.1 %collective-permute-start.2 = (bf16[128,4096]{1,0:T(8,128)(2,1)}, bf16[128,4096]{1,0:T(8,128)(2,1)S(1)}, u32[]{:S(2)}, u32[]{:S(2)}) collective-permute-start(bf16[128,4096]{1,0:T(8,128)(2,1)} %get-tuple-element.30.pack_hbm.pack_ref), channel_id=1, source_target_pairs={{0,32},{32,0},{64,96},{96,64},{1,33},{33,1},{65,97},{97,65},{2,34}... | collective-permute-start | bytes 3145736 | tf_op jit(solution)/shard_map/ppermute | solution.py:751
  74.6 1.0 copy-start.19
  79.2 6.7 %copy-start.8 = (bf16[192,1024]{1,0:T(8,128)(2,1)S(1)}, bf16[192,1024]{1,0:T(8,128)(2,1)}, u32[]{:S(2)}) copy-start(bf16[192,1024]{1,0:T(8,128)(2,1)} %get-tuple-element.36.residc_ref) | copy-start | bytes 1179652
  79.2 6.7 %copy-start.17 = (s32[5]{0:T(128)S(1)}, s32[5]{0:T(128)}, u32[]{:S(2)}) copy-start(s32[5]{0:T(128)} %copy-done.16) | copy-start | bytes 64
  79.2 6.7 %copy-start.18 = (s32[8]{0:T(128)S(1)}, s32[8]{0:T(128)}, u32[]{:S(2)}) copy-start(s32[8]{0:T(128)} %site_ref.1) | copy-start | bytes 100
  79.2 49.6 %all-to-all-start.2 = ((bf16[32,16,3072]{2,1,0:T(8,128)(2,1)}), bf16[32,16,3072]{2,1,0:T(8,128)(2,1)S(1)}, u32[]{:S(2)}, u32[]{:S(2)}) async-start(bf16[32,16,3072]{2,1,0:T(8,128)(2,1)} %shard_map.151), calls=%async_computation.2 | async-start | bytes 6291456 | tf_op jit(solution)/shard_map/all_to_all | solution.py:761
  86.0 2.2 %copy-start = (bf16[1024,2048]{1,0:T(8,128)(2,1)S(1)}, bf16[1024,2048]{1,0:T(8,128)(2,1)}, u32[]{:S(2)}) copy-start(bf16[1024,2048]{1,0:T(8,128)(2,1)} %win_ref.1) | copy-start | bytes 12582916
  88.2 1.2 copy-start.1
  89.4 1.2 copy-start.2
  90.6 1.6 %copy-start.3 = (bf16[1024,1024]{1,0:T(8,128)(2,1)S(1)}, bf16[1024,1024]{1,0:T(8,128)(2,1)}, u32[]{:S(2)}) copy-start(bf16[1024,1024]{1,0:T(8,128)(2,1)} %wout_ref.1) | copy-start | bytes 6291460
  92.2 1.2 copy-start.4
  93.4 1.1 copy-start.5
  94.5 1.1 copy-start.6
  95.6 1.0 copy-start.7
  96.6 1.0 copy-start.9
  97.6 0.9 copy-start.10
  98.6 0.9 copy-start.12
  99.5 0.9 copy-start.14
  100.4 0.8 copy-start.15
  129.8 5.7 %collective-permute-start.3 = (bf16[16,1536]{1,0:T(8,128)(2,1)S(1)}, bf16[16,1536]{1,0:T(8,128)(2,1)S(1)}, u32[]{:S(2)}, u32[]{:S(2)}) collective-permute-start(bf16[16,1536]{1,0:T(8,128)(2,1)S(1)} %get-tuple-element.40), channel_id=1, source_target_pairs={{0,64},{32,96},{64,0},{96,32},{1,65},{33,97},{65,1},{97,33},{2,66}... | collective-permute-start | bytes 147464 | tf_op jit(solution)/shard_map/ppermute | solution.py:785

commit v7 on v6

--- a/solution.py
+++ b/solution.py
@@ -57,7 +57,7 @@
 
 
 def sigmoid(values):
-    return 1.0 / (1.0 + jnp.exp(-values))
+    return 0.5 * jnp.tanh(0.5 * values) + 0.5
 
 
 def lane_sum(values):
@@ -69,8 +69,9 @@
 
 def project_kernel(
     clean_hbm, corrupt_hbm, cot_hbm, mask_ref, wq_hbm, wk_hbm, wv_hbm,
+    msg_out, patched_out, up_out, down_out,
     msg_ref, patched_ref, up_ref, down_ref,
-    hidden_ref, mask_col, clean_ref, corrupt_ref, wq_ref, wk_ref, wv_ref, sems,
+    hidden_ref, mask_col, clean_ref, corrupt_ref, wq_ref, wk_ref, wv_ref, sems, out_sems,
 ):
     half = RIM // 2
     copies = [
@@ -111,6 +112,18 @@
     down_ref[RIM : RIM + half, :] = patched_ref[0:half, :]
     for copy in copies[2:]:
         copy.wait()
+    results = [
+        pltpu.make_async_copy(source, target, out_sems.at[i])
+        for i, (source, target) in enumerate((
+            (up_ref, up_out), (down_ref, down_out), (patched_ref, patched_out),
+            *(
+                (msg_ref.at[pl.ds(at, 8)], msg_out.at[pl.ds(at, 8)])
+                for at in (0, 16, 8, 24)
+            ),
+        ))
+    ]
+    for copy in results[:3]:
+        copy.start()
 
     low = lane_of(ROWS) < 64
     low_q = lane_of(64) < 64
@@ -137,6 +150,10 @@
                         dest = base + odd * 2 + side
                         msg_ref[dest, 0:64, :] = kv[odd][side * 64 : side * 64 + 64]
                         msg_ref[dest, 64:128, :] = asked[odd]
+        results[3 + 2 * pair].start()
+        results[4 + 2 * pair].start()
+    for copy in results:
+        copy.wait()
 
 
 def attend_kernel(
@@ -609,7 +626,7 @@
         copy.start()
 
     def send(i):
-        at = pl.ds(i * WIDTH, WIDTH)
+        at = pl.ds(i * 512, 512)
         return pltpu.make_async_copy(out_ref.at[:, :, at], out_hbm.at[:, :, at], out_sems.at[i])
 
     def put(at, product):
@@ -620,19 +637,19 @@
 
     for copy in copies[:4]:
         copy.wait()
-    swished = left_ref[:, 512:1024].T
+    swished = left_ref[:, WIDTH // 2 :].T
     for j in range(0, WIDTH, 256):
         put(2 * WIDTH + j, dot(swished, go_ref[:, j : j + 256]))
-    send(2).start()
+        if j % 512:
+            send(4 + j // 512).start()
     for copy in copies[4:]:
         copy.wait()
-    low = left_ref[:, 0:512].T
+    low = left_ref[:, : WIDTH // 2].T
     for j in range(0, 2 * WIDTH, 256):
         put(j, dot(low, gm_ref[:, j : j + 256]))
-        if j + 256 == WIDTH:
-            send(0).start()
-    send(1).start()
-    for i in range(3):
+        if j % 512:
+            send(j // 512).start()
+    for i in range(6):
         send(i).wait()
 
 
@@ -699,11 +716,13 @@
         [shape((frames, ROWS, 128), BF16), shape((ROWS, WIDTH), BF16),
          shape((2 * RIM, WIDTH), BF16), shape((2 * RIM, WIDTH), BF16)],
         [HBM] * 3 + [VMEM] + [HBM] * 3,
-        [pltpu.VMEM((2 * ROWS, WIDTH), BF16), pltpu.VMEM((ROWS, ROWS), F32),
+        [pltpu.VMEM((frames, ROWS, 128), BF16), pltpu.VMEM((ROWS, WIDTH), BF16),
+         pltpu.VMEM((2 * RIM, WIDTH), BF16), pltpu.VMEM((2 * RIM, WIDTH), BF16),
+         pltpu.VMEM((2 * ROWS, WIDTH), BF16), pltpu.VMEM((ROWS, ROWS), F32),
          pltpu.VMEM((ROWS, WIDTH), BF16), pltpu.VMEM((ROWS, WIDTH), BF16),
          pltpu.VMEM((WIDTH, 512), BF16), pltpu.VMEM((WIDTH, 512), BF16),
-         pltpu.VMEM((WIDTH, 512), BF16), pltpu.SemaphoreType.DMA((7,))],
-        62, 8 * 10**8, 6 * 10**6,
+         pltpu.VMEM((WIDTH, 512), BF16), pltpu.SemaphoreType.DMA((7,)), pltpu.SemaphoreType.DMA((7,))],
+        62, 8 * 10**8, 6 * 10**6, HBM,
     )(clean, corrupt, cot, patch_mask, w_query, w_key, w_value)
     forward = [(i, i + 1) for i in range(frames - 1)]
     backward = [(i + 1, i) for i in range(frames - 1)]
@@ -755,7 +774,7 @@
         [HBM] * 3,
         [pltpu.VMEM((2 * ROWS, WIDTH), BF16), pltpu.VMEM((2 * ROWS, 2 * WIDTH), BF16),
          pltpu.VMEM((2 * ROWS, WIDTH), BF16), pltpu.VMEM((frames, 16, 3 * WIDTH), BF16),
-         pltpu.SemaphoreType.DMA((6,)), pltpu.SemaphoreType.DMA((3,))],
+         pltpu.SemaphoreType.DMA((6,)), pltpu.SemaphoreType.DMA((6,))],
         59, 8 * 10**8, 10**7, HBM,
     )(own, pack, other)
     pieces = lax.all_to_all(partial, "frames", 0, 0, tiled=True)

time: 137 us -> 137 us (level)
  no operation moved by 1% of the time
where the time goes in v7:
time: 137 us; the launch traced here: 136 us
  Pallas kernels  37.1 us (27%)
  waiting for transfers between devices  35.6 us (26%)
  starting transfers between devices  24.6 us (18%)
  blocking collectives  20.6 us (15%)
  local copies, waits for them, and re-layouts  16.4 us (12%)
  between operations  1.46 us (1%)
    all_to_all x1, blocking collectives, per_device(): contexts = lax.all_to_all(context, 'frames', 0, 0, tiled=True)  20.6 us
    all_to_all x1, waiting for transfers between devices, per_device(): pieces = lax.all_to_all(partial, 'frames', 0, 0, tiled=True)  20.3 us
    unnamed x40, local copies, waits for them, and re-layouts  16.3 us
    pallas_call x1, Pallas kernels, per_device(): kernel_call(attend_kernel, [shape((frames, 112, 128), BF16)], [SMEM, VMEM...  10.1 us
    pallas_call x1, Pallas kernels, per_device(): kernel_call(clean_kernel, [shape((ROWS, WIDTH), BF16), shape((ROWS, 4 * W...  10 us
    all_to_all x1, starting transfers between devices, per_device(): recv = lax.all_to_all(msg, 'frames', 0, 0, tiled=True)  9.37 us
    ppermute x1, waiting for transfers between devices, per_device(): from_left = lax.ppermute(up, 'frames', forward)  8.22 us
    pallas_call x1, Pallas kernels, per_device(): kernel_call(patch_kernel, [shape((site_ids.shape[0], ROWS), F32)], [SMEM,...  7.3 us
  transfers between devices with their start and end apart: 6, of which 6 were waited for; matrix products, arithmetic and copies ran while one was open for 0% of the time, Pallas kernels for 5%

profile of v7, /device:TPU:10, one launch (start us, length us, event | category | flops | bytes accessed | tf_op | source)
XLA Modules:
  0.0 135.8 jit_solution(14862777310511083235)
XLA Ops:
  0.6 4.7 %shard_map.148 = (bf16[32,128,128]{2,1,0:T(8,128)(2,1)}, bf16[128,1024]{1,0:T(8,128)(2,1)}, bf16[64,1024]{1,0:T(8,128)(2,1)}, bf16[64,1024]{1,0:T(8,128)(2,1)}) custom-call(bf16[128,1024]{1,0:T(8,128)(2,1)} %bitcast.9, bf16[128,1024]{1,0:T(8,128)(2,1)} %bitcast.8, bf16[128,1024]{1,0:T(8,128)(2,1)} %bitcast.11, s32[1,128]{1,0:T(1,128)} %mask_ref.1, ...), custom_call_target="tpu_custom_call" | custom-call | flops 800000000 | bytes 6000000 | tf_op jit(solution)/shard_map/pallas_call | solution.py:714
  5.3 9.4 %all-to-all-start = ((bf16[32,128,128]{2,1,0:T(8,128)(2,1)}), bf16[32,128,128]{2,1,0:T(8,128)(2,1)S(1)}, u32[]{:S(2)}, u32[]{:S(2)}) async-start(bf16[32,128,128]{2,1,0:T(8,128)(2,1)} %get-tuple-element.23), calls=%async_computation | async-start | bytes 2097152 | tf_op jit(solution)/shard_map/all_to_all | solution.py:731
  14.7 3.4 %collective-permute-start = (bf16[64,1024]{1,0:T(8,128)(2,1)}, bf16[64,1024]{1,0:T(8,128)(2,1)S(1)}, u32[]{:S(2)}, u32[]{:S(2)}) collective-permute-start(bf16[64,1024]{1,0:T(8,128)(2,1)} %get-tuple-element.24), channel_id=1, source_target_pairs={{0,1},{1,2},{2,3},{3,4},{4,5},{5,6},{6,7},{7,8},{8,9},{9,10},{10,1... | collective-permute-start | bytes 393224 | tf_op jit(solution)/shard_map/ppermute | solution.py:729
  18.1 2.5 %collective-permute-start.1 = (bf16[64,1024]{1,0:T(8,128)(2,1)}, bf16[64,1024]{1,0:T(8,128)(2,1)S(1)}, u32[]{:S(2)}, u32[]{:S(2)}) collective-permute-start(bf16[64,1024]{1,0:T(8,128)(2,1)} %get-tuple-element.25), channel_id=1, source_target_pairs={{1,0},{2,1},{3,2},{4,3},{5,4},{6,5},{7,6},{8,7},{9,8},{10,9},{11,1... | collective-permute-start | bytes 393224 | tf_op jit(solution)/shard_map/ppermute | solution.py:730
  21.2 0.1 stack.19.scal_ref
  21.3 8.2 %collective-permute-done.up_hbm.up_ref = bf16[64,1024]{1,0:T(8,128)(2,1)S(1)} collective-permute-done((bf16[64,1024]{1,0:T(8,128)(2,1)}, bf16[64,1024]{1,0:T(8,128)(2,1)S(1)}, u32[]{:S(2)}, u32[]{:S(2)}) %collective-permute-start) | collective-permute-done | bytes 131104 | tf_op jit(solution)/shard_map/ppermute | solution.py:729
  29.5 0.0 copy-start.11
  29.5 0.9 collective-permute-done.1.down_hbm.down_ref
  30.4 0.0 copy-start.13
  30.4 0.1 all-to-all-done.recv_ref
  30.6 10.1 %shard_map.149 = bf16[32,112,128]{2,1,0:T(8,128)(2,1)S(1)} custom-call(s32[5]{0:T(128)S(1)} %stack.19.scal_ref, bf16[32,128,128]{2,1,0:T(8,128)(2,1)S(1)} %all-to-all-done.recv_ref), custom_call_target="tpu_custom_call" | custom-call | flops 8000000000 | bytes 1000000 | tf_op jit(solution)/shard_map/pallas_call | solution.py:734
  40.6 0.0 copy-done.16
  40.7 0.0 copy-done.11
  40.7 0.0 copy-done.13
  40.7 20.6 %all_to_all.15.ctx_hbm.ctx_in = bf16[32,112,128]{2,1,0:T(8,128)(2,1)} all-to-all(bf16[32,112,128]{2,1,0:T(8,128)(2,1)S(1)} %shard_map.149), channel_id=1, replica_groups=mesh['dp'=4,'frames'=32] {'frames'}, dimensions={0} | all-to-all | bytes 1835008 | tf_op jit(solution)/shard_map/all_to_all | solution.py:744
  61.3 10.0 %shard_map.150 = (bf16[128,1024]{1,0:T(8,128)(2,1)}, bf16[128,4096]{1,0:T(8,128)(2,1)}, bf16[160,1024]{1,0:T(8,128)(2,1)}, f32[160,1024]{1,0:T(8,128)}, f32[1024...) custom-call(s32[5]{0:T(128)} %copy-done.16, bf16[32,112,128]{2,1,0:T(8,128)(2,1)} %all_to_all.15.ctx_hbm.ctx_in, ...), custom_call_target="tpu_custom_call" | custom-call | flops 3000000000 | bytes 10000000 | tf_op jit(solution)/shard_map/pallas_call | solution.py:745
  71.3 0.3 collective-permute-start.2
  71.6 2.9 %collective-permute-done.2.other_hbm = bf16[128,4096]{1,0:T(8,128)(2,1)S(1)} collective-permute-done((bf16[128,4096]{1,0:T(8,128)(2,1)}, bf16[128,4096]{1,0:T(8,128)(2,1)S(1)}, u32[]{:S(2)}, u32[]{:S(2)}) %collective-permute-start.2) | collective-permute-done | bytes 1048608 | tf_op jit(solution)/shard_map/ppermute | solution.py:770
  74.4 0.0 copy-start.19
  74.4 1.0 copy-done.19
  75.4 3.4 %shard_map.151 = bf16[32,16,3072]{2,1,0:T(8,128)(2,1)} custom-call(bf16[128,1024]{1,0:T(8,128)(2,1)} %get-tuple-element.29.own_hbm, bf16[128,4096]{1,0:T(8,128)(2,1)} %get-tuple-element.30.pack_hbm.pack_ref, bf16[128,4096]{1,0:T(8,128)(2,1)} %copy-done.19), custom_call_target="tpu_custom_call" | custom-call | flops 800000000 | bytes 10000000 | tf_op jit(solution)/shard_map/pallas_call | solution.py:771
  78.9 0.0 copy-start.8
  78.9 0.0 copy-start.17
  78.9 0.0 copy-start.18
  78.9 6.7 %all-to-all-start.2 = ((bf16[32,16,3072]{2,1,0:T(8,128)(2,1)}), bf16[32,16,3072]{2,1,0:T(8,128)(2,1)S(1)}, u32[]{:S(2)}, u32[]{:S(2)}) async-start(bf16[32,16,3072]{2,1,0:T(8,128)(2,1)} %shard_map.151), calls=%async_computation.2 | async-start | bytes 6291456 | tf_op jit(solution)/shard_map/all_to_all | solution.py:780
  85.6 0.0 copy-done.8
  85.6 0.0 copy-done.17
  85.6 0.0 copy-done.18
  85.7 0.0 copy-start
  85.7 2.2 %copy-done = bf16[1024,2048]{1,0:T(8,128)(2,1)S(1)} copy-done((bf16[1024,2048]{1,0:T(8,128)(2,1)S(1)}, bf16[1024,2048]{1,0:T(8,128)(2,1)}, u32[]{:S(2)}) %copy-start) | copy-done | bytes 4194328
  87.8 1.2 copy-done.1
  89.1 1.2 copy-done.2
  90.3 1.6 %copy-done.3 = bf16[1024,1024]{1,0:T(8,128)(2,1)S(1)} copy-done((bf16[1024,1024]{1,0:T(8,128)(2,1)S(1)}, bf16[1024,1024]{1,0:T(8,128)(2,1)}, u32[]{:S(2)}) %copy-start.3) | copy-done | bytes 2097176
  91.8 1.2 copy-done.4
  93.1 1.1 copy-done.5
  94.2 1.1 copy-done.6
  95.3 1.0 copy-done.7
  96.3 1.0 copy-done.9
  97.3 0.9 copy-done.10
  98.3 0.9 copy-done.12
  99.2 0.9 copy-done.14
  100.1 0.8 copy-done.15
  100.9 7.3 %shard_map.152 = f32[8,128]{1,0:T(8,128)} custom-call(s32[5]{0:T(128)S(1)} %copy-done.17, s32[8]{0:T(128)S(1)} %copy-done.18, bf16[32,112,128]{2,1,0:T(8,128)(2,1)S(1)} %copy-done.2, bf16[128,1024]{1,0:T(8,128)(2,1)S(1)} %copy-done.10, bf16[64,1024]{1,0:T(8,128)(2,1)S(1)} %copy-done.12, bf16[64,1024]{1,0:T(8,128)(2,1)S(1)} %copy-done.14, ...), custom_call_target="tpu_custom_call" | custom-call | flops 3000000000 | bytes 10000000 | tf_op jit(solution)/shard_map/pallas_call | solution.py:781
  108.2 20.3 %all-to-all-done.2.pieces_ref = bf16[32,16,3072]{2,1,0:T(8,128)(2,1)S(1)} async-done(((bf16[32,16,3072]{2,1,0:T(8,128)(2,1)}), bf16[32,16,3072]{2,1,0:T(8,128)(2,1)S(1)}, u32[]{:S(2)}, u32[]{:S(2)}) %all-to-all-start.2) | async-done | bytes 3145760 | tf_op jit(solution)/shard_map/all_to_all | solution.py:780
  128.5 1.0 shard_map.153
  129.5 2.4 %collective-permute-start.3 = (bf16[16,1536]{1,0:T(8,128)(2,1)S(1)}, bf16[16,1536]{1,0:T(8,128)(2,1)S(1)}, u32[]{:S(2)}, u32[]{:S(2)}) collective-permute-start(bf16[16,1536]{1,0:T(8,128)(2,1)S(1)} %get-tuple-element.40), channel_id=1, source_target_pairs={{0,64},{32,96},{64,0},{96,32},{1,65},{33,97},{65,1},{97,33},{2,66}... | collective-permute-start | bytes 147464 | tf_op jit(solution)/shard_map/ppermute | solution.py:804
  131.8 3.3 %collective-permute-done.3.theirs_ref = bf16[16,1536]{1,0:T(8,128)(2,1)S(1)} collective-permute-done((bf16[16,1536]{1,0:T(8,128)(2,1)S(1)}, bf16[16,1536]{1,0:T(8,128)(2,1)S(1)}, u32[]{:S(2)}, u32[]{:S(2)}) %collective-permute-start.3) | collective-permute-done | bytes 49184 | tf_op jit(solution)/shard_map/ppermute | solution.py:804
  135.1 0.6 shard_map.154
  (13 shorter events, 0.0 us)
Async XLA Ops:
  5.3 25.2 %all-to-all-start = ((bf16[32,128,128]{2,1,0:T(8,128)(2,1)}), bf16[32,128,128]{2,1,0:T(8,128)(2,1)S(1)}, u32[]{:S(2)}, u32[]{:S(2)}) async-start(bf16[32,128,128]{2,1,0:T(8,128)(2,1)} %get-tuple-element.23), calls=%async_computation | async-start | bytes 2097152 | tf_op jit(solution)/shard_map/all_to_all | solution.py:731
  14.7 14.8 %collective-permute-start = (bf16[64,1024]{1,0:T(8,128)(2,1)}, bf16[64,1024]{1,0:T(8,128)(2,1)S(1)}, u32[]{:S(2)}, u32[]{:S(2)}) collective-permute-start(bf16[64,1024]{1,0:T(8,128)(2,1)} %get-tuple-element.24), channel_id=1, source_target_pairs={{0,1},{1,2},{2,3},{3,4},{4,5},{5,6},{6,7},{7,8},{8,9},{9,10},{10,1... | collective-permute-start | bytes 393224 | tf_op jit(solution)/shard_map/ppermute | solution.py:729
  18.1 12.3 %collective-permute-start.1 = (bf16[64,1024]{1,0:T(8,128)(2,1)}, bf16[64,1024]{1,0:T(8,128)(2,1)S(1)}, u32[]{:S(2)}, u32[]{:S(2)}) collective-permute-start(bf16[64,1024]{1,0:T(8,128)(2,1)} %get-tuple-element.25), channel_id=1, source_target_pairs={{1,0},{2,1},{3,2},{4,3},{5,4},{6,5},{7,6},{8,7},{9,8},{10,9},{11,1... | collective-permute-start | bytes 393224 | tf_op jit(solution)/shard_map/ppermute | solution.py:730
  21.3 19.3 %copy-start.16 = (s32[5]{0:T(128)}, s32[5]{0:T(128)S(1)}, u32[]{:S(2)}) copy-start(s32[5]{0:T(128)S(1)} %stack.19.scal_ref) | copy-start | bytes 64
  29.5 11.1 %copy-start.11 = (bf16[64,1024]{1,0:T(8,128)(2,1)}, bf16[64,1024]{1,0:T(8,128)(2,1)S(1)}, u32[]{:S(2)}) copy-start(bf16[64,1024]{1,0:T(8,128)(2,1)S(1)} %collective-permute-done.up_hbm.up_ref) | copy-start | bytes 393220
  30.4 10.2 %copy-start.13 = (bf16[64,1024]{1,0:T(8,128)(2,1)}, bf16[64,1024]{1,0:T(8,128)(2,1)S(1)}, u32[]{:S(2)}) copy-start(bf16[64,1024]{1,0:T(8,128)(2,1)S(1)} %collective-permute-done.1.down_hbm.down_ref) | copy-start | bytes 393220
  71.3 3.1 %collective-permute-start.2 = (bf16[128,4096]{1,0:T(8,128)(2,1)}, bf16[128,4096]{1,0:T(8,128)(2,1)S(1)}, u32[]{:S(2)}, u32[]{:S(2)}) collective-permute-start(bf16[128,4096]{1,0:T(8,128)(2,1)} %get-tuple-element.30.pack_hbm.pack_ref), channel_id=1, source_target_pairs={{0,32},{32,0},{64,96},{96,64},{1,33},{33,1},{65,97},{97,65},{2,34}... | collective-permute-start | bytes 3145736 | tf_op jit(solution)/shard_map/ppermute | solution.py:770
  74.4 1.0 copy-start.19
  78.9 6.7 %copy-start.8 = (bf16[192,1024]{1,0:T(8,128)(2,1)S(1)}, bf16[192,1024]{1,0:T(8,128)(2,1)}, u32[]{:S(2)}) copy-start(bf16[192,1024]{1,0:T(8,128)(2,1)} %get-tuple-element.36.residc_ref) | copy-start | bytes 1179652
  78.9 6.7 %copy-start.17 = (s32[5]{0:T(128)S(1)}, s32[5]{0:T(128)}, u32[]{:S(2)}) copy-start(s32[5]{0:T(128)} %copy-done.16) | copy-start | bytes 64
  78.9 6.7 %copy-start.18 = (s32[8]{0:T(128)S(1)}, s32[8]{0:T(128)}, u32[]{:S(2)}) copy-start(s32[8]{0:T(128)} %site_ref.1) | copy-start | bytes 100
  78.9 49.5 %all-to-all-start.2 = ((bf16[32,16,3072]{2,1,0:T(8,128)(2,1)}), bf16[32,16,3072]{2,1,0:T(8,128)(2,1)S(1)}, u32[]{:S(2)}, u32[]{:S(2)}) async-start(bf16[32,16,3072]{2,1,0:T(8,128)(2,1)} %shard_map.151), calls=%async_computation.2 | async-start | bytes 6291456 | tf_op jit(solution)/shard_map/all_to_all | solution.py:780
  85.7 2.2 %copy-start = (bf16[1024,2048]{1,0:T(8,128)(2,1)S(1)}, bf16[1024,2048]{1,0:T(8,128)(2,1)}, u32[]{:S(2)}) copy-start(bf16[1024,2048]{1,0:T(8,128)(2,1)} %win_ref.1) | copy-start | bytes 12582916
  87.8 1.2 copy-start.1
  89.1 1.2 copy-start.2
  90.2 1.6 %copy-start.3 = (bf16[1024,1024]{1,0:T(8,128)(2,1)S(1)}, bf16[1024,1024]{1,0:T(8,128)(2,1)}, u32[]{:S(2)}) copy-start(bf16[1024,1024]{1,0:T(8,128)(2,1)} %wout_ref.1) | copy-start | bytes 6291460
  91.8 1.2 copy-start.4
  93.1 1.1 copy-start.5
  94.2 1.1 copy-start.6
  95.3 1.0 copy-start.7
  96.3 1.0 copy-start.9
  97.3 0.9 copy-start.10
  98.3 0.9 copy-start.12
  99.2 0.9 copy-start.14
  100.1 0.8 copy-start.15
  129.5 5.7 %collective-permute-start.3 = (bf16[16,1536]{1,0:T(8,128)(2,1)S(1)}, bf16[16,1536]{1,0:T(8,128)(2,1)S(1)}, u32[]{:S(2)}, u32[]{:S(2)}) collective-permute-start(bf16[16,1536]{1,0:T(8,128)(2,1)S(1)} %get-tuple-element.40), channel_id=1, source_target_pairs={{0,64},{32,96},{64,0},{96,32},{1,65},{33,97},{65,1},{97,33},{2,66}... | collective-permute-start | bytes 147464 | tf_op jit(solution)/shard_map/ppermute | solution.py:804

commit v8 on v7

--- a/solution.py
+++ b/solution.py
@@ -24,8 +24,8 @@
 GO = 3 * WIDTH
 UNROLL = True
 TAP_UNROLL = 4
-LOAD_UNROLL = 4
-PACK_UNROLL = 4
+LOAD_UNROLL = 16
+PACK_UNROLL = 8
 CHUNK = 256
 
 

time: 137 us -> 136 us (level)
  no operation moved by 1% of the time
where the time goes in v8:
time: 136 us; the launch traced here: 135 us
  Pallas kernels  36.5 us (27%)
  waiting for transfers between devices  35.7 us (26%)
  starting transfers between devices  24.6 us (18%)
  blocking collectives  20.6 us (15%)
  local copies, waits for them, and re-layouts  16.4 us (12%)
  between operations  1.46 us (1%)
    all_to_all x1, blocking collectives, per_device(): contexts = lax.all_to_all(context, 'frames', 0, 0, tiled=True)  20.6 us
    all_to_all x1, waiting for transfers between devices, per_device(): pieces = lax.all_to_all(partial, 'frames', 0, 0, tiled=True)  20.3 us
    unnamed x40, local copies, waits for them, and re-layouts  16.3 us
    pallas_call x1, Pallas kernels, per_device(): kernel_call(clean_kernel, [shape((ROWS, WIDTH), BF16), shape((ROWS, 4 * W...  9.99 us
    pallas_call x1, Pallas kernels, per_device(): kernel_call(attend_kernel, [shape((frames, 112, 128), BF16)], [SMEM, VMEM...  9.43 us
    all_to_all x1, starting transfers between devices, per_device(): recv = lax.all_to_all(msg, 'frames', 0, 0, tiled=True)  9.37 us
    ppermute x1, waiting for transfers between devices, per_device(): from_left = lax.ppermute(up, 'frames', forward)  8.22 us
    pallas_call x1, Pallas kernels, per_device(): kernel_call(patch_kernel, [shape((site_ids.shape[0], ROWS), F32)], [SMEM,...  7.3 us
  transfers between devices with their start and end apart: 6, of which 6 were waited for; matrix products, arithmetic and copies ran while one was open for 0% of the time, Pallas kernels for 5%

profile of v8, /device:TPU:10, one launch (start us, length us, event | category | flops | bytes accessed | tf_op | source)
XLA Modules:
  0.0 135.1 jit_solution(5748756321716894622)
XLA Ops:
  0.6 4.7 %shard_map.148 = (bf16[32,128,128]{2,1,0:T(8,128)(2,1)}, bf16[128,1024]{1,0:T(8,128)(2,1)}, bf16[64,1024]{1,0:T(8,128)(2,1)}, bf16[64,1024]{1,0:T(8,128)(2,1)}) custom-call(bf16[128,1024]{1,0:T(8,128)(2,1)} %bitcast.9, bf16[128,1024]{1,0:T(8,128)(2,1)} %bitcast.8, bf16[128,1024]{1,0:T(8,128)(2,1)} %bitcast.11, s32[1,128]{1,0:T(1,128)} %mask_ref.1, ...), custom_call_target="tpu_custom_call" | custom-call | flops 800000000 | bytes 6000000 | tf_op jit(solution)/shard_map/pallas_call | solution.py:714
  5.3 9.4 %all-to-all-start = ((bf16[32,128,128]{2,1,0:T(8,128)(2,1)}), bf16[32,128,128]{2,1,0:T(8,128)(2,1)S(1)}, u32[]{:S(2)}, u32[]{:S(2)}) async-start(bf16[32,128,128]{2,1,0:T(8,128)(2,1)} %get-tuple-element.23), calls=%async_computation | async-start | bytes 2097152 | tf_op jit(solution)/shard_map/all_to_all | solution.py:731
  14.7 3.4 %collective-permute-start = (bf16[64,1024]{1,0:T(8,128)(2,1)}, bf16[64,1024]{1,0:T(8,128)(2,1)S(1)}, u32[]{:S(2)}, u32[]{:S(2)}) collective-permute-start(bf16[64,1024]{1,0:T(8,128)(2,1)} %get-tuple-element.24), channel_id=1, source_target_pairs={{0,1},{1,2},{2,3},{3,4},{4,5},{5,6},{6,7},{7,8},{8,9},{9,10},{10,1... | collective-permute-start | bytes 393224 | tf_op jit(solution)/shard_map/ppermute | solution.py:729
  18.1 2.5 %collective-permute-start.1 = (bf16[64,1024]{1,0:T(8,128)(2,1)}, bf16[64,1024]{1,0:T(8,128)(2,1)S(1)}, u32[]{:S(2)}, u32[]{:S(2)}) collective-permute-start(bf16[64,1024]{1,0:T(8,128)(2,1)} %get-tuple-element.25), channel_id=1, source_target_pairs={{1,0},{2,1},{3,2},{4,3},{5,4},{6,5},{7,6},{8,7},{9,8},{10,9},{11,1... | collective-permute-start | bytes 393224 | tf_op jit(solution)/shard_map/ppermute | solution.py:730
  21.2 0.1 stack.19.scal_ref
  21.3 0.0 copy-start.16
  21.3 8.2 %collective-permute-done.up_hbm.up_ref = bf16[64,1024]{1,0:T(8,128)(2,1)S(1)} collective-permute-done((bf16[64,1024]{1,0:T(8,128)(2,1)}, bf16[64,1024]{1,0:T(8,128)(2,1)S(1)}, u32[]{:S(2)}, u32[]{:S(2)}) %collective-permute-start) | collective-permute-done | bytes 131104 | tf_op jit(solution)/shard_map/ppermute | solution.py:729
  29.5 0.0 copy-start.11
  29.5 0.9 collective-permute-done.1.down_hbm.down_ref
  30.4 0.0 copy-start.13
  30.4 0.1 all-to-all-done.recv_ref
  30.6 9.4 %shard_map.149 = bf16[32,112,128]{2,1,0:T(8,128)(2,1)S(1)} custom-call(s32[5]{0:T(128)S(1)} %stack.19.scal_ref, bf16[32,128,128]{2,1,0:T(8,128)(2,1)S(1)} %all-to-all-done.recv_ref), custom_call_target="tpu_custom_call" | custom-call | flops 8000000000 | bytes 1000000 | tf_op jit(solution)/shard_map/pallas_call | solution.py:734
  40.0 0.0 copy-done.16
  40.0 0.0 copy-done.11
  40.0 0.0 copy-done.13
  40.0 20.6 %all_to_all.15.ctx_hbm.ctx_in = bf16[32,112,128]{2,1,0:T(8,128)(2,1)} all-to-all(bf16[32,112,128]{2,1,0:T(8,128)(2,1)S(1)} %shard_map.149), channel_id=1, replica_groups=mesh['dp'=4,'frames'=32] {'frames'}, dimensions={0} | all-to-all | bytes 1835008 | tf_op jit(solution)/shard_map/all_to_all | solution.py:744
  60.6 10.0 %shard_map.150 = (bf16[128,1024]{1,0:T(8,128)(2,1)}, bf16[128,4096]{1,0:T(8,128)(2,1)}, bf16[160,1024]{1,0:T(8,128)(2,1)}, f32[160,1024]{1,0:T(8,128)}, f32[1024...) custom-call(s32[5]{0:T(128)} %copy-done.16, bf16[32,112,128]{2,1,0:T(8,128)(2,1)} %all_to_all.15.ctx_hbm.ctx_in, ...), custom_call_target="tpu_custom_call" | custom-call | flops 3000000000 | bytes 10000000 | tf_op jit(solution)/shard_map/pallas_call | solution.py:745
  70.6 0.3 collective-permute-start.2
  70.9 2.9 %collective-permute-done.2.other_hbm = bf16[128,4096]{1,0:T(8,128)(2,1)S(1)} collective-permute-done((bf16[128,4096]{1,0:T(8,128)(2,1)}, bf16[128,4096]{1,0:T(8,128)(2,1)S(1)}, u32[]{:S(2)}, u32[]{:S(2)}) %collective-permute-start.2) | collective-permute-done | bytes 1048608 | tf_op jit(solution)/shard_map/ppermute | solution.py:770
  73.8 1.0 copy-done.19
  74.8 3.4 %shard_map.151 = bf16[32,16,3072]{2,1,0:T(8,128)(2,1)} custom-call(bf16[128,1024]{1,0:T(8,128)(2,1)} %get-tuple-element.29.own_hbm, bf16[128,4096]{1,0:T(8,128)(2,1)} %get-tuple-element.30.pack_hbm.pack_ref, bf16[128,4096]{1,0:T(8,128)(2,1)} %copy-done.19), custom_call_target="tpu_custom_call" | custom-call | flops 800000000 | bytes 10000000 | tf_op jit(solution)/shard_map/pallas_call | solution.py:771
  78.2 0.0 copy-start.8
  78.3 0.0 copy-start.17
  78.3 0.0 copy-start.18
  78.3 6.7 %all-to-all-start.2 = ((bf16[32,16,3072]{2,1,0:T(8,128)(2,1)}), bf16[32,16,3072]{2,1,0:T(8,128)(2,1)S(1)}, u32[]{:S(2)}, u32[]{:S(2)}) async-start(bf16[32,16,3072]{2,1,0:T(8,128)(2,1)} %shard_map.151), calls=%async_computation.2 | async-start | bytes 6291456 | tf_op jit(solution)/shard_map/all_to_all | solution.py:780
  85.0 0.0 copy-done.8
  85.0 0.0 copy-done.17
  85.0 0.0 copy-done.18
  85.0 0.0 copy-start
  85.0 2.2 %copy-done = bf16[1024,2048]{1,0:T(8,128)(2,1)S(1)} copy-done((bf16[1024,2048]{1,0:T(8,128)(2,1)S(1)}, bf16[1024,2048]{1,0:T(8,128)(2,1)}, u32[]{:S(2)}) %copy-start) | copy-done | bytes 4194328
  87.2 1.2 copy-done.1
  88.4 1.2 copy-done.2
  89.6 1.6 %copy-done.3 = bf16[1024,1024]{1,0:T(8,128)(2,1)S(1)} copy-done((bf16[1024,1024]{1,0:T(8,128)(2,1)S(1)}, bf16[1024,1024]{1,0:T(8,128)(2,1)}, u32[]{:S(2)}) %copy-start.3) | copy-done | bytes 2097176
  91.2 1.2 copy-done.4
  92.4 1.1 copy-done.5
  93.6 1.1 copy-done.6
  94.7 1.0 copy-done.7
  95.7 1.0 copy-done.9
  96.7 0.9 copy-done.10
  97.6 0.9 copy-done.12
  98.5 0.9 copy-done.14
  99.4 0.8 copy-done.15
  100.3 7.3 %shard_map.152 = f32[8,128]{1,0:T(8,128)} custom-call(s32[5]{0:T(128)S(1)} %copy-done.17, s32[8]{0:T(128)S(1)} %copy-done.18, bf16[32,112,128]{2,1,0:T(8,128)(2,1)S(1)} %copy-done.2, bf16[128,1024]{1,0:T(8,128)(2,1)S(1)} %copy-done.10, bf16[64,1024]{1,0:T(8,128)(2,1)S(1)} %copy-done.12, bf16[64,1024]{1,0:T(8,128)(2,1)S(1)} %copy-done.14, ...), custom_call_target="tpu_custom_call" | custom-call | flops 3000000000 | bytes 10000000 | tf_op jit(solution)/shard_map/pallas_call | solution.py:781
  107.6 20.3 %all-to-all-done.2.pieces_ref = bf16[32,16,3072]{2,1,0:T(8,128)(2,1)S(1)} async-done(((bf16[32,16,3072]{2,1,0:T(8,128)(2,1)}), bf16[32,16,3072]{2,1,0:T(8,128)(2,1)S(1)}, u32[]{:S(2)}, u32[]{:S(2)}) %all-to-all-start.2) | async-done | bytes 3145760 | tf_op jit(solution)/shard_map/all_to_all | solution.py:780
  127.8 1.0 shard_map.153
  128.8 2.4 %collective-permute-start.3 = (bf16[16,1536]{1,0:T(8,128)(2,1)S(1)}, bf16[16,1536]{1,0:T(8,128)(2,1)S(1)}, u32[]{:S(2)}, u32[]{:S(2)}) collective-permute-start(bf16[16,1536]{1,0:T(8,128)(2,1)S(1)} %get-tuple-element.40), channel_id=1, source_target_pairs={{0,64},{32,96},{64,0},{96,32},{1,65},{33,97},{65,1},{97,33},{2,66}... | collective-permute-start | bytes 147464 | tf_op jit(solution)/shard_map/ppermute | solution.py:804
  131.2 3.3 %collective-permute-done.3.theirs_ref = bf16[16,1536]{1,0:T(8,128)(2,1)S(1)} collective-permute-done((bf16[16,1536]{1,0:T(8,128)(2,1)S(1)}, bf16[16,1536]{1,0:T(8,128)(2,1)S(1)}, u32[]{:S(2)}, u32[]{:S(2)}) %collective-permute-start.3) | collective-permute-done | bytes 49184 | tf_op jit(solution)/shard_map/ppermute | solution.py:804
  134.5 0.6 shard_map.154
  (13 shorter events, 0.0 us)
Async XLA Ops:
  5.3 25.2 %all-to-all-start = ((bf16[32,128,128]{2,1,0:T(8,128)(2,1)}), bf16[32,128,128]{2,1,0:T(8,128)(2,1)S(1)}, u32[]{:S(2)}, u32[]{:S(2)}) async-start(bf16[32,128,128]{2,1,0:T(8,128)(2,1)} %get-tuple-element.23), calls=%async_computation | async-start | bytes 2097152 | tf_op jit(solution)/shard_map/all_to_all | solution.py:731
  14.7 14.8 %collective-permute-start = (bf16[64,1024]{1,0:T(8,128)(2,1)}, bf16[64,1024]{1,0:T(8,128)(2,1)S(1)}, u32[]{:S(2)}, u32[]{:S(2)}) collective-permute-start(bf16[64,1024]{1,0:T(8,128)(2,1)} %get-tuple-element.24), channel_id=1, source_target_pairs={{0,1},{1,2},{2,3},{3,4},{4,5},{5,6},{6,7},{7,8},{8,9},{9,10},{10,1... | collective-permute-start | bytes 393224 | tf_op jit(solution)/shard_map/ppermute | solution.py:729
  18.1 12.3 %collective-permute-start.1 = (bf16[64,1024]{1,0:T(8,128)(2,1)}, bf16[64,1024]{1,0:T(8,128)(2,1)S(1)}, u32[]{:S(2)}, u32[]{:S(2)}) collective-permute-start(bf16[64,1024]{1,0:T(8,128)(2,1)} %get-tuple-element.25), channel_id=1, source_target_pairs={{1,0},{2,1},{3,2},{4,3},{5,4},{6,5},{7,6},{8,7},{9,8},{10,9},{11,1... | collective-permute-start | bytes 393224 | tf_op jit(solution)/shard_map/ppermute | solution.py:730
  21.3 18.7 %copy-start.16 = (s32[5]{0:T(128)}, s32[5]{0:T(128)S(1)}, u32[]{:S(2)}) copy-start(s32[5]{0:T(128)S(1)} %stack.19.scal_ref) | copy-start | bytes 64
  29.5 10.5 %copy-start.11 = (bf16[64,1024]{1,0:T(8,128)(2,1)}, bf16[64,1024]{1,0:T(8,128)(2,1)S(1)}, u32[]{:S(2)}) copy-start(bf16[64,1024]{1,0:T(8,128)(2,1)S(1)} %collective-permute-done.up_hbm.up_ref) | copy-start | bytes 393220
  30.4 9.6 %copy-start.13 = (bf16[64,1024]{1,0:T(8,128)(2,1)}, bf16[64,1024]{1,0:T(8,128)(2,1)S(1)}, u32[]{:S(2)}) copy-start(bf16[64,1024]{1,0:T(8,128)(2,1)S(1)} %collective-permute-done.1.down_hbm.down_ref) | copy-start | bytes 393220
  70.6 3.1 %collective-permute-start.2 = (bf16[128,4096]{1,0:T(8,128)(2,1)}, bf16[128,4096]{1,0:T(8,128)(2,1)S(1)}, u32[]{:S(2)}, u32[]{:S(2)}) collective-permute-start(bf16[128,4096]{1,0:T(8,128)(2,1)} %get-tuple-element.30.pack_hbm.pack_ref), channel_id=1, source_target_pairs={{0,32},{32,0},{64,96},{96,64},{1,33},{33,1},{65,97},{97,65},{2,34}... | collective-permute-start | bytes 3145736 | tf_op jit(solution)/shard_map/ppermute | solution.py:770
  73.8 1.0 copy-start.19
  78.2 6.8 %copy-start.8 = (bf16[192,1024]{1,0:T(8,128)(2,1)S(1)}, bf16[192,1024]{1,0:T(8,128)(2,1)}, u32[]{:S(2)}) copy-start(bf16[192,1024]{1,0:T(8,128)(2,1)} %get-tuple-element.36.residc_ref) | copy-start | bytes 1179652
  78.3 6.8 %copy-start.17 = (s32[5]{0:T(128)S(1)}, s32[5]{0:T(128)}, u32[]{:S(2)}) copy-start(s32[5]{0:T(128)} %copy-done.16) | copy-start | bytes 64
  78.3 6.8 %copy-start.18 = (s32[8]{0:T(128)S(1)}, s32[8]{0:T(128)}, u32[]{:S(2)}) copy-start(s32[8]{0:T(128)} %site_ref.1) | copy-start | bytes 100
  78.3 49.6 %all-to-all-start.2 = ((bf16[32,16,3072]{2,1,0:T(8,128)(2,1)}), bf16[32,16,3072]{2,1,0:T(8,128)(2,1)S(1)}, u32[]{:S(2)}, u32[]{:S(2)}) async-start(bf16[32,16,3072]{2,1,0:T(8,128)(2,1)} %shard_map.151), calls=%async_computation.2 | async-start | bytes 6291456 | tf_op jit(solution)/shard_map/all_to_all | solution.py:780
  85.0 2.2 %copy-start = (bf16[1024,2048]{1,0:T(8,128)(2,1)S(1)}, bf16[1024,2048]{1,0:T(8,128)(2,1)}, u32[]{:S(2)}) copy-start(bf16[1024,2048]{1,0:T(8,128)(2,1)} %win_ref.1) | copy-start | bytes 12582916
  87.2 1.2 copy-start.1
  88.4 1.2 copy-start.2
  89.6 1.6 %copy-start.3 = (bf16[1024,1024]{1,0:T(8,128)(2,1)S(1)}, bf16[1024,1024]{1,0:T(8,128)(2,1)}, u32[]{:S(2)}) copy-start(bf16[1024,1024]{1,0:T(8,128)(2,1)} %wout_ref.1) | copy-start | bytes 6291460
  91.2 1.2 copy-start.4
  92.4 1.1 copy-start.5
  93.6 1.1 copy-start.6
  94.7 1.0 copy-start.7
  95.7 1.0 copy-start.9
  96.7 0.9 copy-start.10
  97.6 0.9 copy-start.12
  98.5 0.9 copy-start.14
  99.4 0.8 copy-start.15
  128.8 5.7 %collective-permute-start.3 = (bf16[16,1536]{1,0:T(8,128)(2,1)S(1)}, bf16[16,1536]{1,0:T(8,128)(2,1)S(1)}, u32[]{:S(2)}, u32[]{:S(2)}) collective-permute-start(bf16[16,1536]{1,0:T(8,128)(2,1)S(1)} %get-tuple-element.40), channel_id=1, source_target_pairs={{0,64},{32,96},{64,0},{96,32},{1,65},{33,97},{65,1},{97,33},{2,66}... | collective-permute-start | bytes 147464 | tf_op jit(solution)/shard_map/ppermute | solution.py:804

commit v9 on v8

--- a/solution.py
+++ b/solution.py
@@ -23,9 +23,9 @@
 GM = WIDTH
 GO = 3 * WIDTH
 UNROLL = True
-TAP_UNROLL = 4
+TAP_UNROLL = 8
 LOAD_UNROLL = 16
-PACK_UNROLL = 8
+PACK_UNROLL = 16
 CHUNK = 256
 
 

time: 136 us -> 136 us (level)
  no operation moved by 1% of the time
where the time goes in v9:
time: 136 us; the launch traced here: 135 us
  Pallas kernels  36.4 us (27%)
  waiting for transfers between devices  35.7 us (26%)
  starting transfers between devices  24.4 us (18%)
  blocking collectives  20.6 us (15%)
  local copies, waits for them, and re-layouts  16.4 us (12%)
  between operations  1.46 us (1%)
    all_to_all x1, blocking collectives, per_device(): contexts = lax.all_to_all(context, 'frames', 0, 0, tiled=True)  20.6 us
    all_to_all x1, waiting for transfers between devices, per_device(): pieces = lax.all_to_all(partial, 'frames', 0, 0, tiled=True)  20.3 us
    unnamed x40, local copies, waits for them, and re-layouts  16.3 us
    pallas_call x1, Pallas kernels, per_device(): kernel_call(clean_kernel, [shape((ROWS, WIDTH), BF16), shape((ROWS, 4 * W...  9.96 us
    pallas_call x1, Pallas kernels, per_device(): kernel_call(attend_kernel, [shape((frames, 112, 128), BF16)], [SMEM, VMEM...  9.41 us
    all_to_all x1, starting transfers between devices, per_device(): recv = lax.all_to_all(msg, 'frames', 0, 0, tiled=True)  9.37 us
    ppermute x1, waiting for transfers between devices, per_device(): from_left = lax.ppermute(up, 'frames', forward)  8.22 us
    pallas_call x1, Pallas kernels, per_device(): kernel_call(patch_kernel, [shape((site_ids.shape[0], ROWS), F32)], [SMEM,...  7.26 us
  transfers between devices with their start and end apart: 6, of which 6 were waited for; matrix products, arithmetic and copies ran while one was open for 0% of the time, Pallas kernels for 5%

profile of v9, /device:TPU:10, one launch (start us, length us, event | category | flops | bytes accessed | tf_op | source)
XLA Modules:
  0.0 134.9 jit_solution(5537317383362915515)
XLA Ops:
  0.6 4.7 %shard_map.148 = (bf16[32,128,128]{2,1,0:T(8,128)(2,1)}, bf16[128,1024]{1,0:T(8,128)(2,1)}, bf16[64,1024]{1,0:T(8,128)(2,1)}, bf16[64,1024]{1,0:T(8,128)(2,1)}) custom-call(bf16[128,1024]{1,0:T(8,128)(2,1)} %bitcast.9, bf16[128,1024]{1,0:T(8,128)(2,1)} %bitcast.8, bf16[128,1024]{1,0:T(8,128)(2,1)} %bitcast.11, s32[1,128]{1,0:T(1,128)} %mask_ref.1, ...), custom_call_target="tpu_custom_call" | custom-call | flops 800000000 | bytes 6000000 | tf_op jit(solution)/shard_map/pallas_call | solution.py:714
  5.3 9.4 %all-to-all-start = ((bf16[32,128,128]{2,1,0:T(8,128)(2,1)}), bf16[32,128,128]{2,1,0:T(8,128)(2,1)S(1)}, u32[]{:S(2)}, u32[]{:S(2)}) async-start(bf16[32,128,128]{2,1,0:T(8,128)(2,1)} %get-tuple-element.23), calls=%async_computation | async-start | bytes 2097152 | tf_op jit(solution)/shard_map/all_to_all | solution.py:731
  14.7 3.4 %collective-permute-start = (bf16[64,1024]{1,0:T(8,128)(2,1)}, bf16[64,1024]{1,0:T(8,128)(2,1)S(1)}, u32[]{:S(2)}, u32[]{:S(2)}) collective-permute-start(bf16[64,1024]{1,0:T(8,128)(2,1)} %get-tuple-element.24), channel_id=1, source_target_pairs={{0,1},{1,2},{2,3},{3,4},{4,5},{5,6},{6,7},{7,8},{8,9},{9,10},{10,1... | collective-permute-start | bytes 393224 | tf_op jit(solution)/shard_map/ppermute | solution.py:729
  18.1 2.5 %collective-permute-start.1 = (bf16[64,1024]{1,0:T(8,128)(2,1)}, bf16[64,1024]{1,0:T(8,128)(2,1)S(1)}, u32[]{:S(2)}, u32[]{:S(2)}) collective-permute-start(bf16[64,1024]{1,0:T(8,128)(2,1)} %get-tuple-element.25), channel_id=1, source_target_pairs={{1,0},{2,1},{3,2},{4,3},{5,4},{6,5},{7,6},{8,7},{9,8},{10,9},{11,1... | collective-permute-start | bytes 393224 | tf_op jit(solution)/shard_map/ppermute | solution.py:730
  21.2 0.1 stack.19.scal_ref
  21.3 0.0 copy-start.16
  21.3 8.2 %collective-permute-done.up_hbm.up_ref = bf16[64,1024]{1,0:T(8,128)(2,1)S(1)} collective-permute-done((bf16[64,1024]{1,0:T(8,128)(2,1)}, bf16[64,1024]{1,0:T(8,128)(2,1)S(1)}, u32[]{:S(2)}, u32[]{:S(2)}) %collective-permute-start) | collective-permute-done | bytes 131104 | tf_op jit(solution)/shard_map/ppermute | solution.py:729
  29.5 0.0 copy-start.11
  29.5 0.9 collective-permute-done.1.down_hbm.down_ref
  30.4 0.0 copy-start.13
  30.4 0.1 all-to-all-done.recv_ref
  30.6 9.4 %shard_map.149 = bf16[32,112,128]{2,1,0:T(8,128)(2,1)S(1)} custom-call(s32[5]{0:T(128)S(1)} %stack.19.scal_ref, bf16[32,128,128]{2,1,0:T(8,128)(2,1)S(1)} %all-to-all-done.recv_ref), custom_call_target="tpu_custom_call" | custom-call | flops 8000000000 | bytes 1000000 | tf_op jit(solution)/shard_map/pallas_call | solution.py:734
  40.0 0.0 copy-done.16
  40.0 0.0 copy-done.11
  40.0 0.0 copy-done.13
  40.0 20.6 %all_to_all.15.ctx_hbm.ctx_in = bf16[32,112,128]{2,1,0:T(8,128)(2,1)} all-to-all(bf16[32,112,128]{2,1,0:T(8,128)(2,1)S(1)} %shard_map.149), channel_id=1, replica_groups=mesh['dp'=4,'frames'=32] {'frames'}, dimensions={0} | all-to-all | bytes 1835008 | tf_op jit(solution)/shard_map/all_to_all | solution.py:744
  60.6 10.0 %shard_map.150 = (bf16[128,1024]{1,0:T(8,128)(2,1)}, bf16[128,4096]{1,0:T(8,128)(2,1)}, bf16[160,1024]{1,0:T(8,128)(2,1)}, f32[160,1024]{1,0:T(8,128)}, f32[1024...) custom-call(s32[5]{0:T(128)} %copy-done.16, bf16[32,112,128]{2,1,0:T(8,128)(2,1)} %all_to_all.15.ctx_hbm.ctx_in, ...), custom_call_target="tpu_custom_call" | custom-call | flops 3000000000 | bytes 10000000 | tf_op jit(solution)/shard_map/pallas_call | solution.py:745
  70.6 0.1 collective-permute-start.2
  70.7 2.9 %collective-permute-done.2.other_hbm = bf16[128,4096]{1,0:T(8,128)(2,1)S(1)} collective-permute-done((bf16[128,4096]{1,0:T(8,128)(2,1)}, bf16[128,4096]{1,0:T(8,128)(2,1)S(1)}, u32[]{:S(2)}, u32[]{:S(2)}) %collective-permute-start.2) | collective-permute-done | bytes 1048608 | tf_op jit(solution)/shard_map/ppermute | solution.py:770
  73.5 1.0 copy-done.19
  74.6 3.4 %shard_map.151 = bf16[32,16,3072]{2,1,0:T(8,128)(2,1)} custom-call(bf16[128,1024]{1,0:T(8,128)(2,1)} %get-tuple-element.29.own_hbm, bf16[128,4096]{1,0:T(8,128)(2,1)} %get-tuple-element.30.pack_hbm.pack_ref, bf16[128,4096]{1,0:T(8,128)(2,1)} %copy-done.19), custom_call_target="tpu_custom_call" | custom-call | flops 800000000 | bytes 10000000 | tf_op jit(solution)/shard_map/pallas_call | solution.py:771
  78.0 0.0 copy-start.8
  78.0 0.0 copy-start.17
  78.0 0.0 copy-start.18
  78.0 6.7 %all-to-all-start.2 = ((bf16[32,16,3072]{2,1,0:T(8,128)(2,1)}), bf16[32,16,3072]{2,1,0:T(8,128)(2,1)S(1)}, u32[]{:S(2)}, u32[]{:S(2)}) async-start(bf16[32,16,3072]{2,1,0:T(8,128)(2,1)} %shard_map.151), calls=%async_computation.2 | async-start | bytes 6291456 | tf_op jit(solution)/shard_map/all_to_all | solution.py:780
  84.8 0.0 copy-done.8
  84.8 0.0 copy-done.17
  84.8 0.0 copy-done.18
  84.8 0.0 copy-start
  84.8 2.2 %copy-done = bf16[1024,2048]{1,0:T(8,128)(2,1)S(1)} copy-done((bf16[1024,2048]{1,0:T(8,128)(2,1)S(1)}, bf16[1024,2048]{1,0:T(8,128)(2,1)}, u32[]{:S(2)}) %copy-start) | copy-done | bytes 4194328
  87.0 1.2 copy-done.1
  88.2 1.2 copy-done.2
  89.4 1.6 %copy-done.3 = bf16[1024,1024]{1,0:T(8,128)(2,1)S(1)} copy-done((bf16[1024,1024]{1,0:T(8,128)(2,1)S(1)}, bf16[1024,1024]{1,0:T(8,128)(2,1)}, u32[]{:S(2)}) %copy-start.3) | copy-done | bytes 2097176
  91.0 1.2 copy-done.4
  92.2 1.1 copy-done.5
  93.4 1.1 copy-done.6
  94.5 1.0 copy-done.7
  95.5 1.0 copy-done.9
  96.5 0.9 copy-done.10
  97.4 0.9 copy-done.12
  98.3 0.9 copy-done.14
  99.2 0.8 copy-done.15
  100.1 7.3 %shard_map.152 = f32[8,128]{1,0:T(8,128)} custom-call(s32[5]{0:T(128)S(1)} %copy-done.17, s32[8]{0:T(128)S(1)} %copy-done.18, bf16[32,112,128]{2,1,0:T(8,128)(2,1)S(1)} %copy-done.2, bf16[128,1024]{1,0:T(8,128)(2,1)S(1)} %copy-done.10, bf16[64,1024]{1,0:T(8,128)(2,1)S(1)} %copy-done.12, bf16[64,1024]{1,0:T(8,128)(2,1)S(1)} %copy-done.14, ...), custom_call_target="tpu_custom_call" | custom-call | flops 3000000000 | bytes 10000000 | tf_op jit(solution)/shard_map/pallas_call | solution.py:781
  107.3 20.3 %all-to-all-done.2.pieces_ref = bf16[32,16,3072]{2,1,0:T(8,128)(2,1)S(1)} async-done(((bf16[32,16,3072]{2,1,0:T(8,128)(2,1)}), bf16[32,16,3072]{2,1,0:T(8,128)(2,1)S(1)}, u32[]{:S(2)}, u32[]{:S(2)}) %all-to-all-start.2) | async-done | bytes 3145760 | tf_op jit(solution)/shard_map/all_to_all | solution.py:780
  127.6 1.0 shard_map.153
  128.6 2.3 %collective-permute-start.3 = (bf16[16,1536]{1,0:T(8,128)(2,1)S(1)}, bf16[16,1536]{1,0:T(8,128)(2,1)S(1)}, u32[]{:S(2)}, u32[]{:S(2)}) collective-permute-start(bf16[16,1536]{1,0:T(8,128)(2,1)S(1)} %get-tuple-element.40), channel_id=1, source_target_pairs={{0,64},{32,96},{64,0},{96,32},{1,65},{33,97},{65,1},{97,33},{2,66}... | collective-permute-start | bytes 147464 | tf_op jit(solution)/shard_map/ppermute | solution.py:804
  130.9 3.3 %collective-permute-done.3.theirs_ref = bf16[16,1536]{1,0:T(8,128)(2,1)S(1)} collective-permute-done((bf16[16,1536]{1,0:T(8,128)(2,1)S(1)}, bf16[16,1536]{1,0:T(8,128)(2,1)S(1)}, u32[]{:S(2)}, u32[]{:S(2)}) %collective-permute-start.3) | collective-permute-done | bytes 49184 | tf_op jit(solution)/shard_map/ppermute | solution.py:804
  134.3 0.6 shard_map.154
  (13 shorter events, 0.0 us)
Async XLA Ops:
  5.3 25.2 %all-to-all-start = ((bf16[32,128,128]{2,1,0:T(8,128)(2,1)}), bf16[32,128,128]{2,1,0:T(8,128)(2,1)S(1)}, u32[]{:S(2)}, u32[]{:S(2)}) async-start(bf16[32,128,128]{2,1,0:T(8,128)(2,1)} %get-tuple-element.23), calls=%async_computation | async-start | bytes 2097152 | tf_op jit(solution)/shard_map/all_to_all | solution.py:731
  14.7 14.8 %collective-permute-start = (bf16[64,1024]{1,0:T(8,128)(2,1)}, bf16[64,1024]{1,0:T(8,128)(2,1)S(1)}, u32[]{:S(2)}, u32[]{:S(2)}) collective-permute-start(bf16[64,1024]{1,0:T(8,128)(2,1)} %get-tuple-element.24), channel_id=1, source_target_pairs={{0,1},{1,2},{2,3},{3,4},{4,5},{5,6},{6,7},{7,8},{8,9},{9,10},{10,1... | collective-permute-start | bytes 393224 | tf_op jit(solution)/shard_map/ppermute | solution.py:729
  18.1 12.3 %collective-permute-start.1 = (bf16[64,1024]{1,0:T(8,128)(2,1)}, bf16[64,1024]{1,0:T(8,128)(2,1)S(1)}, u32[]{:S(2)}, u32[]{:S(2)}) collective-permute-start(bf16[64,1024]{1,0:T(8,128)(2,1)} %get-tuple-element.25), channel_id=1, source_target_pairs={{1,0},{2,1},{3,2},{4,3},{5,4},{6,5},{7,6},{8,7},{9,8},{10,9},{11,1... | collective-permute-start | bytes 393224 | tf_op jit(solution)/shard_map/ppermute | solution.py:730
  21.3 18.7 %copy-start.16 = (s32[5]{0:T(128)}, s32[5]{0:T(128)S(1)}, u32[]{:S(2)}) copy-start(s32[5]{0:T(128)S(1)} %stack.19.scal_ref) | copy-start | bytes 64
  29.5 10.5 %copy-start.11 = (bf16[64,1024]{1,0:T(8,128)(2,1)}, bf16[64,1024]{1,0:T(8,128)(2,1)S(1)}, u32[]{:S(2)}) copy-start(bf16[64,1024]{1,0:T(8,128)(2,1)S(1)} %collective-permute-done.up_hbm.up_ref) | copy-start | bytes 393220
  30.4 9.6 %copy-start.13 = (bf16[64,1024]{1,0:T(8,128)(2,1)}, bf16[64,1024]{1,0:T(8,128)(2,1)S(1)}, u32[]{:S(2)}) copy-start(bf16[64,1024]{1,0:T(8,128)(2,1)S(1)} %collective-permute-done.1.down_hbm.down_ref) | copy-start | bytes 393220
  70.6 3.0 %collective-permute-start.2 = (bf16[128,4096]{1,0:T(8,128)(2,1)}, bf16[128,4096]{1,0:T(8,128)(2,1)S(1)}, u32[]{:S(2)}, u32[]{:S(2)}) collective-permute-start(bf16[128,4096]{1,0:T(8,128)(2,1)} %get-tuple-element.30.pack_hbm.pack_ref), channel_id=1, source_target_pairs={{0,32},{32,0},{64,96},{96,64},{1,33},{33,1},{65,97},{97,65},{2,34}... | collective-permute-start | bytes 3145736 | tf_op jit(solution)/shard_map/ppermute | solution.py:770
  73.5 1.0 copy-start.19
  78.0 6.8 %copy-start.8 = (bf16[192,1024]{1,0:T(8,128)(2,1)S(1)}, bf16[192,1024]{1,0:T(8,128)(2,1)}, u32[]{:S(2)}) copy-start(bf16[192,1024]{1,0:T(8,128)(2,1)} %get-tuple-element.36.residc_ref) | copy-start | bytes 1179652
  78.0 6.8 %copy-start.17 = (s32[5]{0:T(128)S(1)}, s32[5]{0:T(128)}, u32[]{:S(2)}) copy-start(s32[5]{0:T(128)} %copy-done.16) | copy-start | bytes 64
  78.0 6.8 %copy-start.18 = (s32[8]{0:T(128)S(1)}, s32[8]{0:T(128)}, u32[]{:S(2)}) copy-start(s32[8]{0:T(128)} %site_ref.1) | copy-start | bytes 100
  78.0 49.6 %all-to-all-start.2 = ((bf16[32,16,3072]{2,1,0:T(8,128)(2,1)}), bf16[32,16,3072]{2,1,0:T(8,128)(2,1)S(1)}, u32[]{:S(2)}, u32[]{:S(2)}) async-start(bf16[32,16,3072]{2,1,0:T(8,128)(2,1)} %shard_map.151), calls=%async_computation.2 | async-start | bytes 6291456 | tf_op jit(solution)/shard_map/all_to_all | solution.py:780
  84.8 2.2 %copy-start = (bf16[1024,2048]{1,0:T(8,128)(2,1)S(1)}, bf16[1024,2048]{1,0:T(8,128)(2,1)}, u32[]{:S(2)}) copy-start(bf16[1024,2048]{1,0:T(8,128)(2,1)} %win_ref.1) | copy-start | bytes 12582916
  87.0 1.2 copy-start.1
  88.2 1.2 copy-start.2
  89.4 1.6 %copy-start.3 = (bf16[1024,1024]{1,0:T(8,128)(2,1)S(1)}, bf16[1024,1024]{1,0:T(8,128)(2,1)}, u32[]{:S(2)}) copy-start(bf16[1024,1024]{1,0:T(8,128)(2,1)} %wout_ref.1) | copy-start | bytes 6291460
  91.0 1.2 copy-start.4
  92.2 1.1 copy-start.5
  93.4 1.1 copy-start.6
  94.5 1.0 copy-start.7
  95.5 1.0 copy-start.9
  96.5 0.9 copy-start.10
  97.4 0.9 copy-start.12
  98.3 0.9 copy-start.14
  99.2 0.8 copy-start.15
  128.6 5.7 %collective-permute-start.3 = (bf16[16,1536]{1,0:T(8,128)(2,1)S(1)}, bf16[16,1536]{1,0:T(8,128)(2,1)S(1)}, u32[]{:S(2)}, u32[]{:S(2)}) collective-permute-start(bf16[16,1536]{1,0:T(8,128)(2,1)S(1)} %get-tuple-element.40), channel_id=1, source_target_pairs={{0,64},{32,96},{64,0},{96,32},{1,65},{33,97},{65,1},{97,33},{2,66}... | collective-permute-start | bytes 147464 | tf_op jit(solution)/shard_map/ppermute | solution.py:804

commit v10 on v9

--- a/solution.py
+++ b/solution.py
@@ -25,7 +25,7 @@
 UNROLL = True
 TAP_UNROLL = 8
 LOAD_UNROLL = 16
-PACK_UNROLL = 16
+PACK_UNROLL = 32
 CHUNK = 256
 
 

time: 136 us -> 136 us (level)
  no operation moved by 1% of the time
where the time goes in v10:
time: 136 us; the launch traced here: 135 us
  Pallas kernels  36.2 us (27%)
  waiting for transfers between devices  35.7 us (26%)
  starting transfers between devices  24.6 us (18%)
  blocking collectives  20.6 us (15%)
  local copies, waits for them, and re-layouts  16.4 us (12%)
  between operations  1.46 us (1%)
    all_to_all x1, blocking collectives, per_device(): contexts = lax.all_to_all(context, 'frames', 0, 0, tiled=True)  20.6 us
    all_to_all x1, waiting for transfers between devices, per_device(): pieces = lax.all_to_all(partial, 'frames', 0, 0, tiled=True)  20.3 us
    unnamed x40, local copies, waits for them, and re-layouts  16.3 us
    pallas_call x1, Pallas kernels, per_device(): kernel_call(clean_kernel, [shape((ROWS, WIDTH), BF16), shape((ROWS, 4 * W...  9.97 us
    all_to_all x1, starting transfers between devices, per_device(): recv = lax.all_to_all(msg, 'frames', 0, 0, tiled=True)  9.37 us
    pallas_call x1, Pallas kernels, per_device(): kernel_call(attend_kernel, [shape((frames, 112, 128), BF16)], [SMEM, VMEM...  9.23 us
    ppermute x1, waiting for transfers between devices, per_device(): from_left = lax.ppermute(up, 'frames', forward)  8.22 us
    pallas_call x1, Pallas kernels, per_device(): kernel_call(patch_kernel, [shape((site_ids.shape[0], ROWS), F32)], [SMEM,...  7.26 us
  transfers between devices with their start and end apart: 6, of which 6 were waited for; matrix products, arithmetic and copies ran while one was open for 0% of the time, Pallas kernels for 5%

profile of v10, /device:TPU:10, one launch (start us, length us, event | category | flops | bytes accessed | tf_op | source)
XLA Modules:
  0.0 134.9 jit_solution(8352676242168388550)
XLA Ops:
  0.6 4.7 %shard_map.148 = (bf16[32,128,128]{2,1,0:T(8,128)(2,1)}, bf16[128,1024]{1,0:T(8,128)(2,1)}, bf16[64,1024]{1,0:T(8,128)(2,1)}, bf16[64,1024]{1,0:T(8,128)(2,1)}) custom-call(bf16[128,1024]{1,0:T(8,128)(2,1)} %bitcast.9, bf16[128,1024]{1,0:T(8,128)(2,1)} %bitcast.8, bf16[128,1024]{1,0:T(8,128)(2,1)} %bitcast.11, s32[1,128]{1,0:T(1,128)} %mask_ref.1, ...), custom_call_target="tpu_custom_call" | custom-call | flops 800000000 | bytes 6000000 | tf_op jit(solution)/shard_map/pallas_call | solution.py:714
  5.3 9.4 %all-to-all-start = ((bf16[32,128,128]{2,1,0:T(8,128)(2,1)}), bf16[32,128,128]{2,1,0:T(8,128)(2,1)S(1)}, u32[]{:S(2)}, u32[]{:S(2)}) async-start(bf16[32,128,128]{2,1,0:T(8,128)(2,1)} %get-tuple-element.23), calls=%async_computation | async-start | bytes 2097152 | tf_op jit(solution)/shard_map/all_to_all | solution.py:731
  14.7 3.4 %collective-permute-start = (bf16[64,1024]{1,0:T(8,128)(2,1)}, bf16[64,1024]{1,0:T(8,128)(2,1)S(1)}, u32[]{:S(2)}, u32[]{:S(2)}) collective-permute-start(bf16[64,1024]{1,0:T(8,128)(2,1)} %get-tuple-element.24), channel_id=1, source_target_pairs={{0,1},{1,2},{2,3},{3,4},{4,5},{5,6},{6,7},{7,8},{8,9},{9,10},{10,1... | collective-permute-start | bytes 393224 | tf_op jit(solution)/shard_map/ppermute | solution.py:729
  18.1 2.5 %collective-permute-start.1 = (bf16[64,1024]{1,0:T(8,128)(2,1)}, bf16[64,1024]{1,0:T(8,128)(2,1)S(1)}, u32[]{:S(2)}, u32[]{:S(2)}) collective-permute-start(bf16[64,1024]{1,0:T(8,128)(2,1)} %get-tuple-element.25), channel_id=1, source_target_pairs={{1,0},{2,1},{3,2},{4,3},{5,4},{6,5},{7,6},{8,7},{9,8},{10,9},{11,1... | collective-permute-start | bytes 393224 | tf_op jit(solution)/shard_map/ppermute | solution.py:730
  21.2 0.1 stack.19.scal_ref
  21.3 0.0 copy-start.16
  21.3 8.2 %collective-permute-done.up_hbm.up_ref = bf16[64,1024]{1,0:T(8,128)(2,1)S(1)} collective-permute-done((bf16[64,1024]{1,0:T(8,128)(2,1)}, bf16[64,1024]{1,0:T(8,128)(2,1)S(1)}, u32[]{:S(2)}, u32[]{:S(2)}) %collective-permute-start) | collective-permute-done | bytes 131104 | tf_op jit(solution)/shard_map/ppermute | solution.py:729
  29.5 0.0 copy-start.11
  29.5 0.9 collective-permute-done.1.down_hbm.down_ref
  30.4 0.0 copy-start.13
  30.4 0.1 all-to-all-done.recv_ref
  30.6 9.2 %shard_map.149 = bf16[32,112,128]{2,1,0:T(8,128)(2,1)S(1)} custom-call(s32[5]{0:T(128)S(1)} %stack.19.scal_ref, bf16[32,128,128]{2,1,0:T(8,128)(2,1)S(1)} %all-to-all-done.recv_ref), custom_call_target="tpu_custom_call" | custom-call | flops 8000000000 | bytes 1000000 | tf_op jit(solution)/shard_map/pallas_call | solution.py:734
  39.8 0.0 copy-done.16
  39.8 0.0 copy-done.11
  39.8 0.0 copy-done.13
  39.8 20.6 %all_to_all.15.ctx_hbm.ctx_in = bf16[32,112,128]{2,1,0:T(8,128)(2,1)} all-to-all(bf16[32,112,128]{2,1,0:T(8,128)(2,1)S(1)} %shard_map.149), channel_id=1, replica_groups=mesh['dp'=4,'frames'=32] {'frames'}, dimensions={0} | all-to-all | bytes 1835008 | tf_op jit(solution)/shard_map/all_to_all | solution.py:744
  60.4 10.0 %shard_map.150 = (bf16[128,1024]{1,0:T(8,128)(2,1)}, bf16[128,4096]{1,0:T(8,128)(2,1)}, bf16[160,1024]{1,0:T(8,128)(2,1)}, f32[160,1024]{1,0:T(8,128)}, f32[1024...) custom-call(s32[5]{0:T(128)} %copy-done.16, bf16[32,112,128]{2,1,0:T(8,128)(2,1)} %all_to_all.15.ctx_hbm.ctx_in, ...), custom_call_target="tpu_custom_call" | custom-call | flops 3000000000 | bytes 10000000 | tf_op jit(solution)/shard_map/pallas_call | solution.py:745
  70.4 0.3 collective-permute-start.2
  70.7 2.9 %collective-permute-done.2.other_hbm = bf16[128,4096]{1,0:T(8,128)(2,1)S(1)} collective-permute-done((bf16[128,4096]{1,0:T(8,128)(2,1)}, bf16[128,4096]{1,0:T(8,128)(2,1)S(1)}, u32[]{:S(2)}, u32[]{:S(2)}) %collective-permute-start.2) | collective-permute-done | bytes 1048608 | tf_op jit(solution)/shard_map/ppermute | solution.py:770
  73.5 1.0 copy-done.19
  74.6 3.4 %shard_map.151 = bf16[32,16,3072]{2,1,0:T(8,128)(2,1)} custom-call(bf16[128,1024]{1,0:T(8,128)(2,1)} %get-tuple-element.29.own_hbm, bf16[128,4096]{1,0:T(8,128)(2,1)} %get-tuple-element.30.pack_hbm.pack_ref, bf16[128,4096]{1,0:T(8,128)(2,1)} %copy-done.19), custom_call_target="tpu_custom_call" | custom-call | flops 800000000 | bytes 10000000 | tf_op jit(solution)/shard_map/pallas_call | solution.py:771
  78.0 0.0 copy-start.8
  78.0 0.0 copy-start.17
  78.0 0.0 copy-start.18
  78.0 6.7 %all-to-all-start.2 = ((bf16[32,16,3072]{2,1,0:T(8,128)(2,1)}), bf16[32,16,3072]{2,1,0:T(8,128)(2,1)S(1)}, u32[]{:S(2)}, u32[]{:S(2)}) async-start(bf16[32,16,3072]{2,1,0:T(8,128)(2,1)} %shard_map.151), calls=%async_computation.2 | async-start | bytes 6291456 | tf_op jit(solution)/shard_map/all_to_all | solution.py:780
  84.7 0.0 copy-done.8
  84.8 0.0 copy-done.17
  84.8 0.0 copy-done.18
  84.8 0.0 copy-start
  84.8 2.2 %copy-done = bf16[1024,2048]{1,0:T(8,128)(2,1)S(1)} copy-done((bf16[1024,2048]{1,0:T(8,128)(2,1)S(1)}, bf16[1024,2048]{1,0:T(8,128)(2,1)}, u32[]{:S(2)}) %copy-start) | copy-done | bytes 4194328
  87.0 1.2 copy-done.1
  88.2 1.2 copy-done.2
  89.4 1.6 %copy-done.3 = bf16[1024,1024]{1,0:T(8,128)(2,1)S(1)} copy-done((bf16[1024,1024]{1,0:T(8,128)(2,1)S(1)}, bf16[1024,1024]{1,0:T(8,128)(2,1)}, u32[]{:S(2)}) %copy-start.3) | copy-done | bytes 2097176
  91.0 1.2 copy-done.4
  92.2 1.1 copy-done.5
  93.3 1.1 copy-done.6
  94.4 1.0 copy-done.7
  95.5 1.0 copy-done.9
  96.4 0.9 copy-done.10
  97.4 0.9 copy-done.12
  98.3 0.9 copy-done.14
  99.2 0.8 copy-done.15
  100.0 7.3 %shard_map.152 = f32[8,128]{1,0:T(8,128)} custom-call(s32[5]{0:T(128)S(1)} %copy-done.17, s32[8]{0:T(128)S(1)} %copy-done.18, bf16[32,112,128]{2,1,0:T(8,128)(2,1)S(1)} %copy-done.2, bf16[128,1024]{1,0:T(8,128)(2,1)S(1)} %copy-done.10, bf16[64,1024]{1,0:T(8,128)(2,1)S(1)} %copy-done.12, bf16[64,1024]{1,0:T(8,128)(2,1)S(1)} %copy-done.14, ...), custom_call_target="tpu_custom_call" | custom-call | flops 3000000000 | bytes 10000000 | tf_op jit(solution)/shard_map/pallas_call | solution.py:781
  107.3 20.3 %all-to-all-done.2.pieces_ref = bf16[32,16,3072]{2,1,0:T(8,128)(2,1)S(1)} async-done(((bf16[32,16,3072]{2,1,0:T(8,128)(2,1)}), bf16[32,16,3072]{2,1,0:T(8,128)(2,1)S(1)}, u32[]{:S(2)}, u32[]{:S(2)}) %all-to-all-start.2) | async-done | bytes 3145760 | tf_op jit(solution)/shard_map/all_to_all | solution.py:780
  127.6 1.0 shard_map.153
  128.6 2.4 %collective-permute-start.3 = (bf16[16,1536]{1,0:T(8,128)(2,1)S(1)}, bf16[16,1536]{1,0:T(8,128)(2,1)S(1)}, u32[]{:S(2)}, u32[]{:S(2)}) collective-permute-start(bf16[16,1536]{1,0:T(8,128)(2,1)S(1)} %get-tuple-element.40), channel_id=1, source_target_pairs={{0,64},{32,96},{64,0},{96,32},{1,65},{33,97},{65,1},{97,33},{2,66}... | collective-permute-start | bytes 147464 | tf_op jit(solution)/shard_map/ppermute | solution.py:804
  131.0 3.3 %collective-permute-done.3.theirs_ref = bf16[16,1536]{1,0:T(8,128)(2,1)S(1)} collective-permute-done((bf16[16,1536]{1,0:T(8,128)(2,1)S(1)}, bf16[16,1536]{1,0:T(8,128)(2,1)S(1)}, u32[]{:S(2)}, u32[]{:S(2)}) %collective-permute-start.3) | collective-permute-done | bytes 49184 | tf_op jit(solution)/shard_map/ppermute | solution.py:804
  134.3 0.6 shard_map.154
  (13 shorter events, 0.0 us)
Async XLA Ops:
  5.3 25.2 %all-to-all-start = ((bf16[32,128,128]{2,1,0:T(8,128)(2,1)}), bf16[32,128,128]{2,1,0:T(8,128)(2,1)S(1)}, u32[]{:S(2)}, u32[]{:S(2)}) async-start(bf16[32,128,128]{2,1,0:T(8,128)(2,1)} %get-tuple-element.23), calls=%async_computation | async-start | bytes 2097152 | tf_op jit(solution)/shard_map/all_to_all | solution.py:731
  14.7 14.8 %collective-permute-start = (bf16[64,1024]{1,0:T(8,128)(2,1)}, bf16[64,1024]{1,0:T(8,128)(2,1)S(1)}, u32[]{:S(2)}, u32[]{:S(2)}) collective-permute-start(bf16[64,1024]{1,0:T(8,128)(2,1)} %get-tuple-element.24), channel_id=1, source_target_pairs={{0,1},{1,2},{2,3},{3,4},{4,5},{5,6},{6,7},{7,8},{8,9},{9,10},{10,1... | collective-permute-start | bytes 393224 | tf_op jit(solution)/shard_map/ppermute | solution.py:729
  18.1 12.3 %collective-permute-start.1 = (bf16[64,1024]{1,0:T(8,128)(2,1)}, bf16[64,1024]{1,0:T(8,128)(2,1)S(1)}, u32[]{:S(2)}, u32[]{:S(2)}) collective-permute-start(bf16[64,1024]{1,0:T(8,128)(2,1)} %get-tuple-element.25), channel_id=1, source_target_pairs={{1,0},{2,1},{3,2},{4,3},{5,4},{6,5},{7,6},{8,7},{9,8},{10,9},{11,1... | collective-permute-start | bytes 393224 | tf_op jit(solution)/shard_map/ppermute | solution.py:730
  21.3 18.5 %copy-start.16 = (s32[5]{0:T(128)}, s32[5]{0:T(128)S(1)}, u32[]{:S(2)}) copy-start(s32[5]{0:T(128)S(1)} %stack.19.scal_ref) | copy-start | bytes 64
  29.5 10.3 %copy-start.11 = (bf16[64,1024]{1,0:T(8,128)(2,1)}, bf16[64,1024]{1,0:T(8,128)(2,1)S(1)}, u32[]{:S(2)}) copy-start(bf16[64,1024]{1,0:T(8,128)(2,1)S(1)} %collective-permute-done.up_hbm.up_ref) | copy-start | bytes 393220
  30.4 9.4 %copy-start.13 = (bf16[64,1024]{1,0:T(8,128)(2,1)}, bf16[64,1024]{1,0:T(8,128)(2,1)S(1)}, u32[]{:S(2)}) copy-start(bf16[64,1024]{1,0:T(8,128)(2,1)S(1)} %collective-permute-done.1.down_hbm.down_ref) | copy-start | bytes 393220
  70.4 3.1 %collective-permute-start.2 = (bf16[128,4096]{1,0:T(8,128)(2,1)}, bf16[128,4096]{1,0:T(8,128)(2,1)S(1)}, u32[]{:S(2)}, u32[]{:S(2)}) collective-permute-start(bf16[128,4096]{1,0:T(8,128)(2,1)} %get-tuple-element.30.pack_hbm.pack_ref), channel_id=1, source_target_pairs={{0,32},{32,0},{64,96},{96,64},{1,33},{33,1},{65,97},{97,65},{2,34}... | collective-permute-start | bytes 3145736 | tf_op jit(solution)/shard_map/ppermute | solution.py:770
  73.5 1.0 copy-start.19
  78.0 6.8 %copy-start.8 = (bf16[192,1024]{1,0:T(8,128)(2,1)S(1)}, bf16[192,1024]{1,0:T(8,128)(2,1)}, u32[]{:S(2)}) copy-start(bf16[192,1024]{1,0:T(8,128)(2,1)} %get-tuple-element.36.residc_ref) | copy-start | bytes 1179652
  78.0 6.8 %copy-start.17 = (s32[5]{0:T(128)S(1)}, s32[5]{0:T(128)}, u32[]{:S(2)}) copy-start(s32[5]{0:T(128)} %copy-done.16) | copy-start | bytes 64
  78.0 6.7 %copy-start.18 = (s32[8]{0:T(128)S(1)}, s32[8]{0:T(128)}, u32[]{:S(2)}) copy-start(s32[8]{0:T(128)} %site_ref.1) | copy-start | bytes 100
  78.0 49.6 %all-to-all-start.2 = ((bf16[32,16,3072]{2,1,0:T(8,128)(2,1)}), bf16[32,16,3072]{2,1,0:T(8,128)(2,1)S(1)}, u32[]{:S(2)}, u32[]{:S(2)}) async-start(bf16[32,16,3072]{2,1,0:T(8,128)(2,1)} %shard_map.151), calls=%async_computation.2 | async-start | bytes 6291456 | tf_op jit(solution)/shard_map/all_to_all | solution.py:780
  84.8 2.2 %copy-start = (bf16[1024,2048]{1,0:T(8,128)(2,1)S(1)}, bf16[1024,2048]{1,0:T(8,128)(2,1)}, u32[]{:S(2)}) copy-start(bf16[1024,2048]{1,0:T(8,128)(2,1)} %win_ref.1) | copy-start | bytes 12582916
  87.0 1.2 copy-start.1
  88.2 1.2 copy-start.2
  89.4 1.6 %copy-start.3 = (bf16[1024,1024]{1,0:T(8,128)(2,1)S(1)}, bf16[1024,1024]{1,0:T(8,128)(2,1)}, u32[]{:S(2)}) copy-start(bf16[1024,1024]{1,0:T(8,128)(2,1)} %wout_ref.1) | copy-start | bytes 6291460
  91.0 1.2 copy-start.4
  92.2 1.1 copy-start.5
  93.3 1.1 copy-start.6
  94.4 1.0 copy-start.7
  95.5 1.0 copy-start.9
  96.4 0.9 copy-start.10
  97.4 0.9 copy-start.12
  98.3 0.9 copy-start.14
  99.2 0.8 copy-start.15
  128.6 5.7 %collective-permute-start.3 = (bf16[16,1536]{1,0:T(8,128)(2,1)S(1)}, bf16[16,1536]{1,0:T(8,128)(2,1)S(1)}, u32[]{:S(2)}, u32[]{:S(2)}) collective-permute-start(bf16[16,1536]{1,0:T(8,128)(2,1)S(1)} %get-tuple-element.40), channel_id=1, source_target_pairs={{0,64},{32,96},{64,0},{96,32},{1,65},{33,97},{65,1},{97,33},{2,66}... | collective-permute-start | bytes 147464 | tf_op jit(solution)/shard_map/ppermute | solution.py:804
